TPU v7x, 32 devices: a whole 2x2x4 slice. The times are simulated.
32 devices in a mesh: dp: 4 (over z), expert: 4 (over y, x), tensor: 2 (over core).
Axes of the slice: x: 2, y: 2, z: 4, core: 2. Of those that a mesh axis runs over, the one named last changes fastest.
Arguments:
- tokens: bfloat16 [4096, 2048], P(('dp', 'expert')), may hold values from -6 to 6
- segments: int32 [4096], P(('dp', 'expert')), may hold values from 0 to 2, as said below
- routes: int32 [4096, 4], P(('dp', 'expert')), may hold values from 0 to 7, all different within a row; in each aligned block of 256 rows (0 to 255, 256 to 511, ...) at most 192 rows name the same one
- attn_gain: bfloat16 [2048], replicated, may hold values from 0.5 to 1.5
- query_weight: bfloat16 [2048, 2048], P(None, 'tensor'), may hold values from -0.125 to 0.125
- query_bias: bfloat16 [16, 128], P('tensor'), may hold values from -1 to 1
- key_weight: bfloat16 [2048, 2048], P(None, 'tensor'), may hold values from -0.125 to 0.125
- key_bias: bfloat16 [16, 128], P('tensor'), may hold values from -1 to 1
- value_weight: bfloat16 [2048, 2048], P(None, 'tensor'), may hold values from -0.125 to 0.125
- value_bias: bfloat16 [16, 128], P('tensor'), may hold values from -1 to 1
- out_weight: bfloat16 [2048, 2048], P('tensor'), may hold values from -0.5 to 0.5
- mlp_gain: bfloat16 [2048], replicated, may hold values from 0.5 to 1.5
- router_weight: bfloat16 [2048, 8], replicated, may hold values from -0.0625 to 0.0625
- shared_router: bfloat16 [2048], replicated, may hold values from -0.125 to 0.125
- shared_gate: bfloat16 [2048, 5632], P(None, 'tensor'), may hold values from -0.125 to 0.125
- shared_up: bfloat16 [2048, 5632], P(None, 'tensor'), may hold values from -0.125 to 0.125
- shared_down: bfloat16 [5632, 2048], P('tensor'), may hold values from -0.15625 to 0.15625
- expert_gate: bfloat16 [8, 2048, 1408], P('expert', None, 'tensor'), may hold values from -0.125 to 0.125
- expert_up: bfloat16 [8, 2048, 1408], P('expert', None, 'tensor'), may hold values from -0.125 to 0.125
- expert_down: bfloat16 [8, 1408, 2048], P('expert', 'tensor'), may hold values from -0.625 to 0.625
- grad_out: bfloat16 [4096, 2048], P(('dp', 'expert')), may hold values from -6 to 6
Outputs:
- out: bfloat16 [4096, 2048], P(('dp', 'expert'))
- grad_tokens: float32 [4096, 2048], P(('dp', 'expert'))
- grad_attn_gain: float32 [2048], P(('dp', 'expert'))
- grad_query_weight: float32 [2048, 2048], P(('dp', 'expert'), 'tensor')
- grad_query_bias: float32 [16, 128], P('tensor', ('dp', 'expert'))
- grad_key_weight: float32 [2048, 2048], P(('dp', 'expert'), 'tensor')
- grad_key_bias: float32 [16, 128], P('tensor', ('dp', 'expert'))
- grad_value_weight: float32 [2048, 2048], P(('dp', 'expert'), 'tensor')
- grad_value_bias: float32 [16, 128], P('tensor', ('dp', 'expert'))
- grad_out_weight: float32 [2048, 2048], P('tensor', ('dp', 'expert'))
- grad_mlp_gain: float32 [2048], P(('dp', 'expert'))
- grad_router_weight: float32 [2048, 8], P(('dp', 'expert'))
- grad_shared_router: float32 [2048], P(('dp', 'expert'))
- grad_shared_gate: float32 [2048, 5632], P(('dp', 'expert'), 'tensor')
- grad_shared_up: float32 [2048, 5632], P(('dp', 'expert'), 'tensor')
- grad_shared_down: float32 [5632, 2048], P('tensor', ('dp', 'expert'))
- grad_expert_gate: float32 [8, 2048, 1408], P('expert', 'dp', 'tensor')
- grad_expert_up: float32 [8, 2048, 1408], P('expert', 'dp', 'tensor')
- grad_expert_down: float32 [8, 1408, 2048], P('expert', 'tensor', 'dp')
Inputs may be any that keep to these rules, and one draw needn't show every extreme that they name: `segments`: segment numbers never fall; every aligned run of 4096 tokens holds three whole documents of its own, and the middle one covers at least three quarters of the run. `routes`: each token names 4 different experts; among the tokens of one device (aligned blocks of 256 rows) no expert is named more than 192 times, a bound that some block reaches.
All inputs are finite; a program needn't handle non-finite values.
Results may differ from a plain program's by a relative error of at most 0.023.
Values may be sent and summed in bfloat16 or wider, within the bound.
No kernel may reach another device: no remote copies, remote signals or barrier semaphores. Data moves between devices by JAX's collectives and lax.ppermute only.
A program may use at most 384 MiB of HBM per device.

v0:
```python
import jax
import jax.numpy as jnp
from jax import lax
from jax.sharding import PartitionSpec as P

HD = 128
SEQ_LEN = 4096
WINDOW = 1024


EPS = 1e-06
THETA = 1000000.0
NEG_LARGE = -1e30


def passed_along(value, axis, steps):
    count = lax.axis_size(axis)
    first, last = (max(0, -steps), min(count, count - steps))
    return lax.ppermute(value, axis, [(source, source + steps) for source in range(first, last)])


def rotate(values, cosine, sine_table):
    half_dim = values.shape[-1] // 2
    first_half = values[..., :half_dim]
    second_half = values[..., half_dim:]
    cosine = cosine[:, None, :]
    sine_table = sine_table[:, None, :]
    return jnp.concatenate(
        [
            first_half * cosine - second_half * sine_table,
            second_half * cosine + first_half * sine_table,
        ],
        axis=-1,
    )


def silu_slope(values):
    sigmoid_val = jax.nn.sigmoid(values)
    return sigmoid_val * (1.0 + values * (1.0 - sigmoid_val))


def norm_back(values, inv_scale, gain_vec, grad_normed):
    weighted = grad_normed * gain_vec
    inner_mean = jnp.mean(weighted * values, axis=-1, keepdims=True)
    return inv_scale * weighted - values * inv_scale * inv_scale * inv_scale * inner_mean


def per_device(
    tokens,
    segments,
    routes,
    attn_gain,
    query_weight,
    query_bias,
    key_weight,
    key_bias,
    value_weight,
    value_bias,
    out_weight,
    mlp_gain,
    router_weight,
    shared_router,
    shared_gate,
    shared_up,
    shared_down,
    expert_gate,
    expert_up,
    expert_down,
    grad_out,
):
    tok_rows, model_width = tokens.shape
    local_heads = query_weight.shape[1] // HD
    local_width = local_heads * HD
    top_count = routes.shape[1]
    groups = lax.axis_size("expert")
    local_experts = expert_gate.shape[0]
    expert_count = local_experts * groups
    capacity = tok_rows * top_count * 3 // (2 * expert_count)
    score_scale = HD ** (-0.5)
    inputs = tokens.astype(jnp.float32)
    first_row = lax.axis_index(("dp", "expert")) * tok_rows
    row_index = first_row + jnp.arange(tok_rows, dtype=jnp.int32)
    places = (row_index % SEQ_LEN).astype(jnp.float32)
    frequency = THETA ** (-2.0 * jnp.arange(HD // 2, dtype=jnp.float32) / HD)
    angles = places[:, None] * frequency[None, :]
    cosine = jnp.cos(angles)
    sine_table = jnp.sin(angles)
    gain_one = attn_gain.astype(jnp.float32)
    scale_one = lax.rsqrt(jnp.mean(inputs * inputs, axis=-1, keepdims=True) + EPS)
    normed_one = (inputs * scale_one * gain_one).astype(jnp.bfloat16)
    query_pre = jnp.dot(
        normed_one, query_weight, preferred_element_type=jnp.float32
    ) + query_bias.reshape(local_width).astype(jnp.float32)
    key_pre = jnp.dot(
        normed_one, key_weight, preferred_element_type=jnp.float32
    ) + key_bias.reshape(local_width).astype(jnp.float32)
    value_pre = jnp.dot(
        normed_one, value_weight, preferred_element_type=jnp.float32
    ) + value_bias.reshape(local_width).astype(jnp.float32)
    query_rot = rotate(query_pre.reshape(tok_rows, local_heads, HD), cosine, sine_table).astype(
        jnp.bfloat16
    )
    key_rot = rotate(key_pre.reshape(tok_rows, local_heads, HD), cosine, sine_table).astype(
        jnp.bfloat16
    )
    value_low = value_pre.reshape(tok_rows, local_heads, HD).astype(jnp.bfloat16)
    seg_low = segments.astype(jnp.bfloat16)
    reach_count = (WINDOW + tok_rows - 1) // tok_rows
    key_parts = []
    value_parts = []
    seg_parts = []
    for distance in range(reach_count, 0, -1):
        far_keys, far_values, far_segs = passed_along(
            (key_rot, value_low, seg_low), ("dp", "expert"), distance
        )
        key_parts.append(far_keys)
        value_parts.append(far_values)
        seg_parts.append(far_segs)
    key_all = jnp.concatenate(key_parts + [key_rot], axis=0)
    value_all = jnp.concatenate(value_parts + [value_low], axis=0)
    seg_keys = jnp.concatenate(seg_parts + [seg_low], axis=0).astype(jnp.float32)
    key_index = (
        first_row
        - reach_count * tok_rows
        + jnp.arange((reach_count + 1) * tok_rows, dtype=jnp.int32)
    )
    offsets = row_index[:, None] - key_index[None, :]
    allowed = (
        (segments.astype(jnp.float32)[:, None] == seg_keys[None, :])
        & (offsets >= 0)
        & (offsets < WINDOW)
        & (key_index[None, :] >= 0)
    )

    def masked_scores():
        plain_scores = (
            jnp.einsum("qhd,khd->hqk", query_rot, key_all, preferred_element_type=jnp.float32)
            * score_scale
        )
        return jnp.where(allowed[None], plain_scores, NEG_LARGE)

    scores = masked_scores()
    top_score = jnp.max(scores, axis=-1, keepdims=True)
    expo_scores = jnp.exp(scores - top_score)
    total_weight = jnp.sum(expo_scores, axis=-1, keepdims=True)
    log_total = top_score + jnp.log(total_weight)
    probs_low = (expo_scores / total_weight).astype(jnp.bfloat16)
    attended = (
        jnp.einsum("hqk,khd->qhd", probs_low, value_all, preferred_element_type=jnp.float32)
        .reshape(tok_rows, local_width)
        .astype(jnp.bfloat16)
    )
    attn_part = jnp.dot(attended, out_weight, preferred_element_type=jnp.float32)
    after_attn = inputs + lax.psum(attn_part, "tensor")
    gain_two = mlp_gain.astype(jnp.float32)
    scale_two = lax.rsqrt(jnp.mean(after_attn * after_attn, axis=-1, keepdims=True) + EPS)
    normed_two = (after_attn * scale_two * gain_two).astype(jnp.bfloat16)
    gate_columns = jnp.concatenate([router_weight, shared_router[:, None]], axis=1)
    small_logits = jnp.dot(normed_two, gate_columns, preferred_element_type=jnp.float32)
    router_probs = jax.nn.softmax(small_logits[:, :expert_count], axis=-1)
    shared_mix = jax.nn.sigmoid(small_logits[:, expert_count])
    picked = (
        routes[:, :, None] == jnp.arange(expert_count, dtype=jnp.int32)[None, None, :]
    ).astype(jnp.float32)
    gates = jnp.sum(picked * router_probs[:, None, :], axis=-1)
    flat_routes = routes.reshape(-1)
    hit_table = (flat_routes[:, None] == jnp.arange(expert_count, dtype=jnp.int32)[None, :]).astype(
        jnp.int32
    )
    rank_table = jnp.cumsum(hit_table, axis=0) - hit_table
    slot_rows = flat_routes * capacity + jnp.sum(rank_table * hit_table, axis=1)

    def dispatch(values):
        placed = (
            jnp.zeros((expert_count * capacity, values.shape[1]), values.dtype)
            .at[slot_rows]
            .set(values)
        )
        return placed.reshape(groups, local_experts * capacity, values.shape[1])

    def collect(values):
        return values.reshape(expert_count * capacity, model_width)[slot_rows].reshape(
            tok_rows, top_count, model_width
        )

    sent_rows = dispatch(jnp.repeat(normed_two, top_count, axis=0))
    arrived = lax.all_to_all(sent_rows, "expert", split_axis=0, concat_axis=0, tiled=True).reshape(
        groups, local_experts, capacity, model_width
    )
    expert_gate_val = jnp.einsum(
        "secd,edh->sech", arrived, expert_gate, preferred_element_type=jnp.float32
    )
    expert_up_val = jnp.einsum(
        "secd,edh->sech", arrived, expert_up, preferred_element_type=jnp.float32
    )
    expert_inner = (jax.nn.silu(expert_gate_val) * expert_up_val).astype(jnp.bfloat16)
    expert_rows = jnp.einsum(
        "sech,ehd->secd", expert_inner, expert_down, preferred_element_type=jnp.float32
    )
    returned_rows = collect(
        lax.all_to_all(
            expert_rows.reshape(groups, local_experts * capacity, model_width),
            "expert",
            split_axis=0,
            concat_axis=0,
            tiled=True,
        )
    )
    shared_gate_val = jnp.dot(normed_two, shared_gate, preferred_element_type=jnp.float32)
    shared_up_val = jnp.dot(normed_two, shared_up, preferred_element_type=jnp.float32)
    shared_inner = (jax.nn.silu(shared_gate_val) * shared_up_val).astype(jnp.bfloat16)
    shared_out = jnp.dot(shared_inner, shared_down, preferred_element_type=jnp.float32)
    mixed_part = (
        jnp.sum(gates[:, :, None] * returned_rows, axis=1) + shared_mix[:, None] * shared_out
    )
    after_mlp = after_attn + lax.psum(mixed_part.astype(jnp.bfloat16), "tensor").astype(jnp.float32)
    out = after_mlp.astype(jnp.bfloat16)
    grad_top = grad_out.astype(jnp.float32)
    grad_gate_part = jnp.sum(returned_rows * grad_top[:, None, :], axis=-1)
    grad_mix_part = jnp.sum(shared_out * grad_top, axis=-1)
    row_grad = (
        (gates[:, :, None] * grad_top[:, None, :])
        .astype(jnp.bfloat16)
        .reshape(tok_rows * top_count, model_width)
    )
    grad_arrived = lax.all_to_all(
        dispatch(row_grad), "expert", split_axis=0, concat_axis=0, tiled=True
    ).reshape(groups, local_experts, capacity, model_width)
    grad_expert_inner = jnp.einsum(
        "secd,ehd->sech", grad_arrived, expert_down, preferred_element_type=jnp.float32
    )
    grad_expert_down = jnp.einsum(
        "sech,secd->ehd", expert_inner, grad_arrived, preferred_element_type=jnp.float32
    )
    grad_expert_gate_val = (grad_expert_inner * expert_up_val * silu_slope(expert_gate_val)).astype(
        jnp.bfloat16
    )
    grad_expert_up_val = (grad_expert_inner * jax.nn.silu(expert_gate_val)).astype(jnp.bfloat16)
    grad_expert_gate = jnp.einsum(
        "secd,sech->edh", arrived, grad_expert_gate_val, preferred_element_type=jnp.float32
    )
    grad_expert_up = jnp.einsum(
        "secd,sech->edh", arrived, grad_expert_up_val, preferred_element_type=jnp.float32
    )
    grad_expert_in = jnp.einsum(
        "sech,edh->secd", grad_expert_gate_val, expert_gate, preferred_element_type=jnp.float32
    )
    grad_expert_in = grad_expert_in + jnp.einsum(
        "sech,edh->secd", grad_expert_up_val, expert_up, preferred_element_type=jnp.float32
    )
    grad_expert_gate, grad_expert_up, grad_expert_down = (
        lax.psum_scatter(
            grad_expert_gate.astype(jnp.bfloat16), "dp", scatter_dimension=1, tiled=True
        ).astype(jnp.float32),
        lax.psum_scatter(
            grad_expert_up.astype(jnp.bfloat16), "dp", scatter_dimension=1, tiled=True
        ).astype(jnp.float32),
        lax.psum_scatter(
            grad_expert_down.astype(jnp.bfloat16), "dp", scatter_dimension=2, tiled=True
        ).astype(jnp.float32),
    )
    shared_row_grad = (shared_mix[:, None] * grad_top).astype(jnp.bfloat16)
    grad_shared_inner = jnp.einsum(
        "td,fd->tf", shared_row_grad, shared_down, preferred_element_type=jnp.float32
    )
    grad_shared_down = jnp.einsum(
        "tf,td->fd", shared_inner, shared_row_grad, preferred_element_type=jnp.float32
    )
    grad_shared_gate_val = (grad_shared_inner * shared_up_val * silu_slope(shared_gate_val)).astype(
        jnp.bfloat16
    )
    grad_shared_up_val = (grad_shared_inner * jax.nn.silu(shared_gate_val)).astype(jnp.bfloat16)
    grad_shared_gate = jnp.einsum(
        "td,tf->df", normed_two, grad_shared_gate_val, preferred_element_type=jnp.float32
    )
    grad_shared_up = jnp.einsum(
        "td,tf->df", normed_two, grad_shared_up_val, preferred_element_type=jnp.float32
    )
    grad_normed_part = jnp.einsum(
        "tf,df->td", grad_shared_gate_val, shared_gate, preferred_element_type=jnp.float32
    )
    grad_normed_part = grad_normed_part + jnp.einsum(
        "tf,df->td", grad_shared_up_val, shared_up, preferred_element_type=jnp.float32
    )
    returned_grads = lax.all_to_all(
        grad_expert_in.reshape(groups, local_experts * capacity, model_width),
        "expert",
        split_axis=0,
        concat_axis=0,
        tiled=True,
    )
    grad_normed_part = grad_normed_part + jnp.sum(collect(returned_grads), axis=1)
    grad_normed_sum, grad_gates, grad_mix = lax.psum(
        (grad_normed_part, grad_gate_part, grad_mix_part), "tensor"
    )
    grad_router_probs = jnp.sum(picked * grad_gates[:, :, None], axis=1)
    grad_logits = router_probs * (
        grad_router_probs - jnp.sum(router_probs * grad_router_probs, axis=-1, keepdims=True)
    )
    grad_shared_logit = grad_mix * shared_mix * (1.0 - shared_mix)
    grad_small = jnp.concatenate([grad_logits, grad_shared_logit[:, None]], axis=1).astype(
        jnp.bfloat16
    )
    grad_normed_two = grad_normed_sum + jnp.einsum(
        "te,de->td", grad_small, gate_columns, preferred_element_type=jnp.float32
    )
    grad_columns = jnp.einsum(
        "td,te->de", normed_two, grad_small, preferred_element_type=jnp.float32
    )
    grad_router_weight = grad_columns[:, :expert_count]
    grad_shared_router = grad_columns[:, expert_count]
    grad_mlp_gain = jnp.sum(grad_normed_two * after_attn * scale_two, axis=0)
    grad_after = grad_top + norm_back(after_attn, scale_two, gain_two, grad_normed_two)
    grad_attended = grad_after.astype(jnp.bfloat16)
    grad_heads = jnp.einsum(
        "td,hd->th", grad_attended, out_weight, preferred_element_type=jnp.float32
    ).astype(jnp.bfloat16)
    grad_out_weight = jnp.einsum(
        "th,td->hd", attended, grad_attended, preferred_element_type=jnp.float32
    )
    grad_heads_split = grad_heads.reshape(tok_rows, local_heads, HD)
    probs_again = jnp.exp(masked_scores() - log_total)
    grad_probs = jnp.einsum(
        "qhd,khd->hqk", grad_heads_split, value_all, preferred_element_type=jnp.float32
    )
    delta_sum = jnp.sum(probs_again * grad_probs, axis=-1, keepdims=True)
    grad_scores = (probs_again * (grad_probs - delta_sum)).astype(jnp.bfloat16)
    grad_query_rot = (
        jnp.einsum("hqk,khd->qhd", grad_scores, key_all, preferred_element_type=jnp.float32)
        * score_scale
    )
    key_grads = (
        jnp.einsum("hqk,qhd->khd", grad_scores, query_rot, preferred_element_type=jnp.float32)
        * score_scale
    )
    value_grads = jnp.einsum(
        "hqk,qhd->khd",
        probs_again.astype(jnp.bfloat16),
        grad_heads_split,
        preferred_element_type=jnp.float32,
    )
    own_key_grad = key_grads[reach_count * tok_rows :]
    own_value_grad = value_grads[reach_count * tok_rows :]
    for distance in range(reach_count, 0, -1):
        position = reach_count - distance
        came_keys, came_values = passed_along(
            (
                key_grads[position * tok_rows : (position + 1) * tok_rows],
                value_grads[position * tok_rows : (position + 1) * tok_rows],
            ),
            ("dp", "expert"),
            -distance,
        )
        own_key_grad = own_key_grad + came_keys
        own_value_grad = own_value_grad + came_values
    grad_query = (
        rotate(grad_query_rot, cosine, -sine_table)
        .reshape(tok_rows, local_width)
        .astype(jnp.bfloat16)
    )
    grad_key = (
        rotate(own_key_grad, cosine, -sine_table)
        .reshape(tok_rows, local_width)
        .astype(jnp.bfloat16)
    )
    grad_value = own_value_grad.reshape(tok_rows, local_width).astype(jnp.bfloat16)
    grad_query_weight = jnp.einsum(
        "td,th->dh", normed_one, grad_query, preferred_element_type=jnp.float32
    )
    grad_key_weight = jnp.einsum(
        "td,th->dh", normed_one, grad_key, preferred_element_type=jnp.float32
    )
    grad_value_weight = jnp.einsum(
        "td,th->dh", normed_one, grad_value, preferred_element_type=jnp.float32
    )
    grad_query_bias = jnp.sum(grad_query, axis=0, dtype=jnp.float32).reshape(local_heads, HD)
    grad_key_bias = jnp.sum(grad_key, axis=0, dtype=jnp.float32).reshape(local_heads, HD)
    grad_value_bias = jnp.sum(grad_value, axis=0, dtype=jnp.float32).reshape(local_heads, HD)
    grad_normed_one = jnp.einsum(
        "th,dh->td", grad_query, query_weight, preferred_element_type=jnp.float32
    )
    grad_normed_one = grad_normed_one + jnp.einsum(
        "th,dh->td", grad_key, key_weight, preferred_element_type=jnp.float32
    )
    grad_normed_one = grad_normed_one + jnp.einsum(
        "th,dh->td", grad_value, value_weight, preferred_element_type=jnp.float32
    )
    grad_normed_one = lax.psum(grad_normed_one.astype(jnp.bfloat16), "tensor").astype(jnp.float32)
    grad_attn_gain = jnp.sum(grad_normed_one * inputs * scale_one, axis=0)
    grad_tokens = grad_after + norm_back(inputs, scale_one, gain_one, grad_normed_one)
    (
        grad_shared_gate,
        grad_shared_up,
        grad_shared_down,
        grad_router_weight,
        grad_shared_router,
        grad_mlp_gain,
        grad_query_weight,
        grad_key_weight,
        grad_value_weight,
        grad_out_weight,
        grad_query_bias,
        grad_key_bias,
        grad_value_bias,
        grad_attn_gain,
    ) = (
        lax.psum_scatter(grad_shared_gate, ("dp", "expert"), scatter_dimension=0, tiled=True),
        lax.psum_scatter(grad_shared_up, ("dp", "expert"), scatter_dimension=0, tiled=True),
        lax.psum_scatter(grad_shared_down, ("dp", "expert"), scatter_dimension=1, tiled=True),
        lax.psum_scatter(grad_router_weight, ("dp", "expert"), scatter_dimension=0, tiled=True),
        lax.psum_scatter(grad_shared_router, ("dp", "expert"), scatter_dimension=0, tiled=True),
        lax.psum_scatter(grad_mlp_gain, ("dp", "expert"), scatter_dimension=0, tiled=True),
        lax.psum_scatter(grad_query_weight, ("dp", "expert"), scatter_dimension=0, tiled=True),
        lax.psum_scatter(grad_key_weight, ("dp", "expert"), scatter_dimension=0, tiled=True),
        lax.psum_scatter(grad_value_weight, ("dp", "expert"), scatter_dimension=0, tiled=True),
        lax.psum_scatter(grad_out_weight, ("dp", "expert"), scatter_dimension=1, tiled=True),
        lax.psum_scatter(grad_query_bias, ("dp", "expert"), scatter_dimension=1, tiled=True),
        lax.psum_scatter(grad_key_bias, ("dp", "expert"), scatter_dimension=1, tiled=True),
        lax.psum_scatter(grad_value_bias, ("dp", "expert"), scatter_dimension=1, tiled=True),
        lax.psum_scatter(grad_attn_gain, ("dp", "expert"), scatter_dimension=0, tiled=True),
    )
    return (
        out,
        grad_tokens,
        grad_attn_gain,
        grad_query_weight,
        grad_query_bias,
        grad_key_weight,
        grad_key_bias,
        grad_value_weight,
        grad_value_bias,
        grad_out_weight,
        grad_mlp_gain,
        grad_router_weight,
        grad_shared_router,
        grad_shared_gate,
        grad_shared_up,
        grad_shared_down,
        grad_expert_gate,
        grad_expert_up,
        grad_expert_down,
    )


def solution(mesh):
    placed = (
        P(("dp", "expert"), None),
        P(("dp", "expert")),
        P(("dp", "expert"), None),
        P(),
        P(None, "tensor"),
        P("tensor", None),
        P(None, "tensor"),
        P("tensor", None),
        P(None, "tensor"),
        P("tensor", None),
        P("tensor", None),
        P(),
        P(),
        P(),
        P(None, "tensor"),
        P(None, "tensor"),
        P("tensor", None),
        P("expert", None, "tensor"),
        P("expert", None, "tensor"),
        P("expert", "tensor", None),
        P(("dp", "expert"), None),
    )
    return jax.shard_map(
        per_device,
        mesh=mesh,
        in_specs=placed,
        out_specs=(
            P(("dp", "expert"), None),
            P(("dp", "expert"), None),
            P(("dp", "expert")),
            P(("dp", "expert"), "tensor"),
            P("tensor", ("dp", "expert")),
            P(("dp", "expert"), "tensor"),
            P("tensor", ("dp", "expert")),
            P(("dp", "expert"), "tensor"),
            P("tensor", ("dp", "expert")),
            P("tensor", ("dp", "expert")),
            P(("dp", "expert")),
            P(("dp", "expert"), None),
            P(("dp", "expert")),
            P(("dp", "expert"), "tensor"),
            P(("dp", "expert"), "tensor"),
            P("tensor", ("dp", "expert")),
            P("expert", "dp", "tensor"),
            P("expert", "dp", "tensor"),
            P("expert", "tensor", "dp"),
        ),
        check_vma=False,
    )
```

profile of v0, /device:TPU:1, one launch (start us, length us, event | category | flops | bytes accessed | tf_op | source)
XLA Modules:
  0.0 3386.4 jit_solution(6471015112410504047)
XLA Ops:
  64.2 21.6 collective-permute-start.9
  115.2 45.6 %all-reduce.13.cloned.1.call-done = f32[256,2048]{1,0:T(8,128)} async-done(((f32[256,2048]{1,0:T(8,128)}), f32[256,2048]{1,0:T(8,128)}) %all-reduce.13.cloned.1.call-update) | async-done | bytes 2097168 | tf_op jit(solution)/shard_map/psum | solution.py:154
  168.5 6.9 reshape.480
  175.4 11.2 scatter_custom_fusion
  197.6 10.1 mul.494
  209.1 12.2 scatter_custom_fusion.1
  221.2 40.8 %all-to-all-done = bf16[4,384,2048]{2,1,0:T(8,128)(2,1)} async-done(((bf16[4,384,2048]{2,1,0:T(8,128)(2,1)}), bf16[4,384,2048]{2,1,0:T(8,128)(2,1)}, u32[]{:S(2)}, u32[]{:S(2)}) %all-to-all-start) | async-done | bytes 6291488 | tf_op jit(solution)/shard_map/all_to_all | solution.py:187
  267.5 10.3 fusion.4
  277.8 10.3 fusion.8
  288.1 48.7 %all-to-all-done.2 = bf16[4,384,2048]{2,1,0:T(8,128)(2,1)} async-done(((bf16[4,384,2048]{2,1,0:T(8,128)(2,1)}), bf16[4,384,2048]{2,1,0:T(8,128)(2,1)}, u32[]{:S(2)}, u32[]{:S(2)}) %all-to-all-start.2) | async-done | bytes 6291488 | tf_op jit(solution)/shard_map/all_to_all | solution.py:226
  336.9 12.7 fusion.29
  349.5 8.8 fusion.2
  358.4 11.0 add_bitcast_fusion
  369.4 11.3 copy.169
  387.1 9.0 fusion.120
  396.1 9.0 fusion.119
  405.1 15.0 multiply_convert_fusion.3
  421.2 8.8 fusion.121
  430.0 93.8 %all-to-all-done.3 = f32[4,384,2048]{2,1,0:T(8,128)} async-done(((f32[4,384,2048]{2,1,0:T(8,128)}), f32[4,384,2048]{2,1,0:T(8,128)}, u32[]{:S(2)}, u32[]{:S(2)}) %all-to-all-start.3) | async-done | bytes 12582944 | tf_op jit(solution)/shard_map/all_to_all | solution.py:285
  523.8 13.5 gather_fusion.1
  537.3 10.0 reshape.455
  547.3 8.7 reduce_sum.190
  556.0 9.8 fusion.48
  565.8 10.7 bitcast_convert_fusion
  576.8 10.7 bitcast_convert_fusion.2
  587.5 10.9 fusion.19
  598.4 11.8 copy.166
  618.3 9.7 bitcast_convert_fusion.1
  628.5 124.7 %all-to-all-done.1 = f32[4,384,2048]{2,1,0:T(8,128)} async-done(((f32[4,384,2048]{2,1,0:T(8,128)}), f32[4,384,2048]{2,1,0:T(8,128)}, u32[]{:S(2)}, u32[]{:S(2)}) %all-to-all-start.1) | async-done | bytes 12582944 | tf_op jit(solution)/shard_map/all_to_all | solution.py:201
  753.2 13.5 gather_fusion
  766.7 9.9 reshape.450
  776.7 10.1 multiply_reduce_fusion.1
  786.9 9.0 multiply_reduce_fusion.5
  808.5 6.7 multiply_reduce_fusion
  839.3 52.4 %collective-permute-done.12 = f32[256,8,128]{2,0,1:T(8,128)S(1)} collective-permute-done((f32[256,8,128]{2,0,1:T(8,128)}, f32[256,8,128]{2,0,1:T(8,128)S(1)}, u32[]{:S(2)}, u32[]{:S(2)}) %collective-permute-start.12) | collective-permute-done | bytes 1048608 | tf_op jit(solution)/shard_map/ppermute | solution.py:19
  908.4 121.3 %collective-permute-done.16 = f32[256,8,128]{0,2,1:T(8,128)} collective-permute-done((f32[256,8,128]{0,2,1:T(8,128)}, f32[256,8,128]{0,2,1:T(8,128)}, u32[]{:S(2)}, u32[]{:S(2)}) %collective-permute-start.16) | collective-permute-done | bytes 1048608 | tf_op jit(solution)/shard_map/ppermute | solution.py:19
  1066.2 12.6 fusion.82
  1078.8 12.5 fusion.124
  1091.6 12.5 fusion.123
  1116.9 12.2 all-reduce.17.cloned.1.call-done
  1130.9 118.0 %all-reduce.6 = (f32[2048]{0:T(1024)S(1)}, f32[8,128]{1,0:T(8,128)S(1)}, f32[8,128]{1,0:T(8,128)S(1)}, f32[8,128]{1,0:T(8,128)S(1)}, f32[2048]{0:T(1024)S(1)}, /*index=5*/f32[2048]{0:T(1024)S(1)}) all-reduce(f32[2048]{0:T(1024)S(1)} %get-tuple-element.23, ...), channel_id=2, replica_groups=mesh['dp'=4,'expert'=4,'tensor'=2] {'dp','expert'}, use_global_device_ids=true, to_apply=%region_28.29.clone | all-reduce | flops 9216 | bytes 73728
  1257.2 129.6 %reduce-scatter.21.cloned.1.call-done = f32[1024,128]{1,0:T(8,128)} async-done(((f32[1024,2048]{1,0:T(8,128)}), f32[1024,128]{1,0:T(8,128)}) %reduce-scatter.21.cloned.1.call-update) | async-done | bytes 524304 | tf_op jit(solution)/shard_map/reduce_scatter | solution.py:416
  1386.9 183.0 %reduce-scatter.19.cloned.1.call-done = f32[128,1024]{1,0:T(8,128)} async-done(((f32[2048,1024]{1,0:T(8,128)}), f32[128,1024]{1,0:T(8,128)}) %reduce-scatter.19.cloned.1.call-update) | async-done | bytes 524304 | tf_op jit(solution)/shard_map/reduce_scatter | solution.py:415
  1569.8 183.0 %reduce-scatter.17.cloned.1.call-done = f32[128,1024]{1,0:T(8,128)} async-done(((f32[2048,1024]{1,0:T(8,128)}), f32[128,1024]{1,0:T(8,128)}) %reduce-scatter.17.cloned.1.call-update) | async-done | bytes 524304 | tf_op jit(solution)/shard_map/reduce_scatter | solution.py:414
  1752.8 183.1 %reduce-scatter.15.cloned.1.call-done = f32[128,1024]{1,0:T(8,128)} async-done(((f32[2048,1024]{1,0:T(8,128)}), f32[128,1024]{1,0:T(8,128)}) %reduce-scatter.15.cloned.1.call-update) | async-done | bytes 524304 | tf_op jit(solution)/shard_map/reduce_scatter | solution.py:413
  1936.0 478.4 %reduce-scatter.29.cloned.1.call-done = f32[2816,128]{1,0:T(8,128)} async-done(((f32[2816,2048]{1,0:T(8,128)}), f32[2816,128]{1,0:T(8,128)}) %reduce-scatter.29.cloned.1.call-update) | async-done | bytes 1441808 | tf_op jit(solution)/shard_map/reduce_scatter | solution.py:409
  2414.4 482.7 %reduce-scatter.27.cloned.1.call-done = f32[128,2816]{1,0:T(8,128)} async-done(((f32[2048,2816]{1,0:T(8,128)}), f32[128,2816]{1,0:T(8,128)}) %reduce-scatter.27.cloned.1.call-update) | async-done | bytes 1441808 | tf_op jit(solution)/shard_map/reduce_scatter | solution.py:408
  2897.1 482.5 %reduce-scatter.25.cloned.1.call-done = f32[128,2816]{1,0:T(8,128)} async-done(((f32[2048,2816]{1,0:T(8,128)}), f32[128,2816]{1,0:T(8,128)}) %reduce-scatter.25.cloned.1.call-update) | async-done | bytes 1441808 | tf_op jit(solution)/shard_map/reduce_scatter | solution.py:407
  (341 shorter events, 238.9 us)
Async XLA Ops:
  7.2 153.6 %all-reduce.13.cloned.1.call-start = ((), (), s32[]{:S(2)}) async-start(), calls=%async_computation.15 | async-start | bytes 4194304 | tf_op jit(solution)/shard_map/psum | solution.py:154
  8.0 42.7 %collective-permute-start.7 = (bf16[256]{0:T(256)(128)(2,1)S(1)}, bf16[256]{0:T(256)(128)(2,1)S(1)}, u32[]{:S(2)}, u32[]{:S(2)}) collective-permute-start(bf16[256]{0:T(256)(128)(2,1)S(1)} %get-tuple-element.79), channel_id=1, source_target_pairs={{0,2},{2,4},{4,6},{6,8},{8,10},{10,12},{12,14},{14,16},{16,18},{18... | collective-permute-start | bytes 1544 | tf_op jit(solution)/shard_map/ppermute | solution.py:19
  11.9 36.5 %collective-permute-start.6 = (bf16[256]{0:T(256)(128)(2,1)S(1)}, bf16[256]{0:T(256)(128)(2,1)S(1)}, u32[]{:S(2)}, u32[]{:S(2)}) collective-permute-start(bf16[256]{0:T(256)(128)(2,1)S(1)} %get-tuple-element.79), channel_id=1, source_target_pairs={{0,4},{2,6},{4,8},{6,10},{8,12},{10,14},{12,16},{14,18},{16,20},{1... | collective-permute-start | bytes 1544 | tf_op jit(solution)/shard_map/ppermute | solution.py:19
  15.1 29.3 collective-permute-start.5
  19.2 21.9 collective-permute-start.4
  29.4 60.3 %collective-permute-start.3 = (bf16[256,8,128]{0,2,1:T(8,128)(2,1)S(1)}, bf16[256,8,128]{0,2,1:T(8,128)(2,1)}, u32[]{:S(2)}, u32[]{:S(2)}) collective-permute-start(bf16[256,8,128]{0,2,1:T(8,128)(2,1)S(1)} %bitcast.211), channel_id=1, source_target_pairs={{0,2},{2,4},{4,6},{6,8},{8,10},{10,12},{12,14},{14,16},{16,18},{18... | collective-permute-start | bytes 1572872 | tf_op jit(solution)/shard_map/ppermute | solution.py:19
  40.7 56.0 %copy-start.11 = (bf16[256,8,64]{2,0,1:T(8,128)(2,1)}, bf16[256,8,64]{2,0,1:T(8,128)(2,1)S(1)}, u32[]{:S(2)}) copy-start(bf16[256,8,64]{2,0,1:T(8,128)(2,1)S(1)} %get-tuple-element.57) | copy-start | bytes 786436
  40.7 56.0 %copy-start.13 = (bf16[256,8,64]{2,0,1:T(8,128)(2,1)}, bf16[256,8,64]{2,0,1:T(8,128)(2,1)S(1)}, u32[]{:S(2)}) copy-start(bf16[256,8,64]{2,0,1:T(8,128)(2,1)S(1)} %get-tuple-element.58) | copy-start | bytes 786436
  41.0 45.8 %collective-permute-start.2 = (bf16[256,8,128]{0,2,1:T(8,128)(2,1)S(1)}, bf16[256,8,128]{0,2,1:T(8,128)(2,1)}, u32[]{:S(2)}, u32[]{:S(2)}) collective-permute-start(bf16[256,8,128]{0,2,1:T(8,128)(2,1)S(1)} %bitcast.212), channel_id=1, source_target_pairs={{0,4},{2,6},{4,8},{6,10},{8,12},{10,14},{12,16},{14,18},{16,20},{1... | collective-permute-start | bytes 1572872 | tf_op jit(solution)/shard_map/ppermute | solution.py:19
  44.4 19.7 collective-permute-start.1
  48.4 10.4 collective-permute-start
  50.7 44.7 %collective-permute-start.11 = (bf16[256,8,128]{2,0,1:T(8,128)(2,1)S(1)}, bf16[256,8,128]{2,0,1:T(8,128)(2,1)}, u32[]{:S(2)}, u32[]{:S(2)}) collective-permute-start(bf16[256,8,128]{2,0,1:T(8,128)(2,1)S(1)} %pad_maximum_fusion.1), channel_id=1, source_target_pairs={{0,2},{2,4},{4,6},{6,8},{8,10},{10,12},{12,14},{14,16},{16,18},{18... | collective-permute-start | bytes 1572872 | tf_op jit(solution)/shard_map/ppermute | solution.py:19
  58.9 32.0 collective-permute-start.8
  64.2 28.8 collective-permute-start.9
  86.9 8.5 collective-permute-start.10
  112.1 50.7 %copy-start.39 = (f32[2048]{0:T(1024)}, f32[2048]{0:T(1024)S(1)}, u32[]{:S(2)}) copy-start(f32[2048]{0:T(1024)S(1)} %convert_element_type.219) | copy-start | bytes 24580
  164.3 231.8 %copy-start.5 = (bf16[256,2048]{1,0:T(8,128)(2,1)}, bf16[256,2048]{1,0:T(8,128)(2,1)S(1)}, u32[]{:S(2)}) copy-start(bf16[256,2048]{1,0:T(8,128)(2,1)S(1)} %multiply_convert_fusion.7) | copy-start | bytes 3145732
  186.6 75.4 %all-to-all-start = ((bf16[4,384,2048]{2,1,0:T(8,128)(2,1)}), bf16[4,384,2048]{2,1,0:T(8,128)(2,1)}, u32[]{:S(2)}, u32[]{:S(2)}) async-start(bf16[4,384,2048]{2,1,0:T(8,128)(2,1)} %bitcast.199), calls=%async_computation | async-start | bytes 12582912 | tf_op jit(solution)/shard_map/all_to_all | solution.py:187
  208.1 179.0 %copy-start.37 = (f32[256,9]{0,1:T(8,128)}, f32[256,9]{0,1:T(8,128)S(1)}, u32[]{:S(2)}) copy-start(f32[256,9]{0,1:T(8,128)S(1)} %fusion.118) | copy-start | bytes 27652
  262.0 74.8 %all-to-all-start.2 = ((bf16[4,384,2048]{2,1,0:T(8,128)(2,1)}), bf16[4,384,2048]{2,1,0:T(8,128)(2,1)}, u32[]{:S(2)}, u32[]{:S(2)}) async-start(bf16[4,384,2048]{2,1,0:T(8,128)(2,1)} %bitcast.200), calls=%async_computation.2 | async-start | bytes 12582912 | tf_op jit(solution)/shard_map/all_to_all | solution.py:226
  380.7 143.0 %all-to-all-start.3 = ((f32[4,384,2048]{2,1,0:T(8,128)}), f32[4,384,2048]{2,1,0:T(8,128)}, u32[]{:S(2)}, u32[]{:S(2)}) async-start(f32[4,384,2048]{2,1,0:T(8,128)} %bitcast.198), calls=%async_computation.3 | async-start | bytes 25165824 | tf_op jit(solution)/shard_map/all_to_all | solution.py:285
  387.1 414.5 %all-reduce.15.cloned.1.call-start = ((), (), s32[]{:S(2)}) async-start(), calls=%async_computation.16 | async-start | bytes 4194304 | tf_op jit(solution)/shard_map/psum | solution.py:293
  565.8 540.9 %reduce-scatter.35.cloned.1.call-start = ((), (), s32[]{:S(2)}) async-start(), calls=%async_computation.27 | async-start | bytes 7208960 | tf_op jit(solution)/shard_map/reduce_scatter | solution.py:258
  576.6 533.5 %reduce-scatter.31.cloned.1.call-start = ((), (), s32[]{:S(2)}) async-start(), calls=%async_computation.25 | async-start | bytes 7208960 | tf_op jit(solution)/shard_map/reduce_scatter | solution.py:252
  610.2 143.0 %all-to-all-start.1 = ((f32[4,384,2048]{2,1,0:T(8,128)}), f32[4,384,2048]{2,1,0:T(8,128)}, u32[]{:S(2)}, u32[]{:S(2)}) async-start(f32[4,384,2048]{2,1,0:T(8,128)} %bitcast.197), calls=%async_computation.1 | async-start | bytes 25165824 | tf_op jit(solution)/shard_map/all_to_all | solution.py:201
  616.5 496.9 %reduce-scatter.33.cloned.1.call-start = ((), (), s32[]{:S(2)}) async-start(), calls=%async_computation.26 | async-start | bytes 7208960 | tf_op jit(solution)/shard_map/reduce_scatter | solution.py:255
  628.1 501.0 %all-reduce.17.cloned.1.call-start = ((), (), s32[]{:S(2)}) async-start(), calls=%async_computation.28 | async-start | bytes 4194304 | tf_op jit(solution)/shard_map/psum | solution.py:216
  826.6 65.1 %collective-permute-start.12 = (f32[256,8,128]{2,0,1:T(8,128)}, f32[256,8,128]{2,0,1:T(8,128)S(1)}, u32[]{:S(2)}, u32[]{:S(2)}) collective-permute-start(f32[256,8,128]{2,0,1:T(8,128)} %get-tuple-element.53), channel_id=1, source_target_pairs={{8,0},{10,2},{12,4},{14,6},{16,8},{18,10},{20,12},{22,14},{24,16},... | collective-permute-start | bytes 3145736 | tf_op jit(solution)/shard_map/ppermute | solution.py:19
  827.9 65.1 %collective-permute-start.15 = (f32[256,8,128]{2,0,1:T(8,128)S(1)}, f32[256,8,128]{2,0,1:T(8,128)S(1)}, u32[]{:S(2)}, u32[]{:S(2)}) collective-permute-start(f32[256,8,128]{2,0,1:T(8,128)S(1)} %get-tuple-element.54), channel_id=1, source_target_pairs={{2,0},{4,2},{6,4},{8,6},{10,8},{12,10},{14,12},{16,14},{18,16},{20... | collective-permute-start | bytes 3145736 | tf_op jit(solution)/shard_map/ppermute | solution.py:19
  829.2 65.2 %collective-permute-start.14 = (f32[256,8,128]{2,0,1:T(8,128)S(1)}, f32[256,8,128]{2,0,1:T(8,128)S(1)}, u32[]{:S(2)}, u32[]{:S(2)}) collective-permute-start(f32[256,8,128]{2,0,1:T(8,128)S(1)} %get-tuple-element.55), channel_id=1, source_target_pairs={{4,0},{6,2},{8,4},{10,6},{12,8},{14,10},{16,12},{18,14},{20,16},{2... | collective-permute-start | bytes 3145736 | tf_op jit(solution)/shard_map/ppermute | solution.py:19
  830.5 69.4 %collective-permute-start.13 = (f32[256,8,128]{2,0,1:T(8,128)S(1)}, f32[256,8,128]{2,0,1:T(8,128)S(1)}, u32[]{:S(2)}, u32[]{:S(2)}) collective-permute-start(f32[256,8,128]{2,0,1:T(8,128)S(1)} %get-tuple-element.56), channel_id=1, source_target_pairs={{6,0},{8,2},{10,4},{12,6},{14,8},{16,10},{18,12},{20,14},{22,16},{... | collective-permute-start | bytes 3145736 | tf_op jit(solution)/shard_map/ppermute | solution.py:19
  834.1 61.8 %copy-start.21 = (bf16[1280,8,128]{2,0,1:T(8,128)(2,1)S(1)}, bf16[1280,8,128]{2,0,1:T(8,128)(2,1)}, u32[]{:S(2)}) copy-start(bf16[1280,8,128]{2,0,1:T(8,128)(2,1)} %copy-done.20) | copy-start | bytes 7864324
  838.0 191.7 %collective-permute-start.16 = (f32[256,8,128]{0,2,1:T(8,128)}, f32[256,8,128]{0,2,1:T(8,128)}, u32[]{:S(2)}, u32[]{:S(2)}) collective-permute-start(f32[256,8,128]{0,2,1:T(8,128)} %get-tuple-element.49), channel_id=1, source_target_pairs={{8,0},{10,2},{12,4},{14,6},{16,8},{18,10},{20,12},{22,14},{24,16},... | collective-permute-start | bytes 3145736 | tf_op jit(solution)/shard_map/ppermute | solution.py:19
  891.8 138.0 %collective-permute-start.19 = (f32[256,8,128]{0,2,1:T(8,128)}, f32[256,8,128]{0,2,1:T(8,128)}, u32[]{:S(2)}, u32[]{:S(2)}) collective-permute-start(f32[256,8,128]{0,2,1:T(8,128)} %get-tuple-element.50), channel_id=1, source_target_pairs={{2,0},{4,2},{6,4},{8,6},{10,8},{12,10},{14,12},{16,14},{18,16},{20... | collective-permute-start | bytes 3145736 | tf_op jit(solution)/shard_map/ppermute | solution.py:19
  893.1 136.7 %collective-permute-start.18 = (f32[256,8,128]{0,2,1:T(8,128)}, f32[256,8,128]{0,2,1:T(8,128)}, u32[]{:S(2)}, u32[]{:S(2)}) collective-permute-start(f32[256,8,128]{0,2,1:T(8,128)} %get-tuple-element.51), channel_id=1, source_target_pairs={{4,0},{6,2},{8,4},{10,6},{12,8},{14,10},{16,12},{18,14},{20,16},{2... | collective-permute-start | bytes 3145736 | tf_op jit(solution)/shard_map/ppermute | solution.py:19
  894.4 135.4 %collective-permute-start.17 = (f32[256,8,128]{0,2,1:T(8,128)}, f32[256,8,128]{0,2,1:T(8,128)}, u32[]{:S(2)}, u32[]{:S(2)}) collective-permute-start(f32[256,8,128]{0,2,1:T(8,128)} %get-tuple-element.52), channel_id=1, source_target_pairs={{6,0},{8,2},{10,4},{12,6},{14,8},{16,10},{18,12},{20,14},{22,16},{... | collective-permute-start | bytes 3145736 | tf_op jit(solution)/shard_map/ppermute | solution.py:19
  904.8 129.2 %copy-start.15 = (bf16[256,8,128]{0,2,1:T(8,128)(2,1)}, bf16[256,8,128]{0,2,1:T(8,128)(2,1)S(1)}, u32[]{:S(2)}) copy-start(bf16[256,8,128]{0,2,1:T(8,128)(2,1)S(1)} %copy.178) | copy-start | bytes 1572868
  908.4 124.2 %copy-start.24 = (bf16[256,8,128]{0,2,1:T(8,128)(2,1)}, bf16[256,8,128]{0,2,1:T(8,128)(2,1)S(1)}, u32[]{:S(2)}) copy-start(bf16[256,8,128]{0,2,1:T(8,128)(2,1)S(1)} %copy.175) | copy-start | bytes 1572868
  908.4 124.2 %copy-start.61 = (bf16[2048,1024]{1,0:T(8,128)(2,1)S(1)}, bf16[2048,1024]{1,0:T(8,128)(2,1)}, u32[]{:S(2)}) copy-start(bf16[2048,1024]{1,0:T(8,128)(2,1)} %param.25) | copy-start | bytes 12582916
  1039.5 217.7 %reduce-scatter.23.cloned.1.call-start = ((), (), s32[]{:S(2)}) async-start(), calls=%async_computation.21 | async-start | bytes 69632 | tf_op jit(solution)/shard_map/reduce_scatter | solution.py:410
  1039.8 66.9 %copy-start.36 = (f32[2048,9]{0,1:T(8,128)}, f32[2048,9]{0,1:T(8,128)S(1)}, u32[]{:S(2)}) copy-start(f32[2048,9]{0,1:T(8,128)S(1)} %fusion.89) | copy-start | bytes 221188
  1040.5 346.3 %reduce-scatter.21.cloned.1.call-start = ((), (), s32[]{:S(2)}) async-start(), calls=%async_computation.20 | async-start | bytes 8912896 | tf_op jit(solution)/shard_map/reduce_scatter | solution.py:416
  1047.0 522.9 %reduce-scatter.19.cloned.1.call-start = ((), (), s32[]{:S(2)}) async-start(), calls=%async_computation.19 | async-start | bytes 8912896 | tf_op jit(solution)/shard_map/reduce_scatter | solution.py:415
  1054.0 698.8 %reduce-scatter.17.cloned.1.call-start = ((), (), s32[]{:S(2)}) async-start(), calls=%async_computation.18 | async-start | bytes 8912896 | tf_op jit(solution)/shard_map/reduce_scatter | solution.py:414
  1060.2 875.7 %reduce-scatter.15.cloned.1.call-start = ((), (), s32[]{:S(2)}) async-start(), calls=%async_computation.17 | async-start | bytes 8912896 | tf_op jit(solution)/shard_map/reduce_scatter | solution.py:413
  1066.2 1348.3 %reduce-scatter.29.cloned.1.call-start = ((), (), s32[]{:S(2)}) async-start(), calls=%async_computation.24 | async-start | bytes 24510464 | tf_op jit(solution)/shard_map/reduce_scatter | solution.py:409
  1078.8 1818.3 %reduce-scatter.27.cloned.1.call-start = ((), (), s32[]{:S(2)}) async-start(), calls=%async_computation.23 | async-start | bytes 24510464 | tf_op jit(solution)/shard_map/reduce_scatter | solution.py:408
  1091.4 2288.2 %reduce-scatter.25.cloned.1.call-start = ((), (), s32[]{:S(2)}) async-start(), calls=%async_computation.22 | async-start | bytes 24510464 | tf_op jit(solution)/shard_map/reduce_scatter | solution.py:407
  (61 other events, 376.1 us)
Sparse Core Ops, SparseCore 0:
  111.8 48.9 all-reduce.12
  565.9 22.7 all-reduce.14
  591.0 103.0 reduce-scatter.34
  696.3 102.7 reduce-scatter.30
  801.3 167.7 reduce-scatter.32
  1039.6 89.3 all-reduce.16
  1132.0 64.6 reduce-scatter.22
  1199.5 187.3 reduce-scatter.20
  1389.7 180.0 reduce-scatter.18
  1572.5 180.2 reduce-scatter.16
  1755.7 180.2 reduce-scatter.14
  1938.7 475.6 reduce-scatter.28
  2417.3 479.7 reduce-scatter.26
  2899.8 479.7 reduce-scatter.24
where the time goes:
time: 3400 us; the launch traced here: 3390 us
  waiting for transfers between devices  2670 us (79%)
  matrix products  263 us (8%)
  local copies, waits for them, and re-layouts  145 us (4%)
  blocking collectives  123 us (4%)
  starting transfers between devices  93.2 us (3%)
  other arithmetic  74 us (2%)
    reduce_scatter x1, waiting for transfers between devices, per_device(): lax.psum_scatter(grad_shared_up, ('dp', 'expert'), scatter_dimension=0, t...  483 us
    reduce_scatter x1, waiting for transfers between devices, per_device(): lax.psum_scatter(grad_shared_gate, ('dp', 'expert'), scatter_dimension=0,...  483 us
    reduce_scatter x1, waiting for transfers between devices, per_device(): lax.psum_scatter(grad_shared_down, ('dp', 'expert'), scatter_dimension=1,...  478 us
    reduce_scatter x1, waiting for transfers between devices, per_device(): lax.psum_scatter(grad_query_weight, ('dp', 'expert'), scatter_dimension=0...  183 us
    reduce_scatter x1, waiting for transfers between devices, per_device(): lax.psum_scatter(grad_key_weight, ('dp', 'expert'), scatter_dimension=0,...  183 us
    reduce_scatter x1, waiting for transfers between devices, per_device(): lax.psum_scatter(grad_value_weight, ('dp', 'expert'), scatter_dimension=0...  183 us
    ppermute x20, waiting for transfers between devices, passed_along(): lax.ppermute(value, axis, [(source, source + steps) for source in range(f...  182 us
    reduce_scatter x1, waiting for transfers between devices, per_device(): lax.psum_scatter(grad_out_weight, ('dp', 'expert'), scatter_dimension=1,...  130 us
  transfers between devices with their start and end apart: 38, of which 18 were waited for; matrix products, arithmetic and copies ran while one was open for 10% of the time, Pallas kernels for 0%

commit v1 on v0

v1 whole, which is shorter than its diff:
```python
import functools

import jax
import jax.numpy as jnp
from jax import lax
from jax.experimental import pallas as pl
from jax.experimental.pallas import tpu as pltpu
from jax.sharding import PartitionSpec as P

HD = 128
SEQ_LEN = 4096
WINDOW = 1024
EPS = 1e-06
THETA = 1000000.0
NEG_LARGE = -1e30
QUERY_BLOCK = 256
F32 = jnp.float32
BF16 = jnp.bfloat16


def dot(left, right):
    return jnp.dot(left, right, preferred_element_type=F32)


def dot_nt(left, right):
    return lax.dot_general(left, right, (((1,), (1,)), ((), ())), preferred_element_type=F32)


def dot_tn(left, right):
    return lax.dot_general(left, right, (((0,), (0,)), ((), ())), preferred_element_type=F32)


def shift_pairs(count, step):
    if count & (count - 1) == 0:
        return [(source, source ^ step) for source in range(count)]
    return [(source, (source + step) % count) for source in range(count)]


def partner(index, count, step):
    if count & (count - 1) == 0:
        return index ^ step
    return (index + step) % count


def source(index, count, step):
    if count & (count - 1) == 0:
        return index ^ step
    return (index - step + count) % count


def gather_plane(own):
    groups, cores = lax.axis_size("expert"), lax.axis_size("tensor")
    mine, core = lax.axis_index("expert"), lax.axis_index("tensor")
    rows, width = own.shape
    pieces = jnp.zeros((groups, rows, width), own.dtype)
    pieces = lax.dynamic_update_slice(pieces, own[None], (mine, 0, 0))
    for step in range(1, groups):
        came = lax.ppermute(own, "expert", shift_pairs(groups, step))
        pieces = lax.dynamic_update_slice(pieces, came[None], (source(mine, groups, step), 0, 0))
    whole = jnp.zeros((groups, cores, rows, width), own.dtype)
    whole = lax.dynamic_update_slice(whole, pieces[:, None], (0, core, 0, 0))
    for step in range(1, cores):
        came = lax.ppermute(pieces, "tensor", shift_pairs(cores, step))
        whole = lax.dynamic_update_slice(whole, came[:, None], (0, source(core, cores, step), 0, 0))
    return whole.reshape(groups * cores * rows, width)


def scatter_plane(partial):
    groups, cores = lax.axis_size("expert"), lax.axis_size("tensor")
    mine, core = lax.axis_index("expert"), lax.axis_index("tensor")
    total, width = partial.shape
    rows = total // (groups * cores)
    blocks = partial.reshape(groups, cores, rows, width)

    def of_core(index):
        return lax.dynamic_slice(blocks, (0, index, 0, 0), (groups, 1, rows, width))[:, 0]

    held = of_core(core).astype(F32)
    for step in range(1, cores):
        sent = of_core(partner(core, cores, step)).astype(BF16)
        held = held + lax.ppermute(sent, "tensor", shift_pairs(cores, step)).astype(F32)

    def of_group(index):
        return lax.dynamic_slice(held, (index, 0, 0), (1, rows, width))[0]

    result = of_group(mine)
    for step in range(1, groups):
        sent = of_group(partner(mine, groups, step)).astype(BF16)
        result = result + lax.ppermute(sent, "expert", shift_pairs(groups, step)).astype(F32)
    return result


def rotate(values, cosine, sine_table):
    rows, width = values.shape
    split = values.reshape(rows, width // HD, 2, HD // 2)
    first_half, second_half = split[:, :, 0], split[:, :, 1]
    cosine = cosine[:, None, :]
    sine_table = sine_table[:, None, :]
    return jnp.concatenate(
        [
            first_half * cosine - second_half * sine_table,
            second_half * cosine + first_half * sine_table,
        ],
        axis=-1,
    ).reshape(rows, width)


def norm_back(values, inv_scale, gain_vec, grad_normed):
    weighted = grad_normed * gain_vec
    inner_mean = jnp.mean(weighted * values, axis=-1, keepdims=True)
    return inv_scale * weighted - values * inv_scale * inv_scale * inv_scale * inner_mean


def masked_scores(query, keys, seg_query, seg_keys, offset):
    scores = dot_nt(query, keys) * (HD ** (-0.5))
    rows, columns = scores.shape
    distance = (
        lax.broadcasted_iota(jnp.int32, (rows, columns), 0)
        - lax.broadcasted_iota(jnp.int32, (rows, columns), 1)
        + offset
    )
    allowed = (seg_query == seg_keys) & (distance >= 0) & (distance < WINDOW)
    return jnp.where(allowed, scores, NEG_LARGE)


def key_ranges(start, block, rows):
    first_before = min(rows, max(0, (start + rows - WINDOW + 1) // block * block))
    first_own = max(0, (start - WINDOW + 1) // block * block)
    return (first_before, rows), (first_own, start + block)


def probabilities(query, parts, seg_query):
    scores = [masked_scores(query, keys, seg_query, seg_keys, offset) for keys, seg_keys, offset in parts]
    top = functools.reduce(jnp.maximum, [jnp.max(part, axis=-1, keepdims=True) for part in scores])
    expo = [jnp.exp(part - top) for part in scores]
    total = functools.reduce(jnp.add, [jnp.sum(part, axis=-1, keepdims=True) for part in expo])
    inverse = 1.0 / total
    return [part * inverse for part in expo]


def attend_kernel(block, q_ref, kb_ref, vb_ref, ko_ref, vo_ref, sq_ref, sb_ref, so_ref, out_ref):
    rows = q_ref.shape[0]
    for start in range(0, rows, block):
        (before, before_end), (own, own_end) = key_ranges(start, block, rows)
        parts, values = [], []
        if before < before_end:
            parts.append((kb_ref[before:before_end, :], sb_ref[:, before:before_end], start + rows - before))
            values.append(vb_ref[before:before_end, :])
        parts.append((ko_ref[own:own_end, :], so_ref[:, own:own_end], start - own))
        values.append(vo_ref[own:own_end, :])
        probs = probabilities(q_ref[start : start + block, :], parts, sq_ref[start : start + block, :])
        total = functools.reduce(
            jnp.add, [dot(part.astype(BF16), value) for part, value in zip(probs, values, strict=True)]
        )
        out_ref[start : start + block, :] = total.astype(BF16)


def attend_back_kernel(
    block,
    q_ref,
    kb_ref,
    vb_ref,
    ko_ref,
    vo_ref,
    sq_ref,
    sb_ref,
    so_ref,
    grad_ref,
    gq_ref,
    gkb_ref,
    gvb_ref,
    gko_ref,
    gvo_ref,
):
    rows = q_ref.shape[0]
    for ref in (gkb_ref, gvb_ref, gko_ref, gvo_ref):
        ref[...] = jnp.zeros_like(ref)
    scale = HD ** (-0.5)
    for start in range(0, rows, block):
        (before, before_end), (own, own_end) = key_ranges(start, block, rows)
        query = q_ref[start : start + block, :]
        grad = grad_ref[start : start + block, :]
        parts, values, sinks = [], [], []
        if before < before_end:
            parts.append((kb_ref[before:before_end, :], sb_ref[:, before:before_end], start + rows - before))
            values.append(vb_ref[before:before_end, :])
            sinks.append((gkb_ref, gvb_ref, before, before_end))
        parts.append((ko_ref[own:own_end, :], so_ref[:, own:own_end], start - own))
        values.append(vo_ref[own:own_end, :])
        sinks.append((gko_ref, gvo_ref, own, own_end))
        probs = probabilities(query, parts, sq_ref[start : start + block, :])
        grad_probs = [dot_nt(grad, value) for value in values]
        delta = functools.reduce(
            jnp.add,
            [jnp.sum(p * g, axis=-1, keepdims=True) for p, g in zip(probs, grad_probs, strict=True)],
        )
        grad_query = None
        for p, g, part, (gk_ref, gv_ref, low, high) in zip(probs, grad_probs, parts, sinks, strict=True):
            grad_scores = (p * (g - delta)).astype(BF16)
            term = dot(grad_scores, part[0])
            grad_query = term if grad_query is None else grad_query + term
            gk_ref[low:high, :] += dot_tn(grad_scores, query) * scale
            gv_ref[low:high, :] += dot_tn(p.astype(BF16), grad)
        gq_ref[start : start + block, :] = grad_query * scale


def attention_specs(rows, heads):
    column = pl.BlockSpec((rows, HD), lambda h: (0, h))
    value_column = pl.BlockSpec((rows, HD), lambda h: (0, heads + h))
    seg_rows = pl.BlockSpec((rows, 1), lambda h: (0, 0))
    seg_columns = pl.BlockSpec((1, rows), lambda h: (0, 0))
    return column, [column, column, value_column, column, value_column, seg_rows, seg_columns, seg_columns]


def attend(query, before, own, seg_rows, seg_before, seg_own):
    rows, width = query.shape
    heads = width // HD
    column, specs = attention_specs(rows, heads)
    return pl.pallas_call(
        functools.partial(attend_kernel, min(QUERY_BLOCK, rows)),
        grid=(heads,),
        in_specs=specs,
        out_specs=column,
        out_shape=jax.ShapeDtypeStruct((rows, width), BF16),
        compiler_params=pltpu.CompilerParams(vmem_limit_bytes=48 * 2**20),
        cost_estimate=pl.CostEstimate(
            flops=4 * rows * WINDOW * width, bytes_accessed=12 * rows * width, transcendentals=rows * WINDOW * heads
        ),
        name="attend",
    )(query, before, before, own, own, seg_rows, seg_before, seg_own)


def attend_back(query, before, own, seg_rows, seg_before, seg_own, grad_heads):
    rows, width = query.shape
    heads = width // HD
    column, specs = attention_specs(rows, heads)
    return pl.pallas_call(
        functools.partial(attend_back_kernel, min(QUERY_BLOCK, rows)),
        grid=(heads,),
        in_specs=specs + [column],
        out_specs=[column] * 5,
        out_shape=[jax.ShapeDtypeStruct((rows, width), F32)] * 5,
        compiler_params=pltpu.CompilerParams(vmem_limit_bytes=48 * 2**20),
        cost_estimate=pl.CostEstimate(
            flops=10 * rows * WINDOW * width, bytes_accessed=32 * rows * width, transcendentals=rows * WINDOW * heads
        ),
        name="attend_back",
    )(query, before, before, own, own, seg_rows, seg_before, seg_own, grad_heads)


def per_device(
    tokens,
    segments,
    routes,
    attn_gain,
    query_weight,
    query_bias,
    key_weight,
    key_bias,
    value_weight,
    value_bias,
    out_weight,
    mlp_gain,
    router_weight,
    shared_router,
    shared_gate,
    shared_up,
    shared_down,
    expert_gate,
    expert_up,
    expert_down,
    grad_out,
):
    tok_rows, model_width = tokens.shape
    groups, cores = lax.axis_size("expert"), lax.axis_size("tensor")
    planes = lax.axis_size("dp")
    mine, core, plane = lax.axis_index("expert"), lax.axis_index("tensor"), lax.axis_index("dp")
    rows = tok_rows // cores
    plane_rows = tok_rows * groups
    heads_here = query_weight.shape[1] // HD
    width = query_weight.shape[1] // groups
    heads = width // HD
    local_experts, _, hidden = expert_gate.shape
    expert_count = local_experts * groups
    shared_hidden = shared_gate.shape[1] // groups

    picks = jnp.sum(1 << routes, axis=1).astype(jnp.int32)
    facts = lax.all_gather(jnp.stack([segments, picks]), ("dp", "expert"), axis=1, tiled=True)
    facts_own = lax.dynamic_slice(facts, (0, plane * plane_rows), (2, plane_rows))
    seg_own = facts_own[:1]
    seg_before = lax.dynamic_slice(facts, (0, jnp.maximum(plane - 1, 0) * plane_rows), (1, plane_rows))
    seg_before = jnp.where(plane > 0, seg_before, -1)
    seg_rows = seg_own.reshape(plane_rows, 1)
    chosen = (facts_own[1][:, None] >> jnp.arange(expert_count, dtype=jnp.int32)[None, :]) & 1

    grad_top_plane = lax.all_gather(grad_out, "expert", axis=0, tiled=True)

    own_tokens = lax.dynamic_slice(tokens, (core * rows, 0), (rows, model_width))
    inputs = own_tokens.astype(F32)
    gain_one = attn_gain.astype(F32)
    scale_one = lax.rsqrt(jnp.mean(inputs * inputs, axis=-1, keepdims=True) + EPS)
    normed_one = gather_plane((inputs * scale_one * gain_one).astype(BF16))

    def columns(weight):
        return lax.dynamic_slice(weight, (0, mine * width), (model_width, width))

    def bias_of(bias):
        return lax.dynamic_slice(bias, (mine * heads, 0), (heads, HD)).reshape(1, width).astype(F32)

    weight_kv = jnp.concatenate([columns(key_weight), columns(value_weight)], axis=1)
    weight_q = columns(query_weight)
    row_index = plane * plane_rows + jnp.arange(plane_rows, dtype=jnp.int32)
    places = (row_index % SEQ_LEN).astype(F32)
    frequency = THETA ** (-2.0 * jnp.arange(HD // 2, dtype=F32) / HD)
    angles = places[:, None] * frequency[None, :]
    cosine = jnp.cos(angles)
    sine_table = jnp.sin(angles)
    kv_pre = dot(normed_one, weight_kv) + jnp.concatenate([bias_of(key_bias), bias_of(value_bias)], axis=1)
    own_kv = jnp.concatenate(
        [rotate(kv_pre[:, :width], cosine, sine_table).astype(BF16), kv_pre[:, width:].astype(BF16)], axis=1
    )
    before_kv = lax.ppermute(own_kv, "dp", [(i, i + 1) for i in range(planes - 1)])
    query_pre = dot(normed_one, weight_q) + bias_of(query_bias)
    query_rot = rotate(query_pre, cosine, sine_table).astype(BF16)
    attended = attend(query_rot, before_kv, own_kv, seg_rows, seg_before, seg_own)
    out_rows = lax.dynamic_slice(out_weight, (mine * width, 0), (width, model_width))
    after_attn = inputs + scatter_plane(dot(attended, out_rows))

    gain_two = mlp_gain.astype(F32)
    scale_two = lax.rsqrt(jnp.mean(after_attn * after_attn, axis=-1, keepdims=True) + EPS)
    normed_two = gather_plane((after_attn * scale_two * gain_two).astype(BF16))
    gate_columns = jnp.concatenate([router_weight, shared_router[:, None]], axis=1)
    small_logits = dot(normed_two, gate_columns)
    router_probs = jax.nn.softmax(small_logits[:, :expert_count], axis=-1)
    shared_mix = jax.nn.sigmoid(small_logits[:, expert_count:])
    combine = router_probs * chosen.astype(F32)
    own_gates = lax.dynamic_slice(combine, (0, mine * local_experts), (plane_rows, local_experts))

    def shared_columns(weight):
        return lax.dynamic_slice(weight, (0, mine * shared_hidden), (model_width, shared_hidden))

    shared_rows = lax.dynamic_slice(shared_down, (mine * shared_hidden, 0), (shared_hidden, model_width))
    segments_of_hidden = [
        (expert_gate[e], expert_up[e], expert_down[e], own_gates[:, e : e + 1]) for e in range(local_experts)
    ] + [(shared_columns(shared_gate), shared_columns(shared_up), shared_rows, shared_mix)]
    mixed_part, grad_normed_part = None, None
    gate_slopes, gate_grads, up_grads, down_grads = [], [], [], []
    for w_gate, w_up, w_down, gate in segments_of_hidden:
        gate_val = dot(normed_two, w_gate)
        up_val = dot(normed_two, w_up)
        inner_grad = dot_nt(grad_top_plane, w_down)
        sigmoid_val = jax.nn.sigmoid(gate_val)
        silu_val = gate_val * sigmoid_val
        inner = silu_val * up_val
        gate_slopes.append(jnp.sum(inner * inner_grad, axis=-1, keepdims=True))
        gated = (gate * inner).astype(BF16)
        inner_grad = gate * inner_grad
        grad_gate_val = (inner_grad * up_val * (sigmoid_val * (1.0 + gate_val * (1.0 - sigmoid_val)))).astype(BF16)
        grad_up_val = (inner_grad * silu_val).astype(BF16)
        term = dot(gated, w_down)
        mixed_part = term if mixed_part is None else mixed_part + term
        term = dot_nt(grad_gate_val, w_gate) + dot_nt(grad_up_val, w_up)
        grad_normed_part = term if grad_normed_part is None else grad_normed_part + term
        down_grads.append(dot_tn(gated, grad_top_plane).astype(BF16))
        gate_grads.append(dot_tn(normed_two, grad_gate_val).astype(BF16))
        up_grads.append(dot_tn(normed_two, grad_up_val).astype(BF16))

    slopes = jnp.concatenate(gate_slopes[:local_experts], axis=1)
    slopes = lax.dynamic_update_slice(
        jnp.zeros((plane_rows, expert_count), F32), slopes, (0, mine * local_experts)
    ) * chosen.astype(F32)
    grad_logits = router_probs * (slopes - jnp.sum(router_probs * slopes, axis=-1, keepdims=True))
    grad_shared_logit = gate_slopes[local_experts] * shared_mix * (1.0 - shared_mix)
    grad_small = jnp.concatenate([grad_logits, grad_shared_logit], axis=1).astype(BF16)
    grad_normed_part = grad_normed_part + dot_nt(grad_small, gate_columns)
    grad_columns = dot_tn(normed_two, grad_small)
    mixed_part = mixed_part.astype(BF16)
    mixed = lax.psum_scatter(mixed_part, ("expert", "tensor"), scatter_dimension=0, tiled=True)
    out_own = (after_attn + mixed.astype(F32)).astype(BF16)
    out = lax.all_gather(out_own, "tensor", axis=0, tiled=True)

    def summed_rows(pieces):
        return lax.psum_scatter(jnp.concatenate(pieces, axis=1), "dp", scatter_dimension=0, tiled=True)

    def shared_of_rows(values):
        part_rows = values.shape[0] // groups
        return (
            lax.all_to_all(values.reshape(groups, part_rows, shared_hidden), "expert", 0, 0)
            .transpose(1, 0, 2)
            .reshape(part_rows, groups * shared_hidden)
        )

    gate_sum = summed_rows(gate_grads)
    up_sum = summed_rows(up_grads)
    down_sum = lax.psum_scatter(jnp.concatenate(down_grads, axis=0), "dp", scatter_dimension=1, tiled=True)
    routed = local_experts * hidden
    part_rows = model_width // planes

    def expert_columns(values):
        return values[:, :routed].reshape(part_rows, local_experts, hidden).transpose(1, 0, 2).astype(F32)

    grad_expert_gate = expert_columns(gate_sum)
    grad_expert_up = expert_columns(up_sum)
    grad_expert_down = down_sum[:routed].reshape(local_experts, hidden, part_rows).astype(F32)
    grad_shared_gate = shared_of_rows(gate_sum[:, routed:]).astype(F32)
    grad_shared_up = shared_of_rows(up_sum[:, routed:]).astype(F32)
    grad_shared_down = lax.all_to_all(
        down_sum[routed:].reshape(shared_hidden, groups, part_rows // groups), "expert", 1, 0
    ).reshape(groups * shared_hidden, part_rows // groups).astype(F32)

    grad_top = lax.dynamic_slice(grad_out, (core * rows, 0), (rows, model_width)).astype(F32)
    grad_normed_two = scatter_plane(grad_normed_part)
    grad_mlp_gain = jnp.sum(grad_normed_two * after_attn * scale_two, axis=0)
    grad_after = grad_top + norm_back(after_attn, scale_two, gain_two, grad_normed_two)

    grad_attended = gather_plane(grad_after.astype(BF16))
    grad_heads = dot_nt(grad_attended, out_rows).astype(BF16)
    grad_out_part = dot_tn(attended, grad_attended).astype(BF16)
    grad_query_rot, back_keys, back_values, own_keys, own_values = attend_back(
        query_rot, before_kv, own_kv, seg_rows, seg_before, seg_own, grad_heads
    )
    back_kv = jnp.concatenate([back_keys, back_values], axis=1).astype(BF16)
    came_kv = lax.ppermute(back_kv, "dp", [(i + 1, i) for i in range(planes - 1)]).astype(F32)
    grad_query = rotate(grad_query_rot, cosine, -sine_table).astype(BF16)
    grad_key = rotate(own_keys + came_kv[:, :width], cosine, -sine_table).astype(BF16)
    grad_value = (own_values + came_kv[:, width:]).astype(BF16)
    grad_qkv = jnp.concatenate([grad_query, grad_key, grad_value], axis=1)
    weight_qkv = jnp.concatenate([weight_q, weight_kv], axis=1)
    grad_normed_one = scatter_plane(dot_nt(grad_qkv, weight_qkv))
    grad_attn_gain = jnp.sum(grad_normed_one * inputs * scale_one, axis=0)
    grad_own = grad_after + norm_back(inputs, scale_one, gain_one, grad_normed_one)
    grad_tokens = lax.all_gather(grad_own, "tensor", axis=0, tiled=True)

    grad_qkv_part = dot_tn(normed_one, grad_qkv).astype(BF16)
    qkv_sum = lax.psum_scatter(grad_qkv_part, "dp", scatter_dimension=0, tiled=True)
    qkv_rows = (
        lax.all_to_all(qkv_sum.reshape(groups, part_rows // groups, 3, width), "expert", 0, 0)
        .transpose(2, 1, 0, 3)
        .reshape(3, part_rows // groups, groups * width)
        .astype(F32)
    )
    out_sum = lax.psum_scatter(grad_out_part, "dp", scatter_dimension=1, tiled=True)
    grad_out_weight = lax.all_to_all(
        out_sum.reshape(width, groups, part_rows // groups), "expert", 1, 0
    ).reshape(groups * width, part_rows // groups).astype(F32)

    bias_sums = jnp.sum(grad_qkv, axis=0, dtype=F32).reshape(1, 3, heads, HD)
    bias_table = lax.dynamic_update_slice(
        jnp.zeros((cores, 3, heads_here, HD), F32), bias_sums, (core, 0, mine * heads, 0)
    )
    devices = planes * groups
    spread = jnp.concatenate(
        [
            grad_attn_gain.reshape(devices, -1),
            grad_mlp_gain.reshape(devices, -1),
            grad_columns.reshape(devices, -1),
            bias_table.reshape(cores * 3 * heads_here, devices, HD // devices).transpose(1, 0, 2).reshape(devices, -1),
        ],
        axis=1,
    )
    sums = lax.psum_scatter(lax.psum(spread, "tensor"), ("dp", "expert"), scatter_dimension=0, tiled=True)[0]
    gain_part = model_width // devices
    grad_attn_gain, grad_mlp_gain = sums[:gain_part], sums[gain_part : 2 * gain_part]
    table = sums[2 * gain_part :]
    column_size = gain_part * (expert_count + 1)
    column_sums = table[:column_size].reshape(gain_part, expert_count + 1)
    bias_sums = table[column_size:].reshape(cores, 3, heads_here, HD // devices)
    bias_sums = lax.dynamic_slice(bias_sums, (core, 0, 0, 0), (1, 3, heads_here, HD // devices))[0]
    return (
        out,
        grad_tokens,
        grad_attn_gain,
        qkv_rows[0],
        bias_sums[0],
        qkv_rows[1],
        bias_sums[1],
        qkv_rows[2],
        bias_sums[2],
        grad_out_weight,
        grad_mlp_gain,
        column_sums[:, :expert_count],
        column_sums[:, expert_count],
        grad_shared_gate,
        grad_shared_up,
        grad_shared_down,
        grad_expert_gate,
        grad_expert_up,
        grad_expert_down,
    )


def solution(mesh):
    tokens = ("dp", "expert")
    return jax.shard_map(
        per_device,
        mesh=mesh,
        in_specs=(
            P(tokens, None),
            P(tokens),
            P(tokens, None),
            P(),
            P(None, "tensor"),
            P("tensor", None),
            P(None, "tensor"),
            P("tensor", None),
            P(None, "tensor"),
            P("tensor", None),
            P("tensor", None),
            P(),
            P(),
            P(),
            P(None, "tensor"),
            P(None, "tensor"),
            P("tensor", None),
            P("expert", None, "tensor"),
            P("expert", None, "tensor"),
            P("expert", "tensor", None),
            P(tokens, None),
        ),
        out_specs=(
            P(tokens, None),
            P(tokens, None),
            P(tokens),
            P(tokens, "tensor"),
            P("tensor", tokens),
            P(tokens, "tensor"),
            P("tensor", tokens),
            P(tokens, "tensor"),
            P("tensor", tokens),
            P("tensor", tokens),
            P(tokens),
            P(tokens, None),
            P(tokens),
            P(tokens, "tensor"),
            P(tokens, "tensor"),
            P("tensor", tokens),
            P("expert", "dp", "tensor"),
            P("expert", "dp", "tensor"),
            P("expert", "tensor", "dp"),
        ),
        check_vma=False,
    )
```

time: 3400 us -> 1240 us (0.36)
  waiting for transfers between devices: 2670 us -> 734 us
  local copies, waits for them, and re-layouts: 145 us -> 59.7 us
  blocking collectives: 123 us -> 54.5 us
  matrix products: 263 us -> 219 us
  starting transfers between devices: 93.2 us -> 59.1 us
    reduce_scatter x11 -> x6, waiting for transfers between devices: 2120 us -> 494 us  [the longest x2 294 us: summed_rows(): lax.psum_scatter(jnp.concatenate(pieces, axis=1), 'dp', scatter_dimension...]
    all_to_all x4 -> x5, waiting for transfers between devices: 308 us -> 4.91 us  [the longest x1 3.63 us: per_device(): lax.all_to_all(out_sum.reshape(width, groups, part_rows // groups), 'expe...]
    unnamed x1 -> x0, blocking collectives: 118 us -> none
    psum x3 -> x0, waiting for transfers between devices: 57.7 us -> none  [the longest x1 45.6 us: per_device(): after_attn = inputs + lax.psum(attn_part, 'tensor')]
    all_gather x0 -> x1, blocking collectives: none -> 49.9 us  [per_device(): lax.all_gather(jnp.stack([segments, picks]), ('dp', 'expert'), axis=1, ti...]
    dot_general x39 -> x37, matrix products: 263 us -> 219 us  [the longest x12 100 us: dot_nt(): lax.dot_general(left, right, (((1,), (1,)), ((), ())), preferred_element_...]
    ppermute x20 -> x26, waiting for transfers between devices: 182 us -> 180 us  [the longest x9 63.9 us: gather_plane(): came = lax.ppermute(own, 'expert', shift_pairs(groups, step))]
  transfers between devices with their start and end apart: 38 -> 41, of which waited for: 18 -> 30; matrix products, arithmetic and copies ran while one was open for 10% -> 19% of each run, Pallas kernels for 0% -> 0%
where the time goes in v1:
time: 1240 us; the launch traced here: 1230 us
  waiting for transfers between devices  734 us (59%)
  matrix products  219 us (18%)
  other arithmetic  65.8 us (5%)
  local copies, waits for them, and re-layouts  59.7 us (5%)
  starting transfers between devices  59.1 us (5%)
  blocking collectives  54.5 us (4%)
  Pallas kernels  20.8 us (2%)
  between operations  16.1 us (1%)
    reduce_scatter x2, waiting for transfers between devices, summed_rows(): lax.psum_scatter(jnp.concatenate(pieces, axis=1), 'dp', scatter_dimension...  294 us
    reduce_scatter x1, waiting for transfers between devices, per_device(): lax.psum_scatter(jnp.concatenate(down_grads, axis=0), 'dp', scatter_dimen...  142 us
    dot_general x12, matrix products, dot_nt(): lax.dot_general(left, right, (((1,), (1,)), ((), ())), preferred_element_...  100 us
    ppermute x9, waiting for transfers between devices, gather_plane(): came = lax.ppermute(own, 'expert', shift_pairs(groups, step))  63.9 us
    dot_general x13, matrix products, dot(): return jnp.dot(left, right, preferred_element_type=F32)  63.8 us
    ppermute x9, waiting for transfers between devices, scatter_plane(): lax.ppermute(sent, 'expert', shift_pairs(groups, step)).astype(F32)  63.7 us
    reduce_scatter x1, waiting for transfers between devices, per_device(): lax.psum_scatter(grad_qkv_part, 'dp', scatter_dimension=0, tiled=True)  57.6 us
    dot_general x12, matrix products, dot_tn(): lax.dot_general(left, right, (((0,), (0,)), ((), ())), preferred_element_...  55.2 us
  transfers between devices with their start and end apart: 41, of which 30 were waited for; matrix products, arithmetic and copies ran while one was open for 19% of the time, Pallas kernels for 0%

profile of v1, /device:TPU:1, one launch (start us, length us, event | category | flops | bytes accessed | tf_op | source)
XLA Modules:
  0.0 1229.2 jit_solution(16027989091449838165)
XLA Ops:
  13.8 10.7 collective-permute-done
  25.7 10.9 collective-permute-done.2
  60.0 49.9 %all_gather.12 = s32[2,4096]{1,0:T(2,128)S(1)} all-gather(s32[2,256]{1,0:T(2,128)S(1)} %pad_add_fusion), channel_id=1, replica_groups=mesh['dp'=4,'expert'=4,'tensor'=2] {'dp','expert'}, dimensions={1}, use_global_device_ids=true | all-gather | bytes 34816 | tf_op jit(solution)/shard_map/all_gather | solution.py:288
  113.3 7.1 attend.1
  123.4 7.4 collective-permute-start.5
  138.4 10.5 collective-permute-done.6
  148.9 11.3 collective-permute-done.7
  164.0 9.6 collective-permute-done.9
  174.1 11.6 collective-permute-done.11
  195.5 4.7 fusion.25
  200.3 4.7 fusion.13
  209.8 5.1 fusion.17
  214.9 22.9 %all-gather.6.cloned.1.call-done = bf16[1024,2048]{1,0:T(8,128)(2,1)} async-done(((bf16[256,2048]{1,0:T(8,128)(2,1)}), bf16[1024,2048]{1,0:T(8,128)(2,1)}) %all-gather.6.cloned.1.call-update) | async-done | bytes 4194320 | tf_op jit(solution)/shard_map/all_gather | solution.py:296
  237.8 8.4 multiply_reduce_fusion.1
  246.3 5.5 multiply_reduce_fusion
  251.9 6.1 fusion.40
  258.1 7.9 fusion.36
  265.9 9.1 fusion.6
  278.3 5.9 fusion.21
  287.2 5.7 fusion.9
  297.1 8.7 add_convert_fusion
  306.3 9.5 fusion.23
  315.8 8.0 fusion.27
  323.8 5.7 fusion.11
  329.6 5.7 fusion.15
  335.2 9.7 fusion.34
  344.9 9.5 fusion.38
  354.5 20.5 %add_add_fusion = f32[1024,2048]{1,0:T(8,128)} fusion(f32[1024,2048]{1,0:T(8,128)} %fusion.38, f32[1024,2048]{1,0:T(8,128)} %fusion.34, f32[1024,2048]{1,0:T(8,128)} %fusion.15, f32[1024,2048]{1,0:T(8,128)} %fusion.11, f32[1024,2048]{1,0:T(8,128)} %fusion.27, f32[1024,2048]{1,0:T(8,128)} %fusion.23, ...), kind=kOutput, calls=%fused_computation.3 | convolution fusion | flops 50368512 | bytes 58775552 | tf_op jit(solution)/shard_map/dot_general | solution.py:26
  389.9 10.6 collective-permute-done.14
  401.2 11.3 collective-permute-done.16
  420.1 9.3 collective-permute-done.17
  429.5 11.5 collective-permute-done.19
  450.9 13.7 %attend_back.1 = (f32[1024,256]{1,0:T(8,128)S(1)}, f32[1024,256]{1,0:T(8,128)S(1)}, f32[1024,256]{1,0:T(8,128)S(1)}, f32[1024,256]{1,0:T(8,128)S(1)}, f32[1024,256]{1,0:T(8,128)}) custom-call(bf16[1024,256]{1,0:T(8,128)(2,1)S(1)} %copy.177.q_ref, bf16[1024,512]{1,0:T(8,128)(2,1)} %copy-done.1, bf16[1024,512]{1,0:T(8,128)(2,1)} %copy-done.1, ...), custom_call_target="tpu_custom_call" | custom-call | flops 2684354560 | bytes 8388608 | tf_op jit(solution)/shard_map/attend_back/pallas_call | solution.py:237
  473.0 34.9 %collective-permute-done.21 = bf16[1024,512]{1,0:T(8,128)(2,1)} collective-permute-done((bf16[1024,512]{1,0:T(8,128)(2,1)}, bf16[1024,512]{1,0:T(8,128)(2,1)}, u32[]{:S(2)}, u32[]{:S(2)}) %collective-permute-start.21) | collective-permute-done | bytes 1048608 | tf_op jit(solution)/shard_map/ppermute | solution.py:423
  514.6 5.3 fusion
  543.0 7.0 collective-permute-done.23
  550.9 11.3 collective-permute-done.25
  565.7 7.6 convolution_convert_fusion
  573.4 5.9 convolution_convert_fusion.3
  590.4 7.4 convolution_convert_fusion.6
  599.4 5.9 convolution_convert_fusion.5
  614.2 5.7 convolution_convert_fusion.9
  641.2 25.6 %all-reduce.3.cloned.1.call-done = f32[16,1792]{1,0:T(8,128)} async-done(((f32[16,1792]{1,0:T(8,128)}), f32[16,1792]{1,0:T(8,128)}) %all-reduce.3.cloned.1.call-update) | async-done | bytes 114704
  672.9 57.6 %reduce-scatter.9.cloned.1.call-done = bf16[512,768]{1,0:T(8,128)(2,1)} async-done(((bf16[2048,768]{1,0:T(8,128)(2,1)}), bf16[512,768]{1,0:T(8,128)(2,1)}) %reduce-scatter.9.cloned.1.call-update) | async-done | bytes 786448 | tf_op jit(solution)/shard_map/reduce_scatter | solution.py:435
  738.9 142.6 %reduce-scatter.15.cloned.1.call-done = bf16[512,2112]{0,1:T(8,128)(2,1)} async-done(((bf16[2048,2112]{0,1:T(8,128)(2,1)}), bf16[512,2112]{0,1:T(8,128)(2,1)}) %reduce-scatter.15.cloned.1.call-update) | async-done | bytes 2162704 | tf_op jit(solution)/shard_map/reduce_scatter | solution.py:383
  888.9 6.7 all-gather.8.cloned.1.call-done
  895.6 151.7 %reduce-scatter.13.cloned.1.call-done = bf16[512,2112]{0,1:T(8,128)(2,1)} async-done(((bf16[2048,2112]{0,1:T(8,128)(2,1)}), bf16[512,2112]{0,1:T(8,128)(2,1)}) %reduce-scatter.13.cloned.1.call-update) | async-done | bytes 2162704 | tf_op jit(solution)/shard_map/reduce_scatter | solution.py:383
  1056.8 142.1 %reduce-scatter.17.cloned.1.call-done = bf16[2112,512]{1,0:T(8,128)(2,1)} async-done(((bf16[2112,2048]{1,0:T(8,128)(2,1)}), bf16[2112,512]{1,0:T(8,128)(2,1)}) %reduce-scatter.17.cloned.1.call-update) | async-done | bytes 2162704 | tf_op jit(solution)/shard_map/reduce_scatter | solution.py:395
  (404 shorter events, 246.7 us)
Async XLA Ops:
  7.2 230.6 %all-gather.6.cloned.1.call-start = ((), (), s32[]{:S(2)}) async-start(), calls=%async_computation.13 | async-start | bytes 5242880 | tf_op jit(solution)/shard_map/all_gather | solution.py:296
  10.5 14.0 %collective-permute-start = (bf16[128,2048]{1,0:T(8,128)(2,1)}, bf16[128,2048]{1,0:T(8,128)(2,1)}, u32[]{:S(2)}, u32[]{:S(2)}) collective-permute-start(bf16[128,2048]{1,0:T(8,128)(2,1)} %get-tuple-element.104), channel_id=1, source_target_pairs={{0,2},{2,0},{4,6},{6,4},{1,3},{3,1},{5,7},{7,5},{8,10},{10,8},{12,... | collective-permute-start | bytes 1572872 | tf_op jit(solution)/shard_map/ppermute | solution.py:58
  12.6 13.0 %collective-permute-start.1 = (bf16[128,2048]{1,0:T(8,128)(2,1)}, bf16[128,2048]{1,0:T(8,128)(2,1)S(1)}, u32[]{:S(2)}, u32[]{:S(2)}) collective-permute-start(bf16[128,2048]{1,0:T(8,128)(2,1)} %get-tuple-element.104), channel_id=1, source_target_pairs={{0,4},{2,6},{4,0},{6,2},{1,5},{3,7},{5,1},{7,3},{8,12},{10,14},{12... | collective-permute-start | bytes 1572872 | tf_op jit(solution)/shard_map/ppermute | solution.py:58
  13.8 22.8 %collective-permute-start.2 = (bf16[128,2048]{1,0:T(8,128)(2,1)}, bf16[128,2048]{1,0:T(8,128)(2,1)S(1)}, u32[]{:S(2)}, u32[]{:S(2)}) collective-permute-start(bf16[128,2048]{1,0:T(8,128)(2,1)} %get-tuple-element.104), channel_id=1, source_target_pairs={{0,6},{2,4},{4,2},{6,0},{1,7},{3,5},{5,3},{7,1},{8,14},{10,12},{12... | collective-permute-start | bytes 1572872 | tf_op jit(solution)/shard_map/ppermute | solution.py:58
  36.7 10.0 collective-permute-start.3
  56.6 63.7 %copy-start = (bf16[1024,512]{1,0:T(8,128)(2,1)}, bf16[1024,512]{1,0:T(8,128)(2,1)S(1)}, u32[]{:S(2)}) copy-start(bf16[1024,512]{1,0:T(8,128)(2,1)S(1)} %pad_maximum_fusion.4.ko_ref.vo_ref) | copy-start | bytes 3145732
  56.6 56.6 %collective-permute-start.4 = (bf16[1024,512]{1,0:T(8,128)(2,1)S(1)}, bf16[1024,512]{1,0:T(8,128)(2,1)S(1)}, u32[]{:S(2)}, u32[]{:S(2)}) collective-permute-start(bf16[1024,512]{1,0:T(8,128)(2,1)S(1)} %pad_maximum_fusion.4.ko_ref.vo_ref), channel_id=1, source_target_pairs={{0,8},{8,16},{16,24},{1,9},{9,17},{17,25},{2,10},{10,18},{18,26},{... | collective-permute-start | bytes 3145736 | tf_op jit(solution)/shard_map/ppermute | solution.py:322
  123.4 11.2 collective-permute-start.5
  135.7 13.2 %collective-permute-start.6 = (bf16[128,2048]{1,0:T(8,128)(2,1)S(1)}, bf16[128,2048]{1,0:T(8,128)(2,1)S(1)}, u32[]{:S(2)}, u32[]{:S(2)}) collective-permute-start(bf16[128,2048]{1,0:T(8,128)(2,1)S(1)} %get-tuple-element.120), channel_id=1, source_target_pairs={{0,2},{2,0},{4,6},{6,4},{1,3},{3,1},{5,7},{7,5},{8,10},{10,8},{12,... | collective-permute-start | bytes 1572872 | tf_op jit(solution)/shard_map/ppermute | solution.py:89
  135.8 24.4 %collective-permute-start.7 = (bf16[128,2048]{1,0:T(8,128)(2,1)S(1)}, bf16[128,2048]{1,0:T(8,128)(2,1)S(1)}, u32[]{:S(2)}, u32[]{:S(2)}) collective-permute-start(bf16[128,2048]{1,0:T(8,128)(2,1)S(1)} %get-tuple-element.122), channel_id=1, source_target_pairs={{0,4},{2,6},{4,0},{6,2},{1,5},{3,7},{5,1},{7,3},{8,12},{10,14},{12... | collective-permute-start | bytes 1572872 | tf_op jit(solution)/shard_map/ppermute | solution.py:89
  135.9 24.4 %collective-permute-start.8 = (bf16[128,2048]{1,0:T(8,128)(2,1)S(1)}, bf16[128,2048]{1,0:T(8,128)(2,1)S(1)}, u32[]{:S(2)}, u32[]{:S(2)}) collective-permute-start(bf16[128,2048]{1,0:T(8,128)(2,1)S(1)} %get-tuple-element.121), channel_id=1, source_target_pairs={{0,6},{2,4},{4,2},{6,0},{1,7},{3,5},{5,3},{7,1},{8,14},{10,12},{12... | collective-permute-start | bytes 1572872 | tf_op jit(solution)/shard_map/ppermute | solution.py:89
  161.1 27.4 %copy-start.61 = (bf16[2048,8]{0,1:T(8,128)(2,1)S(1)}, bf16[2048,8]{0,1:T(8,128)(2,1)}, u32[]{:S(2)}) copy-start(bf16[2048,8]{0,1:T(8,128)(2,1)} %param.33) | copy-start | bytes 98308
  161.1 27.4 %copy-start.67 = (bf16[2048]{0:T(1024)(128)(2,1)S(1)}, bf16[2048]{0:T(1024)(128)(2,1)}, u32[]{:S(2)}) copy-start(bf16[2048]{0:T(1024)(128)(2,1)} %param.34) | copy-start | bytes 12292
  161.3 12.3 collective-permute-start.9
  162.4 11.6 collective-permute-start.10
  162.8 22.8 %collective-permute-start.11 = (bf16[128,2048]{1,0:T(8,128)(2,1)S(1)}, bf16[128,2048]{1,0:T(8,128)(2,1)S(1)}, u32[]{:S(2)}, u32[]{:S(2)}) collective-permute-start(bf16[128,2048]{1,0:T(8,128)(2,1)S(1)} %get-tuple-element.100), channel_id=1, source_target_pairs={{0,6},{2,4},{4,2},{6,0},{1,7},{3,5},{5,3},{7,1},{8,14},{10,12},{12... | collective-permute-start | bytes 1572872 | tf_op jit(solution)/shard_map/ppermute | solution.py:58
  185.7 6.4 collective-permute-start.12
  188.2 224.3 %reduce-scatter.7.cloned.1.call-start = ((), (), s32[]{:S(2)}) async-start(), calls=%async_computation.11 | async-start | bytes 4718592 | tf_op jit(solution)/shard_map/reduce_scatter | solution.py:378
  287.1 42.4 %copy-start.46 = (bf16[1024,704]{0,1:T(8,128)(2,1)}, bf16[1024,704]{0,1:T(8,128)(2,1)S(1)}, u32[]{:S(2)}) copy-start(bf16[1024,704]{0,1:T(8,128)(2,1)S(1)} %get-tuple-element.109) | copy-start | bytes 4325380
  305.8 325.1 %reduce-scatter.11.cloned.1.call-start = ((), (), s32[]{:S(2)}) async-start(), calls=%async_computation.16 | async-start | bytes 1310720 | tf_op jit(solution)/shard_map/reduce_scatter | solution.py:442
  377.5 4.6 collective-permute-start.13
  387.2 13.3 %collective-permute-start.14 = (bf16[128,2048]{1,0:T(8,128)(2,1)S(1)}, bf16[128,2048]{1,0:T(8,128)(2,1)}, u32[]{:S(2)}, u32[]{:S(2)}) collective-permute-start(bf16[128,2048]{1,0:T(8,128)(2,1)S(1)} %get-tuple-element.117), channel_id=1, source_target_pairs={{0,2},{2,0},{4,6},{6,4},{1,3},{3,1},{5,7},{7,5},{8,10},{10,8},{12,... | collective-permute-start | bytes 1572872 | tf_op jit(solution)/shard_map/ppermute | solution.py:89
  388.3 12.9 %collective-permute-start.15 = (bf16[128,2048]{1,0:T(8,128)(2,1)S(1)}, bf16[128,2048]{1,0:T(8,128)(2,1)}, u32[]{:S(2)}, u32[]{:S(2)}) collective-permute-start(bf16[128,2048]{1,0:T(8,128)(2,1)S(1)} %get-tuple-element.119), channel_id=1, source_target_pairs={{0,4},{2,6},{4,0},{6,2},{1,5},{3,7},{5,1},{7,3},{8,12},{10,14},{12... | collective-permute-start | bytes 1572872 | tf_op jit(solution)/shard_map/ppermute | solution.py:89
  388.4 27.7 %copy-start.33 = (bf16[256,2048]{1,0:T(8,128)(2,1)S(1)}, bf16[256,2048]{1,0:T(8,128)(2,1)}, u32[]{:S(2)}) copy-start(bf16[256,2048]{1,0:T(8,128)(2,1)} %param.41) | copy-start | bytes 3145732
  388.4 24.2 %collective-permute-start.16 = (bf16[128,2048]{1,0:T(8,128)(2,1)S(1)}, bf16[128,2048]{1,0:T(8,128)(2,1)}, u32[]{:S(2)}, u32[]{:S(2)}) collective-permute-start(bf16[128,2048]{1,0:T(8,128)(2,1)S(1)} %get-tuple-element.118), channel_id=1, source_target_pairs={{0,6},{2,4},{4,2},{6,0},{1,7},{3,5},{5,3},{7,1},{8,14},{10,12},{12... | collective-permute-start | bytes 1572872 | tf_op jit(solution)/shard_map/ppermute | solution.py:89
  417.4 12.0 collective-permute-start.17
  417.8 11.7 collective-permute-start.18
  418.9 22.1 %collective-permute-start.19 = (bf16[128,2048]{1,0:T(8,128)(2,1)S(1)}, bf16[128,2048]{1,0:T(8,128)(2,1)S(1)}, u32[]{:S(2)}, u32[]{:S(2)}) collective-permute-start(bf16[128,2048]{1,0:T(8,128)(2,1)S(1)} %get-tuple-element.92), channel_id=1, source_target_pairs={{0,6},{2,4},{4,2},{6,0},{1,7},{3,5},{5,3},{7,1},{8,14},{10,12},{12... | collective-permute-start | bytes 1572872 | tf_op jit(solution)/shard_map/ppermute | solution.py:58
  441.0 6.3 collective-permute-start.20
  466.6 41.3 %collective-permute-start.21 = (bf16[1024,512]{1,0:T(8,128)(2,1)}, bf16[1024,512]{1,0:T(8,128)(2,1)}, u32[]{:S(2)}, u32[]{:S(2)}) collective-permute-start(bf16[1024,512]{1,0:T(8,128)(2,1)} %pad_maximum_fusion.5), channel_id=1, source_target_pairs={{8,0},{16,8},{24,16},{9,1},{17,9},{25,17},{10,2},{18,10},{26,18},{... | collective-permute-start | bytes 3145736 | tf_op jit(solution)/shard_map/ppermute | solution.py:423
  472.9 36.5 %copy-start.5 = (f32[1024,256]{1,0:T(8,128)S(1)}, f32[1024,256]{1,0:T(8,128)}, u32[]{:S(2)}) copy-start(f32[1024,256]{1,0:T(8,128)} %copy-done.4) | copy-start | bytes 3145732
  473.0 163.8 %all-gather.4.cloned.1.call-start = ((), (), s32[]{:S(2)}) async-start(), calls=%async_computation.12 | async-start | bytes 1572864 | tf_op jit(solution)/shard_map/all_gather | solution.py:380
  513.8 27.3 %copy-start.34 = (bf16[1024,256]{1,0:T(8,128)(2,1)}, bf16[1024,256]{1,0:T(8,128)(2,1)S(1)}, u32[]{:S(2)}) copy-start(bf16[1024,256]{1,0:T(8,128)(2,1)S(1)} %copy.179) | copy-start | bytes 1572868
  523.6 5.9 collective-permute-start.22
  525.6 141.2 %all-reduce.3.cloned.1.call-start = ((), (), s32[]{:S(2)}) async-start(), calls=%async_computation.20 | async-start | bytes 229376
  536.7 13.4 %collective-permute-start.23 = (bf16[128,2048]{1,0:T(8,128)(2,1)}, bf16[128,2048]{1,0:T(8,128)(2,1)}, u32[]{:S(2)}, u32[]{:S(2)}) collective-permute-start(bf16[128,2048]{1,0:T(8,128)(2,1)} %get-tuple-element.114), channel_id=1, source_target_pairs={{0,2},{2,0},{4,6},{6,4},{1,3},{3,1},{5,7},{7,5},{8,10},{10,8},{12,... | collective-permute-start | bytes 1572872 | tf_op jit(solution)/shard_map/ppermute | solution.py:89
  537.8 13.1 %collective-permute-start.24 = (bf16[128,2048]{1,0:T(8,128)(2,1)}, bf16[128,2048]{1,0:T(8,128)(2,1)}, u32[]{:S(2)}, u32[]{:S(2)}) collective-permute-start(bf16[128,2048]{1,0:T(8,128)(2,1)} %get-tuple-element.116), channel_id=1, source_target_pairs={{0,4},{2,6},{4,0},{6,2},{1,5},{3,7},{5,1},{7,3},{8,12},{10,14},{12... | collective-permute-start | bytes 1572872 | tf_op jit(solution)/shard_map/ppermute | solution.py:89
  538.0 24.2 %collective-permute-start.25 = (bf16[128,2048]{1,0:T(8,128)(2,1)}, bf16[128,2048]{1,0:T(8,128)(2,1)}, u32[]{:S(2)}, u32[]{:S(2)}) collective-permute-start(bf16[128,2048]{1,0:T(8,128)(2,1)} %get-tuple-element.115), channel_id=1, source_target_pairs={{0,6},{2,4},{4,2},{6,0},{1,7},{3,5},{5,3},{7,1},{8,14},{10,12},{12... | collective-permute-start | bytes 1572872 | tf_op jit(solution)/shard_map/ppermute | solution.py:89
  565.2 165.3 %reduce-scatter.9.cloned.1.call-start = ((), (), s32[]{:S(2)}) async-start(), calls=%async_computation.15 | async-start | bytes 3932160 | tf_op jit(solution)/shard_map/reduce_scatter | solution.py:435
  573.3 308.3 %reduce-scatter.15.cloned.1.call-start = ((), (), s32[]{:S(2)}) async-start(), calls=%async_computation.18 | async-start | bytes 10813440 | tf_op jit(solution)/shard_map/reduce_scatter | solution.py:383
  590.3 305.3 %all-gather.8.cloned.1.call-start = ((), (), s32[]{:S(2)}) async-start(), calls=%async_computation.14 | async-start | bytes 3145728 | tf_op jit(solution)/shard_map/all_gather | solution.py:432
  599.2 448.1 %reduce-scatter.13.cloned.1.call-start = ((), (), s32[]{:S(2)}) async-start(), calls=%async_computation.17 | async-start | bytes 10813440 | tf_op jit(solution)/shard_map/reduce_scatter | solution.py:383
  612.9 586.0 %reduce-scatter.17.cloned.1.call-start = ((), (), s32[]{:S(2)}) async-start(), calls=%async_computation.19 | async-start | bytes 10813440 | tf_op jit(solution)/shard_map/reduce_scatter | solution.py:395
  632.7 7.6 all-to-all-start.1
  734.4 149.3 %all-to-all-start = ((bf16[4,128,3,256]{1,3,2,0:T(8,128)(2,1)}), bf16[4,128,3,256]{1,3,2,0:T(8,128)(2,1)S(1)}, u32[]{:S(2)}, u32[]{:S(2)}) async-start(bf16[4,128,3,256]{1,3,2,0:T(8,128)(2,1)} %copy.163), calls=%async_computation.2 | async-start | bytes 1572864 | tf_op jit(solution)/shard_map/all_to_all | solution.py:437
  883.6 165.7 %all-to-all-start.3 = ((bf16[4,128,704]{1,2,0:T(8,128)(2,1)}), bf16[4,128,704]{1,2,0:T(8,128)(2,1)S(1)}, u32[]{:S(2)}, u32[]{:S(2)}) async-start(bf16[4,128,704]{1,2,0:T(8,128)(2,1)} %copy_bitcast_fusion), calls=%async_computation.8 | async-start | bytes 1441792 | tf_op jit(solution)/shard_map/all_to_all | solution.py:388
  1049.4 154.1 %all-to-all-start.2 = ((bf16[4,128,704]{1,2,0:T(8,128)(2,1)}), bf16[4,128,704]{1,2,0:T(8,128)(2,1)}, u32[]{:S(2)}, u32[]{:S(2)}) async-start(bf16[4,128,704]{1,2,0:T(8,128)(2,1)} %copy_bitcast_fusion.1), calls=%async_computation.6 | async-start | bytes 1441792 | tf_op jit(solution)/shard_map/all_to_all | solution.py:388
  1203.4 14.1 %all-to-all-start.4 = ((bf16[1,704,4,128]{3,1,0,2:T(8,128)(2,1)}), bf16[1,704,4,128]{3,1,0,2:T(8,128)(2,1)}, u32[]{:S(2)}, u32[]{:S(2)}) async-start(bf16[1,704,4,128]{3,1,0,2:T(8,128)(2,1)} %copy.168), calls=%async_computation.10 | async-start | bytes 1441792 | tf_op jit(solution)/shard_map/all_to_all | solution.py:407
  (80 other events, 701.4 us)
Sparse Core Ops, SparseCore 0:
  188.3 49.4 all-gather.5
  305.9 51.3 reduce-scatter.6
  473.1 39.7 reduce-scatter.10
  525.7 7.6 all-gather.3
  565.3 101.4 all-reduce.2
  669.0 61.5 reduce-scatter.8
  732.9 148.6 reduce-scatter.14
  883.7 11.9 all-gather.7
  898.0 149.2 reduce-scatter.12
  1049.5 149.4 reduce-scatter.16

commit v2 on v1

--- a/solution.py
+++ b/solution.py
@@ -14,6 +14,10 @@
 THETA = 1000000.0
 NEG_LARGE = -1e30
 QUERY_BLOCK = 256
+FEED_BLOCK = 512
+LANE = 128
+FACT_ROWS = 16
+GATHERED_PLANES = 4
 F32 = jnp.float32
 BF16 = jnp.bfloat16
 
@@ -48,46 +52,77 @@
     return (index - step + count) % count
 
 
-def gather_plane(own):
+def joined(own, came, axis_name):
+    core = lax.axis_index(axis_name)
+    first = jnp.where(core == 0, own, came)
+    second = jnp.where(core == 0, came, own)
+    return jnp.concatenate([first, second], axis=0)
+
+
+def gather_plane(own, meanwhile=()):
     groups, cores = lax.axis_size("expert"), lax.axis_size("tensor")
     mine, core = lax.axis_index("expert"), lax.axis_index("tensor")
     rows, width = own.shape
-    pieces = jnp.zeros((groups, rows, width), own.dtype)
-    pieces = lax.dynamic_update_slice(pieces, own[None], (mine, 0, 0))
+    pieces = jnp.zeros((groups * rows, width), own.dtype)
+    pieces = lax.dynamic_update_slice(pieces, own, (mine * rows, 0))
     for step in range(1, groups):
         came = lax.ppermute(own, "expert", shift_pairs(groups, step))
-        pieces = lax.dynamic_update_slice(pieces, came[None], (source(mine, groups, step), 0, 0))
-    whole = jnp.zeros((groups, cores, rows, width), own.dtype)
-    whole = lax.dynamic_update_slice(whole, pieces[:, None], (0, core, 0, 0))
+        came = after(came, own, *meanwhile)
+        pieces = lax.dynamic_update_slice(pieces, came, (source(mine, groups, step) * rows, 0))
+    if cores == 2:
+        return joined(pieces, lax.ppermute(pieces, "tensor", shift_pairs(cores, 1)), "tensor")
+    return core_blocks(pieces)
+
+
+def core_blocks(own):
+    cores, core = lax.axis_size("tensor"), lax.axis_index("tensor")
+    rows, width = own.shape
+    whole = lax.dynamic_update_slice(jnp.zeros((cores * rows, width), own.dtype), own, (core * rows, 0))
     for step in range(1, cores):
-        came = lax.ppermute(pieces, "tensor", shift_pairs(cores, step))
-        whole = lax.dynamic_update_slice(whole, came[:, None], (0, source(core, cores, step), 0, 0))
-    return whole.reshape(groups * cores * rows, width)
-
-
-def scatter_plane(partial):
+        came = lax.ppermute(own, "tensor", shift_pairs(cores, step))
+        whole = lax.dynamic_update_slice(whole, came, (source(core, cores, step) * rows, 0))
+    return whole
+
+
+def scatter_plane(partial_of_core, meanwhile=None):
     groups, cores = lax.axis_size("expert"), lax.axis_size("tensor")
     mine, core = lax.axis_index("expert"), lax.axis_index("tensor")
-    total, width = partial.shape
-    rows = total // (groups * cores)
-    blocks = partial.reshape(groups, cores, rows, width)
-
-    def of_core(index):
-        return lax.dynamic_slice(blocks, (0, index, 0, 0), (groups, 1, rows, width))[:, 0]
-
-    held = of_core(core).astype(F32)
-    for step in range(1, cores):
-        sent = of_core(partner(core, cores, step)).astype(BF16)
-        held = held + lax.ppermute(sent, "tensor", shift_pairs(cores, step)).astype(F32)
+    sent = [partial_of_core(partner(core, cores, step)).astype(BF16) for step in range(1, cores)]
+    came = [lax.ppermute(sent[step - 1], "tensor", shift_pairs(cores, step)) for step in range(1, cores)]
+    held = functools.reduce(jnp.add, [part.astype(F32) for part in came], partial_of_core(core).astype(F32))
+    rows, width = held.shape[0] // groups, held.shape[1]
 
     def of_group(index):
-        return lax.dynamic_slice(held, (index, 0, 0), (1, rows, width))[0]
-
+        return lax.dynamic_slice(held, (index * rows, 0), (rows, width))
+
+    sent = [of_group(partner(mine, groups, step)).astype(BF16) for step in range(1, groups)]
+    came = [lax.ppermute(sent[step - 1], "expert", shift_pairs(groups, step)) for step in range(1, groups)]
     result = of_group(mine)
-    for step in range(1, groups):
-        sent = of_group(partner(mine, groups, step)).astype(BF16)
-        result = result + lax.ppermute(sent, "expert", shift_pairs(groups, step)).astype(F32)
-    return result
+    if meanwhile is None:
+        return functools.reduce(jnp.add, [part.astype(F32) for part in came], result)
+    side = meanwhile(tuple(sent))
+    came = lax.optimization_barrier((tuple(came), side))[0]
+    return functools.reduce(jnp.add, [part.astype(F32) for part in came], result), side
+
+
+def after(value, *others):
+    return lax.optimization_barrier((value, *others))[0]
+
+
+def both_cores(own):
+    if lax.axis_size("tensor") == 2:
+        return joined(own, lax.ppermute(own, "tensor", shift_pairs(2, 1)), "tensor")
+    return core_blocks(own)
+
+
+def token_order(values, groups, cores):
+    total, width = values.shape
+    return values.reshape(cores, groups, -1, width).transpose(1, 0, 2, 3).reshape(total, width)
+
+
+def core_order(values, groups, cores):
+    total, width = values.shape
+    return values.reshape(groups, cores, -1, width).transpose(1, 0, 2, 3).reshape(total, width)
 
 
 def rotate(values, cosine, sine_table):
@@ -248,6 +283,294 @@
     )(query, before, before, own, own, seg_rows, seg_before, seg_own, grad_heads)
 
 
+def hidden_grads(rows, top, gate, weight_gu, weight_down):
+    hidden = weight_down.shape[0]
+    both = dot_nt(rows, weight_gu)
+    inner_grad = dot_nt(top, weight_down)
+    gate_val, up_val = both[:, :hidden], both[:, hidden:]
+    sigmoid_val = jax.nn.sigmoid(gate_val)
+    silu_val = gate_val * sigmoid_val
+    inner = silu_val * up_val
+    slope = jnp.sum(inner * inner_grad, axis=-1, keepdims=True)
+    inner_grad = inner_grad * gate
+    gated = (inner * gate).astype(BF16)
+    grad_gate_val = (inner_grad * up_val * (sigmoid_val + silu_val * (1.0 - sigmoid_val))).astype(BF16)
+    grad_up_val = (inner_grad * silu_val).astype(BF16)
+    return gated, grad_gate_val, grad_up_val, slope
+
+
+def gate_of(gates, block):
+    lane = lax.broadcasted_iota(jnp.int32, gates.shape, 1)
+    return jnp.sum(jnp.where(lane == block, gates, 0.0), axis=1, keepdims=True)
+
+
+def feed_kernel(chunk_ref, rows_ref, top_ref, gates_ref, gu_ref, down_ref, gated_ref, grad_ref, slope_ref):
+    del chunk_ref
+    hidden = down_ref.shape[0]
+    gate = gate_of(gates_ref[...], pl.program_id(0))
+    gated, grad_gate_val, grad_up_val, slope = hidden_grads(
+        rows_ref[...], top_ref[...], gate, gu_ref[...], down_ref[...]
+    )
+    gated_ref[...] = gated
+    grad_ref[:, :hidden] = grad_gate_val
+    grad_ref[:, hidden:] = grad_up_val
+    slope_ref[0] = slope
+
+
+def weight_kernel(
+    routed,
+    hidden_out,
+    chunk_ref,
+    rows_ref,
+    top_ref,
+    rows_t_ref,
+    top_t_ref,
+    gates_ref,
+    gu_ref,
+    down_ref,
+    gu_in,
+    down_in,
+    *rest,
+):
+    del chunk_ref
+    gate_out, up_out, down_out, gate_sum, up_sum, down_sum = rest[-6:]
+    hidden = down_ref.shape[0]
+    step = pl.program_id(0)
+
+    @pl.when(step == 0)
+    def _():
+        gate_sum[...] = gu_in[:, :hidden]
+        up_sum[...] = gu_in[:, hidden:]
+        down_sum[...] = down_in[...]
+
+    gate = gate_of(gates_ref[...], routed)
+    gated, grad_gate_val, grad_up_val, _ = hidden_grads(
+        rows_ref[...], top_ref[...], gate, gu_ref[...], down_ref[...]
+    )
+    gate_sum[...] += dot(rows_t_ref[...], grad_gate_val)
+    up_sum[...] += dot(rows_t_ref[...], grad_up_val)
+    down_sum[...] += dot(top_t_ref[...], gated)
+
+    @pl.when(step == pl.num_programs(0) - 1)
+    def _():
+        if len(gate_out.shape) == 3 and gate_out.shape[0] == 1:
+            gate_out[0] = gate_sum[...].T[:hidden_out]
+            up_out[0] = up_sum[...].T[:hidden_out]
+            down_out[0] = down_sum[...].T[:hidden_out]
+        else:
+            groups, part = gate_out.shape[:2]
+            turned = down_sum[...].T.astype(BF16)
+            for g in range(groups):
+                gate_out[g] = gate_sum[g * part : (g + 1) * part, :].astype(BF16)
+                up_out[g] = up_sum[g * part : (g + 1) * part, :].astype(BF16)
+                down_out[g] = turned[:, g * part : (g + 1) * part]
+
+
+def pack_kernel(local, hidden, units, window_ref, *refs):
+    gate_ref, up_ref, down_ref = refs[:3]
+    shared_gate, shared_up = refs[3 : 3 + units], refs[3 + units : 3 + 2 * units]
+    shared_down = refs[3 + 2 * units : 3 + 3 * units]
+    gu_out, down_out = refs[-2:]
+    padded = units * LANE
+    columns = down_out.shape[1]
+    for e in range(local):
+        for ref, out, at in ((gate_ref, gu_out, 2 * e), (up_ref, gu_out, 2 * e + 1), (down_ref, down_out, e)):
+            out[at * padded : at * padded + hidden, :] = ref[e]
+            if hidden < padded:
+                out[at * padded + hidden : (at + 1) * padded, :] = jnp.zeros((padded - hidden, columns), BF16)
+    skip = window_ref[1]
+    for k in range(units):
+        line = lax.broadcasted_iota(jnp.int32, (LANE, columns), 0) + k * LANE
+        keep = (line >= skip) & (line < skip + hidden)
+        for block, out, at in (
+            (shared_gate[k][...].T, gu_out, 2 * local),
+            (shared_up[k][...].T, gu_out, 2 * local + 1),
+            (shared_down[k][...], down_out, local),
+        ):
+            out[at * padded + k * LANE : at * padded + (k + 1) * LANE, :] = jnp.where(
+                keep, block.astype(F32), 0.0
+            ).astype(BF16)
+
+
+def pack_weights(window, expert_gate, expert_up, expert_down, shared_gate, shared_up, shared_down, padded):
+    local, hidden, model_width = expert_down.shape
+    units = padded // LANE
+    blocks = local + 1
+    tile = min(256, model_width)
+    expert_spec = pl.BlockSpec((local, hidden, tile), lambda i, w: (0, 0, i))
+    column_specs = [pl.BlockSpec((tile, LANE), lambda i, w, k=k: (i, w[0] + k)) for k in range(units)]
+    row_specs = [pl.BlockSpec((LANE, tile), lambda i, w, k=k: (w[0] + k, i)) for k in range(units)]
+    return pl.pallas_call(
+        functools.partial(pack_kernel, local, hidden, units),
+        grid_spec=pltpu.PrefetchScalarGridSpec(
+            num_scalar_prefetch=1,
+            grid=(model_width // tile,),
+            in_specs=[expert_spec] * 3 + column_specs * 2 + row_specs,
+            out_specs=[
+                pl.BlockSpec((2 * blocks * padded, tile), lambda i, w: (0, i)),
+                pl.BlockSpec((blocks * padded, tile), lambda i, w: (0, i)),
+            ],
+        ),
+        out_shape=[
+            jax.ShapeDtypeStruct((2 * blocks * padded, model_width), BF16),
+            jax.ShapeDtypeStruct((blocks * padded, model_width), BF16),
+        ],
+        compiler_params=pltpu.CompilerParams(vmem_limit_bytes=40 * 2**20),
+        cost_estimate=pl.CostEstimate(
+            flops=0, bytes_accessed=12 * blocks * padded * model_width, transcendentals=0
+        ),
+        name="pack_weights",
+    )(
+        window,
+        jnp.swapaxes(expert_gate, 1, 2),
+        jnp.swapaxes(expert_up, 1, 2),
+        expert_down,
+        *([shared_gate] * units),
+        *([shared_up] * units),
+        *([shared_down] * units),
+    )
+
+
+def turn_kernel(plane_ref, part_ref, out_ref):
+    del plane_ref
+    out_ref[...] = part_ref[...].T
+
+
+def turn_logits_kernel(plane_ref, part_ref, rows_ref, columns_ref, out_ref, logits_ref):
+    del plane_ref
+    out_ref[...] = part_ref[...].T
+    logits_ref[...] = dot(rows_ref[...], columns_ref[...])
+
+
+def turn(plane, values, part, columns=None):
+    total, model_width = values.shape
+    tile = min(512, total)
+    specs = [pl.BlockSpec((tile, part), lambda i, p: (i, p[0]))]
+    turned = pl.BlockSpec((part, tile), lambda i, p: (0, i))
+    shape = jax.ShapeDtypeStruct((part, total), BF16)
+    args, out_specs, shapes, kernel = [values], turned, shape, turn_kernel
+    if columns is not None:
+        specs += [
+            pl.BlockSpec((tile, model_width), lambda i, p: (i, 0)),
+            pl.BlockSpec(columns.shape, lambda i, p: (0, 0)),
+        ]
+        args += [values, columns]
+        out_specs = [turned, pl.BlockSpec((tile, columns.shape[1]), lambda i, p: (i, 0))]
+        shapes = [shape, jax.ShapeDtypeStruct((total, columns.shape[1]), F32)]
+        kernel = turn_logits_kernel
+    return pl.pallas_call(
+        kernel,
+        grid_spec=pltpu.PrefetchScalarGridSpec(
+            num_scalar_prefetch=1, grid=(total // tile,), in_specs=specs, out_specs=out_specs
+        ),
+        out_shape=shapes,
+        compiler_params=pltpu.CompilerParams(vmem_limit_bytes=40 * 2**20),
+        cost_estimate=pl.CostEstimate(flops=0, bytes_accessed=2 * total * model_width, transcendentals=0),
+        name="turn",
+    )(plane, *args)
+
+
+def feed(chunk, rows, top_all, gates, weight_gu, weight_down, blocks):
+    count, model_width = rows.shape
+    hidden = weight_down.shape[0] // blocks
+    tile = min(FEED_BLOCK, count)
+    steps = count // tile
+    grid_spec = pltpu.PrefetchScalarGridSpec(
+        num_scalar_prefetch=1,
+        grid=(blocks, steps),
+        in_specs=[
+            pl.BlockSpec((tile, model_width), lambda s, i, c: (i, 0)),
+            pl.BlockSpec((tile, model_width), lambda s, i, c: (c[0] * steps + i, 0)),
+            pl.BlockSpec((tile, gates.shape[1]), lambda s, i, c: (i, 0)),
+            pl.BlockSpec((2 * hidden, model_width), lambda s, i, c: (s, 0)),
+            pl.BlockSpec((hidden, model_width), lambda s, i, c: (s, 0)),
+        ],
+        out_specs=[
+            pl.BlockSpec((tile, hidden), lambda s, i, c: (i, s)),
+            pl.BlockSpec((tile, 2 * hidden), lambda s, i, c: (i, s)),
+            pl.BlockSpec((1, tile, 1), lambda s, i, c: (s, i, 0)),
+        ],
+    )
+    return pl.pallas_call(
+        feed_kernel,
+        grid_spec=grid_spec,
+        out_shape=[
+            jax.ShapeDtypeStruct((count, blocks * hidden), BF16),
+            jax.ShapeDtypeStruct((count, 2 * blocks * hidden), BF16),
+            jax.ShapeDtypeStruct((blocks, count, 1), F32),
+        ],
+        compiler_params=pltpu.CompilerParams(vmem_limit_bytes=56 * 2**20),
+        cost_estimate=pl.CostEstimate(
+            flops=6 * count * model_width * hidden * blocks,
+            bytes_accessed=6 * model_width * hidden * blocks + 4 * count * model_width * blocks,
+            transcendentals=count * hidden * blocks,
+        ),
+        name="feed",
+    )(chunk, rows, top_all, gates, weight_gu, weight_down)
+
+
+def weight_grads(plane, planes, block, rows_all, top_all, rows_t, top_t, gates, packed, sums, outs, groups, hidden):
+    weight_gu, weight_down = packed
+    total, model_width = rows_all.shape
+    count = total // planes
+    part = rows_t.shape[0]
+    padded = sums[1].shape[1]
+    tile = min(FEED_BLOCK, count)
+    steps = count // tile
+    local = outs[0] if isinstance(outs[0], int) else outs[0].shape[0]
+
+    def at(i, c):
+        return lax.rem(c[0] + 1 + i // steps, planes) * steps + lax.rem(i, steps)
+
+    tokens = pl.BlockSpec((tile, model_width), lambda i, c: (at(i, c), 0))
+    turned = pl.BlockSpec((part, tile), lambda i, c: (0, at(i, c)))
+    in_specs = [
+        tokens,
+        tokens,
+        turned,
+        turned,
+        pl.BlockSpec((tile, gates.shape[1]), lambda i, c: (at(i, c), 0)),
+        pl.BlockSpec((2 * padded, model_width), lambda i, c: (block, 0)),
+        pl.BlockSpec((padded, model_width), lambda i, c: (block, 0)),
+        pl.BlockSpec((part, 2 * padded), lambda i, c: (0, 0)),
+        pl.BlockSpec((part, padded), lambda i, c: (0, 0)),
+    ]
+    args = [rows_all, top_all, rows_t, top_t, gates, weight_gu, weight_down, *sums]
+    aliases = {}
+    if block < local:
+        out_shape = [jax.ShapeDtypeStruct((local, hidden, part), F32)] * 3
+        out_specs = [pl.BlockSpec((1, hidden, part), lambda i, c: (block, 0, 0))] * 3
+        if not isinstance(outs[0], int):
+            in_specs += [pl.BlockSpec(memory_space=pl.ANY)] * 3
+            aliases = {len(args) + 1 + k: k for k in range(3)}
+            args += list(outs)
+    else:
+        wide = jax.ShapeDtypeStruct((groups, part // groups, padded), BF16)
+        out_shape = [wide, wide, jax.ShapeDtypeStruct((groups, padded, part // groups), BF16)]
+        out_specs = [
+            pl.BlockSpec(shape.shape, lambda i, c: (0, 0, 0)) for shape in out_shape
+        ]
+    return pl.pallas_call(
+        functools.partial(weight_kernel, block, hidden),
+        grid_spec=pltpu.PrefetchScalarGridSpec(
+            num_scalar_prefetch=1,
+            grid=((planes - 1) * steps,),
+            in_specs=in_specs,
+            out_specs=out_specs,
+            scratch_shapes=[pltpu.VMEM((part, padded), F32)] * 3,
+        ),
+        out_shape=out_shape,
+        input_output_aliases=aliases,
+        compiler_params=pltpu.CompilerParams(vmem_limit_bytes=62 * 2**20),
+        cost_estimate=pl.CostEstimate(
+            flops=6 * (total - count) * (model_width + part) * padded,
+            bytes_accessed=6 * model_width * padded + 4 * total * model_width,
+            transcendentals=total * padded,
+        ),
+        name="weight_grads",
+    )(plane, *args)
+
+
 def per_device(
     tokens,
     segments,
@@ -282,24 +605,53 @@
     heads = width // HD
     local_experts, _, hidden = expert_gate.shape
     expert_count = local_experts * groups
-    shared_hidden = shared_gate.shape[1] // groups
-
-    picks = jnp.sum(1 << routes, axis=1).astype(jnp.int32)
-    facts = lax.all_gather(jnp.stack([segments, picks]), ("dp", "expert"), axis=1, tiled=True)
-    facts_own = lax.dynamic_slice(facts, (0, plane * plane_rows), (2, plane_rows))
-    seg_own = facts_own[:1]
-    seg_before = lax.dynamic_slice(facts, (0, jnp.maximum(plane - 1, 0) * plane_rows), (1, plane_rows))
-    seg_before = jnp.where(plane > 0, seg_before, -1)
-    seg_rows = seg_own.reshape(plane_rows, 1)
-    chosen = (facts_own[1][:, None] >> jnp.arange(expert_count, dtype=jnp.int32)[None, :]) & 1
-
-    grad_top_plane = lax.all_gather(grad_out, "expert", axis=0, tiled=True)
+    blocks = local_experts + 1
+    gathered = planes <= GATHERED_PLANES
+    padded = -(-hidden // LANE) * LANE
+    part_rows = model_width // planes
+
+    def in_tokens(values):
+        return token_order(values, groups, cores)
+
+    def in_cores(values):
+        return core_order(values, groups, cores)
+
+    first_unit = mine * hidden // LANE
+    window = jnp.stack([first_unit, mine * hidden - first_unit * LANE]).astype(jnp.int32)
+    packed = pack_weights(window, expert_gate, expert_up, expert_down, shared_gate, shared_up, shared_down, padded)
 
     own_tokens = lax.dynamic_slice(tokens, (core * rows, 0), (rows, model_width))
     inputs = own_tokens.astype(F32)
     gain_one = attn_gain.astype(F32)
     scale_one = lax.rsqrt(jnp.mean(inputs * inputs, axis=-1, keepdims=True) + EPS)
-    normed_one = gather_plane((inputs * scale_one * gain_one).astype(BF16))
+    weight_gu, weight_down = packed
+    normed_one = gather_plane((inputs * scale_one * gain_one).astype(BF16), (weight_gu, weight_down))
+    grad_top_own = lax.dynamic_slice(grad_out, (core * rows, 0), (rows, model_width))
+    picks = jnp.sum(1 << routes, axis=1)
+    facts_own = jnp.zeros((FACT_ROWS, tok_rows), BF16)
+    facts_own = facts_own.at[0].set(segments.astype(BF16)).at[1].set(picks.astype(BF16))
+    facts = jnp.zeros((groups, FACT_ROWS, tok_rows), BF16)
+    facts = lax.dynamic_update_slice(facts, facts_own[None], (mine, 0, 0))
+    for step in range(1, groups):
+        came = lax.ppermute(facts_own, "expert", shift_pairs(groups, step))
+        facts = lax.dynamic_update_slice(facts, came[None], (source(mine, groups, step), 0, 0))
+    facts = facts.transpose(1, 0, 2).reshape(FACT_ROWS, plane_rows)
+    facts_all = jnp.zeros((planes, FACT_ROWS, plane_rows), BF16)
+    facts_all = lax.dynamic_update_slice(facts_all, facts[None], (plane, 0, 0))
+    seg_before = facts[:1]
+    for step in range(1, planes):
+        came = lax.ppermute(facts, "dp", [(i, (i + step) % planes) for i in range(planes)])
+        if step == 1:
+            seg_before = came[:1]
+        facts_all = lax.dynamic_update_slice(facts_all, came[None], ((plane - step + planes) % planes, 0, 0))
+    top_axes = ("dp", "tensor", "expert") if gathered else ("tensor", "expert")
+    grad_top_all = lax.all_gather(grad_top_own, top_axes, axis=0, tiled=True)
+    seg_own = facts[:1].astype(F32)
+    seg_before = jnp.where(plane > 0, seg_before.astype(F32), -1.0)
+    seg_rows = seg_own.reshape(plane_rows, 1)
+    bits_all = (
+        facts_all[:, 1].reshape(planes, groups, cores, rows).transpose(0, 2, 1, 3).reshape(-1, 1).astype(jnp.int32)
+    )
 
     def columns(weight):
         return lax.dynamic_slice(weight, (0, mine * width), (model_width, width))
@@ -315,134 +667,197 @@
     angles = places[:, None] * frequency[None, :]
     cosine = jnp.cos(angles)
     sine_table = jnp.sin(angles)
-    kv_pre = dot(normed_one, weight_kv) + jnp.concatenate([bias_of(key_bias), bias_of(value_bias)], axis=1)
+    kv_pre = in_tokens(
+        dot(normed_one, weight_kv) + jnp.concatenate([bias_of(key_bias), bias_of(value_bias)], axis=1)
+    )
     own_kv = jnp.concatenate(
         [rotate(kv_pre[:, :width], cosine, sine_table).astype(BF16), kv_pre[:, width:].astype(BF16)], axis=1
     )
-    before_kv = lax.ppermute(own_kv, "dp", [(i, i + 1) for i in range(planes - 1)])
-    query_pre = dot(normed_one, weight_q) + bias_of(query_bias)
+    before_kv = after(lax.ppermute(own_kv, "dp", [(i, i + 1) for i in range(planes - 1)]), facts_all)
+    query_pre = in_tokens(dot(normed_one, weight_q) + bias_of(query_bias))
     query_rot = rotate(query_pre, cosine, sine_table).astype(BF16)
-    attended = attend(query_rot, before_kv, own_kv, seg_rows, seg_before, seg_own)
+    attended = in_cores(attend(query_rot, before_kv, own_kv, seg_rows, seg_before, seg_own))
     out_rows = lax.dynamic_slice(out_weight, (mine * width, 0), (width, model_width))
-    after_attn = inputs + scatter_plane(dot(attended, out_rows))
+    half = plane_rows // cores
+
+    def of_core(values, index):
+        return lax.dynamic_slice(values, (index * half, 0), (half, values.shape[1]))
+
+    after_attn = inputs + scatter_plane(lambda index: dot(of_core(attended, index), out_rows))
 
     gain_two = mlp_gain.astype(F32)
     scale_two = lax.rsqrt(jnp.mean(after_attn * after_attn, axis=-1, keepdims=True) + EPS)
-    normed_two = gather_plane((after_attn * scale_two * gain_two).astype(BF16))
+    normed_own = (after_attn * scale_two * gain_two).astype(BF16)
+    normed_two = gather_plane(normed_own)
+    if gathered:
+        normed_all = lax.all_gather(after(normed_own, normed_two), ("dp", "tensor", "expert"), axis=0, tiled=True)
     gate_columns = jnp.concatenate([router_weight, shared_router[:, None]], axis=1)
-    small_logits = dot(normed_two, gate_columns)
-    router_probs = jax.nn.softmax(small_logits[:, :expert_count], axis=-1)
-    shared_mix = jax.nn.sigmoid(small_logits[:, expert_count:])
-    combine = router_probs * chosen.astype(F32)
-    own_gates = lax.dynamic_slice(combine, (0, mine * local_experts), (plane_rows, local_experts))
-
-    def shared_columns(weight):
-        return lax.dynamic_slice(weight, (0, mine * shared_hidden), (model_width, shared_hidden))
-
-    shared_rows = lax.dynamic_slice(shared_down, (mine * shared_hidden, 0), (shared_hidden, model_width))
-    segments_of_hidden = [
-        (expert_gate[e], expert_up[e], expert_down[e], own_gates[:, e : e + 1]) for e in range(local_experts)
-    ] + [(shared_columns(shared_gate), shared_columns(shared_up), shared_rows, shared_mix)]
-    mixed_part, grad_normed_part = None, None
-    gate_slopes, gate_grads, up_grads, down_grads = [], [], [], []
-    for w_gate, w_up, w_down, gate in segments_of_hidden:
-        gate_val = dot(normed_two, w_gate)
-        up_val = dot(normed_two, w_up)
-        inner_grad = dot_nt(grad_top_plane, w_down)
-        sigmoid_val = jax.nn.sigmoid(gate_val)
-        silu_val = gate_val * sigmoid_val
-        inner = silu_val * up_val
-        gate_slopes.append(jnp.sum(inner * inner_grad, axis=-1, keepdims=True))
-        gated = (gate * inner).astype(BF16)
-        inner_grad = gate * inner_grad
-        grad_gate_val = (inner_grad * up_val * (sigmoid_val * (1.0 + gate_val * (1.0 - sigmoid_val)))).astype(BF16)
-        grad_up_val = (inner_grad * silu_val).astype(BF16)
-        term = dot(gated, w_down)
-        mixed_part = term if mixed_part is None else mixed_part + term
-        term = dot_nt(grad_gate_val, w_gate) + dot_nt(grad_up_val, w_up)
-        grad_normed_part = term if grad_normed_part is None else grad_normed_part + term
-        down_grads.append(dot_tn(gated, grad_top_plane).astype(BF16))
-        gate_grads.append(dot_tn(normed_two, grad_gate_val).astype(BF16))
-        up_grads.append(dot_tn(normed_two, grad_up_val).astype(BF16))
-
-    slopes = jnp.concatenate(gate_slopes[:local_experts], axis=1)
-    slopes = lax.dynamic_update_slice(
-        jnp.zeros((plane_rows, expert_count), F32), slopes, (0, mine * local_experts)
-    ) * chosen.astype(F32)
-    grad_logits = router_probs * (slopes - jnp.sum(router_probs * slopes, axis=-1, keepdims=True))
-    grad_shared_logit = gate_slopes[local_experts] * shared_mix * (1.0 - shared_mix)
+
+    def gates_from(logits, bits):
+        router_probs = jax.nn.softmax(logits[:, :expert_count], axis=-1)
+        shared_mix = jax.nn.sigmoid(logits[:, expert_count : expert_count + 1])
+        chosen = ((bits >> jnp.arange(expert_count, dtype=jnp.int32)[None, :]) & 1).astype(F32)
+        own = lax.dynamic_slice(router_probs * chosen, (0, mine * local_experts), (bits.shape[0], local_experts))
+        return jnp.concatenate([own, shared_mix], axis=1), router_probs, chosen
+
+    bits = lax.dynamic_slice(bits_all, (plane * plane_rows, 0), (plane_rows, 1))
+    gates, router_probs, chosen = gates_from(dot(normed_two, gate_columns), bits)
+    shared_mix = gates[:, local_experts:]
+    plane_number = plane.reshape(1).astype(jnp.int32)
+    top_chunk = plane_number if gathered else jnp.zeros_like(plane_number)
+    gated, grad_hidden, slopes = feed(top_chunk, normed_two, grad_top_all, gates, weight_gu, weight_down, blocks)
+
+    own_slopes = jnp.concatenate([slopes[e] for e in range(local_experts)], axis=1)
+    all_slopes = lax.dynamic_update_slice(
+        jnp.zeros((plane_rows, expert_count), F32), own_slopes, (0, mine * local_experts)
+    ) * chosen
+    grad_logits = router_probs * (all_slopes - jnp.sum(router_probs * all_slopes, axis=-1, keepdims=True))
+    grad_shared_logit = slopes[local_experts] * shared_mix * (1.0 - shared_mix)
     grad_small = jnp.concatenate([grad_logits, grad_shared_logit], axis=1).astype(BF16)
-    grad_normed_part = grad_normed_part + dot_nt(grad_small, gate_columns)
+    grad_normed_part = (dot(grad_hidden, weight_gu) + dot_nt(grad_small, gate_columns)).astype(BF16)
+    own_part = lax.dynamic_slice(normed_two, (0, plane * part_rows), (plane_rows, part_rows))
+
+    def mix_meanwhile(token):
+        values, grads = after((gated, grad_hidden), token)
+        mixed_part = dot(values, weight_down).astype(BF16)
+        return mixed_part, dot_tn(own_part, grads[:, 2 * local_experts * padded :]) if gathered else ()
+
+    grad_normed_two, (mixed_part, shared_sum) = scatter_plane(
+        lambda index: of_core(grad_normed_part, index), mix_meanwhile
+    )
+    mixed = lax.psum_scatter(
+        after(mixed_part, grad_normed_two), ("tensor", "expert"), scatter_dimension=0, tiled=True
+    )
+    out = both_cores((after_attn + mixed.astype(F32)).astype(BF16))
     grad_columns = dot_tn(normed_two, grad_small)
-    mixed_part = mixed_part.astype(BF16)
-    mixed = lax.psum_scatter(mixed_part, ("expert", "tensor"), scatter_dimension=0, tiled=True)
-    out_own = (after_attn + mixed.astype(F32)).astype(BF16)
-    out = lax.all_gather(out_own, "tensor", axis=0, tiled=True)
-
-    def summed_rows(pieces):
-        return lax.psum_scatter(jnp.concatenate(pieces, axis=1), "dp", scatter_dimension=0, tiled=True)
-
-    def shared_of_rows(values):
-        part_rows = values.shape[0] // groups
-        return (
-            lax.all_to_all(values.reshape(groups, part_rows, shared_hidden), "expert", 0, 0)
-            .transpose(1, 0, 2)
-            .reshape(part_rows, groups * shared_hidden)
-        )
-
-    gate_sum = summed_rows(gate_grads)
-    up_sum = summed_rows(up_grads)
-    down_sum = lax.psum_scatter(jnp.concatenate(down_grads, axis=0), "dp", scatter_dimension=1, tiled=True)
-    routed = local_experts * hidden
-    part_rows = model_width // planes
-
-    def expert_columns(values):
-        return values[:, :routed].reshape(part_rows, local_experts, hidden).transpose(1, 0, 2).astype(F32)
-
-    grad_expert_gate = expert_columns(gate_sum)
-    grad_expert_up = expert_columns(up_sum)
-    grad_expert_down = down_sum[:routed].reshape(local_experts, hidden, part_rows).astype(F32)
-    grad_shared_gate = shared_of_rows(gate_sum[:, routed:]).astype(F32)
-    grad_shared_up = shared_of_rows(up_sum[:, routed:]).astype(F32)
-    grad_shared_down = lax.all_to_all(
-        down_sum[routed:].reshape(shared_hidden, groups, part_rows // groups), "expert", 1, 0
-    ).reshape(groups * shared_hidden, part_rows // groups).astype(F32)
-
-    grad_top = lax.dynamic_slice(grad_out, (core * rows, 0), (rows, model_width)).astype(F32)
-    grad_normed_two = scatter_plane(grad_normed_part)
+
     grad_mlp_gain = jnp.sum(grad_normed_two * after_attn * scale_two, axis=0)
-    grad_after = grad_top + norm_back(after_attn, scale_two, gain_two, grad_normed_two)
-
-    grad_attended = gather_plane(grad_after.astype(BF16))
-    grad_heads = dot_nt(grad_attended, out_rows).astype(BF16)
-    grad_out_part = dot_tn(attended, grad_attended).astype(BF16)
+    grad_after = grad_top_own.astype(F32) + norm_back(after_attn, scale_two, gain_two, grad_normed_two)
+
+    grad_sent = grad_after.astype(BF16)
+    values, grads, top_all = after((gated, grad_hidden, grad_top_all), grad_sent)
+    own_sums = []
+    if gathered:
+        top_t = turn(plane_number, top_all, part_rows)
+        own_top_t = lax.dynamic_slice(top_t, (0, plane * plane_rows), (part_rows, plane_rows))
+    for block in range(blocks if gathered else 0):
+        if block < local_experts:
+            gu_sum = dot_tn(own_part, grads[:, 2 * block * padded : 2 * (block + 1) * padded])
+        else:
+            gu_sum = shared_sum
+        own_sums.append((gu_sum, dot(own_top_t, values[:, block * padded : (block + 1) * padded])))
+    grad_attended = gather_plane(grad_sent, tuple(own_sums))
+    grad_heads = in_tokens(dot_nt(grad_attended, out_rows).astype(BF16))
     grad_query_rot, back_keys, back_values, own_keys, own_values = attend_back(
         query_rot, before_kv, own_kv, seg_rows, seg_before, seg_own, grad_heads
     )
     back_kv = jnp.concatenate([back_keys, back_values], axis=1).astype(BF16)
-    came_kv = lax.ppermute(back_kv, "dp", [(i + 1, i) for i in range(planes - 1)]).astype(F32)
+    small_rows = part_rows // groups
+
+    def to_owners(values):
+        return lax.all_to_all(values, "expert", 0, 0)
+
+    def placed(pieces, axis):
+        total = None
+        for j in range(groups):
+            at = j * hidden // LANE * LANE
+            pads = [(0, 0), (0, 0)]
+            pads[axis] = (at, groups * hidden - at - padded)
+            piece = jnp.pad(pieces[j].astype(F32), pads)
+            total = piece if total is None else total + piece
+        return total
+
+    if gathered:
+        wide_columns = jnp.concatenate(
+            [gate_columns, jnp.zeros((model_width, LANE - expert_count - 1), BF16)], axis=1
+        )
+        normed_all = after(normed_all, back_kv)
+        rows_t, logits_all = turn(plane_number, normed_all, part_rows, wide_columns)
+        gates_all, _, _ = gates_from(logits_all, bits_all)
+
+        def weight_sums(block, outs, *tokens):
+            return weight_grads(
+                plane_number,
+                planes,
+                block,
+                after(normed_all, *tokens),
+                grad_top_all,
+                rows_t,
+                top_t,
+                gates_all,
+                (weight_gu, weight_down),
+                own_sums[block],
+                outs,
+                groups,
+                hidden,
+            )
+
+        shared_grads = weight_sums(local_experts, (local_experts,), back_kv)
+    else:
+        gu_part = lax.psum_scatter(
+            dot_tn(normed_two, grad_hidden).astype(BF16), "dp", scatter_dimension=0, tiled=True
+        )
+        down_part = lax.psum_scatter(
+            dot_tn(grad_top_all, gated).astype(BF16), "dp", scatter_dimension=0, tiled=True
+        )
+
+        def block_of(values, index, size):
+            return values[:, index * padded : index * padded + size]
+
+        shared_grads = [
+            block_of(gu_part, 2 * local_experts, padded).reshape(groups, small_rows, padded),
+            block_of(gu_part, 2 * local_experts + 1, padded).reshape(groups, small_rows, padded),
+            block_of(down_part, local_experts, padded).reshape(groups, small_rows, padded).transpose(0, 2, 1),
+        ]
+    wide_grads = to_owners(jnp.stack(shared_grads[:2], axis=1))
+    shared_down_grads = to_owners(shared_grads[2])
+    came_kv = after(
+        lax.ppermute(back_kv, "dp", [(i + 1, i) for i in range(planes - 1)]), shared_grads
+    ).astype(F32)
     grad_query = rotate(grad_query_rot, cosine, -sine_table).astype(BF16)
     grad_key = rotate(own_keys + came_kv[:, :width], cosine, -sine_table).astype(BF16)
     grad_value = (own_values + came_kv[:, width:]).astype(BF16)
-    grad_qkv = jnp.concatenate([grad_query, grad_key, grad_value], axis=1)
+    grad_qkv = in_cores(jnp.concatenate([grad_query, grad_key, grad_value], axis=1))
     weight_qkv = jnp.concatenate([weight_q, weight_kv], axis=1)
-    grad_normed_one = scatter_plane(dot_nt(grad_qkv, weight_qkv))
+    grad_one_part = dot_nt(grad_qkv, weight_qkv).astype(BF16)
+    grad_part = jnp.concatenate([dot_tn(normed_one, grad_qkv), dot_tn(grad_attended, attended)], axis=1).astype(BF16)
+    weight_sum = lax.psum_scatter(grad_part, "dp", scatter_dimension=0, tiled=True)
+    weight_sum = weight_sum.reshape(groups, small_rows, 4, width)
+    if gathered:
+        expert_grads = (local_experts,)
+        for e in range(local_experts - 2):
+            expert_grads = weight_sums(e, expert_grads, grad_part)
+        grad_normed_one, expert_grads = scatter_plane(
+            lambda index: of_core(grad_one_part, index),
+            lambda token: weight_sums(local_experts - 2, expert_grads, token, grad_part),
+        )
+        wide_grads, shared_down_grads = after((wide_grads, shared_down_grads), expert_grads)
+    else:
+        grad_normed_one = scatter_plane(lambda index: of_core(grad_one_part, index))
+    grad_shared_gate = placed(wide_grads[:, 0], 1)
+    grad_shared_up = placed(wide_grads[:, 1], 1)
+    grad_shared_down = placed(shared_down_grads, 0)
     grad_attn_gain = jnp.sum(grad_normed_one * inputs * scale_one, axis=0)
     grad_own = grad_after + norm_back(inputs, scale_one, gain_one, grad_normed_one)
-    grad_tokens = lax.all_gather(grad_own, "tensor", axis=0, tiled=True)
-
-    grad_qkv_part = dot_tn(normed_one, grad_qkv).astype(BF16)
-    qkv_sum = lax.psum_scatter(grad_qkv_part, "dp", scatter_dimension=0, tiled=True)
-    qkv_rows = (
-        lax.all_to_all(qkv_sum.reshape(groups, part_rows // groups, 3, width), "expert", 0, 0)
+    if gathered:
+        expert_grads = weight_sums(local_experts - 1, expert_grads, grad_own, weight_sum)
+    else:
+        expert_grads = [
+            jnp.stack([block_of(values, first + stride * e, hidden).T for e in range(local_experts)]).astype(F32)
+            for values, first, stride in ((gu_part, 0, 2), (gu_part, 1, 2), (down_part, 0, 1))
+        ]
+    grad_expert_gate, grad_expert_up = (jnp.swapaxes(grad, 1, 2) for grad in expert_grads[:2])
+    grad_expert_down = expert_grads[2]
+    grad_tokens = both_cores(grad_own)
+
+    weight_rows = (
+        lax.all_to_all(weight_sum, "expert", 0, 0)
         .transpose(2, 1, 0, 3)
-        .reshape(3, part_rows // groups, groups * width)
+        .reshape(4, small_rows, groups * width)
         .astype(F32)
     )
-    out_sum = lax.psum_scatter(grad_out_part, "dp", scatter_dimension=1, tiled=True)
-    grad_out_weight = lax.all_to_all(
-        out_sum.reshape(width, groups, part_rows // groups), "expert", 1, 0
-    ).reshape(groups * width, part_rows // groups).astype(F32)
+    qkv_rows = weight_rows[:3]
+    grad_out_weight = weight_rows[3].T
 
     bias_sums = jnp.sum(grad_qkv, axis=0, dtype=F32).reshape(1, 3, heads, HD)
     bias_table = lax.dynamic_update_slice(
@@ -458,7 +873,8 @@
         ],
         axis=1,
     )
-    sums = lax.psum_scatter(lax.psum(spread, "tensor"), ("dp", "expert"), scatter_dimension=0, tiled=True)[0]
+    sums = jnp.sum(lax.all_to_all(spread, ("dp", "expert"), 0, 0, tiled=True), axis=0, keepdims=True)
+    sums = lax.psum(sums, "tensor")[0] if cores != 2 else (sums + lax.ppermute(sums, "tensor", [(0, 1), (1, 0)]))[0]
     gain_part = model_width // devices
     grad_attn_gain, grad_mlp_gain = sums[:gain_part], sums[gain_part : 2 * gain_part]
     table = sums[2 * gain_part :]

time: 1240 us -> 687 us (0.55)
  waiting for transfers between devices: 734 us -> 128 us
  Pallas kernels: 20.8 us -> 252 us
  matrix products: 219 us -> 86.3 us
  blocking collectives: 54.5 us -> 0 us
  local copies, waits for them, and re-layouts: 59.7 us -> 79.3 us
    reduce_scatter x6 -> x2, waiting for transfers between devices: 494 us -> 0.01 us  [the longest x1 0.01 us: per_device(): lax.psum_scatter(after(mixed_part, grad_normed_two), ('tensor', 'expert')...]
    pallas_call x0 -> x7, Pallas kernels: none -> 231 us  [the longest x3 155 us: weight_grads(): pl.pallas_call(functools.partial(weight_kernel, block, hidden), grid_spec...]
    dot_general x12 -> x3, matrix products: 100 us -> 8.85 us  [dot_nt(): lax.dot_general(left, right, (((1,), (1,)), ((), ())), preferred_element_...]
    all_gather x1 -> x0, blocking collectives: 49.9 us -> none  [per_device(): lax.all_gather(jnp.stack([segments, picks]), ('dp', 'expert'), axis=1, ti...]
    ppermute x1, waiting for transfers between devices: 34.9 us -> 0.01 us  [per_device(): lax.ppermute(back_kv, 'dp', [(i + 1, i) for i in range(planes - 1)])]
    ppermute x9, waiting for transfers between devices: 63.9 us -> 30.5 us  [gather_plane(): came = lax.ppermute(own, 'expert', shift_pairs(groups, step))]
    dot_general x12 -> x6, matrix products: 55.2 us -> 22.1 us  [dot_tn(): lax.dot_general(left, right, (((0,), (0,)), ((), ())), preferred_element_...]
    all_gather x3 -> x2, waiting for transfers between devices: 29.6 us -> 0.02 us  [the longest x1 0.02 us: per_device(): lax.all_gather(after(normed_own, normed_two), ('dp', 'tensor', 'expert'),...]
  transfers between devices with their start and end apart: 41 -> 43, of which waited for: 30 -> 20; matrix products, arithmetic and copies ran while one was open for 19% -> 28% of each run, Pallas kernels for 0% -> 37%
where the time goes in v2:
time: 687 us; the launch traced here: 678 us
  Pallas kernels  252 us (37%)
  waiting for transfers between devices  128 us (19%)
  matrix products  86.3 us (13%)
  local copies, waits for them, and re-layouts  79.3 us (12%)
  other arithmetic  61.9 us (9%)
  starting transfers between devices  54 us (8%)
  between operations  15.7 us (2%)
    pallas_call x3, Pallas kernels, weight_grads(): pl.pallas_call(functools.partial(weight_kernel, block, hidden), grid_spec...  155 us
    dot_general x10, matrix products, dot(): return jnp.dot(left, right, preferred_element_type=F32)  55.3 us
    pallas_call x1, Pallas kernels, feed(): pl.pallas_call(feed_kernel, grid_spec=grid_spec, out_shape=[jax.ShapeDtyp...  40.7 us
    ppermute x9, waiting for transfers between devices, scatter_plane(): lax.ppermute(sent[step - 1], 'expert', shift_pairs(groups, step))  39.9 us
    unnamed x178, local copies, waits for them, and re-layouts  34.2 us
    ppermute x3, waiting for transfers between devices, per_device(): lax.ppermute(facts, 'dp', [(i, (i + step) % planes) for i in range(planes)])  33.5 us
    ppermute x9, waiting for transfers between devices, gather_plane(): came = lax.ppermute(own, 'expert', shift_pairs(groups, step))  30.5 us
    dot_general x6, matrix products, dot_tn(): lax.dot_general(left, right, (((0,), (0,)), ((), ())), preferred_element_...  22.1 us
  transfers between devices with their start and end apart: 43, of which 20 were waited for; matrix products, arithmetic and copies ran while one was open for 28% of the time, Pallas kernels for 37%

profile of v2, /device:TPU:1, one launch (start us, length us, event | category | flops | bytes accessed | tf_op | source)
XLA Modules:
  0.0 677.8 jit_solution(5023997461858127293)
XLA Ops:
  12.5 3.0 collective-permute-start.2
  18.6 2.6 copy-done.2
  21.2 17.6 %pack_weights.1 = (bf16[4608,2048]{1,0:T(8,128)(2,1)}, bf16[2304,2048]{1,0:T(8,128)(2,1)}) custom-call(s32[2]{0:T(128)S(1)} %pad_add_fusion.window_ref, bf16[2,704,2048]{2,1,0:T(8,128)(2,1)S(1)} %bitcast.210, bf16[2,704,2048]{2,1,0:T(8,128)(2,1)S(1)} %bitcast.211, bf16[2,704,2048]{2,1,0:T(8,128)(2,1)} %refs_2_.1, bf16[2048,2816]{1,0:T(8,128)(2,1)} %refs_8_.1, ...), custom_call_target="tpu_custom_call" | custom-call | bytes 56623104 | tf_op jit(solution)/shard_map/pack_weights/pallas_call | solution.py:403
  38.9 4.3 collective-permute-done.1
  64.2 3.5 collective-permute-start.4
  78.0 30.8 %collective-permute-done.10 = bf16[16,1024]{1,0:T(8,128)(2,1)S(1)} collective-permute-done((bf16[16,1024]{1,0:T(8,128)(2,1)S(1)}, bf16[16,1024]{1,0:T(8,128)(2,1)S(1)}, u32[]{:S(2)}, u32[]{:S(2)}) %collective-permute-start.10) | collective-permute-done | bytes 32800 | tf_op jit(solution)/shard_map/ppermute | solution.py:643
  115.2 7.1 %attend.1 = bf16[1024,256]{1,0:T(8,128)(2,1)S(1)} custom-call(bf16[1024,256]{1,0:T(8,128)(2,1)S(1)} %copy.397.q_ref, bf16[1024,512]{1,0:T(8,128)(2,1)S(1)} %collective-permute-done.4.kb_ref.vb_ref, bf16[1024,512]{1,0:T(8,128)(2,1)S(1)} %collective-permute-done.4.kb_ref.vb_ref, bf16[1024,512]{1,0:T(8,128)(2,1)S(1)} %pad_maximum_fusion.17.ko_ref.vo_ref, ...), custom_call_target="tpu_custom_call" | custom-call | flops 1073741824 | bytes 3145728 | tf_op jit(solution)/shard_map/attend/pallas_call | solution.py:254
  125.5 3.9 collective-permute-done.11
  129.4 2.7 convert_add_fusion.2
  135.1 10.2 %collective-permute-done.12 = bf16[128,2048]{1,0:T(8,128)(2,1)S(1)} collective-permute-done((bf16[128,2048]{1,0:T(8,128)(2,1)S(1)}, bf16[128,2048]{1,0:T(8,128)(2,1)S(1)}, u32[]{:S(2)}, u32[]{:S(2)}) %collective-permute-start.12) | collective-permute-done | bytes 524320 | tf_op jit(solution)/shard_map/ppermute | solution.py:99
  145.3 11.9 %collective-permute-done.14 = bf16[128,2048]{1,0:T(8,128)(2,1)S(1)} collective-permute-done((bf16[128,2048]{1,0:T(8,128)(2,1)S(1)}, bf16[128,2048]{1,0:T(8,128)(2,1)S(1)}, u32[]{:S(2)}, u32[]{:S(2)}) %collective-permute-start.14) | collective-permute-done | bytes 524320 | tf_op jit(solution)/shard_map/ppermute | solution.py:99
  163.0 8.9 %collective-permute-done.17 = bf16[128,2048]{1,0:T(8,128)(2,1)S(1)} collective-permute-done((bf16[128,2048]{1,0:T(8,128)(2,1)S(1)}, bf16[128,2048]{1,0:T(8,128)(2,1)S(1)}, u32[]{:S(2)}, u32[]{:S(2)}) %collective-permute-start.17) | collective-permute-done | bytes 524320 | tf_op jit(solution)/shard_map/ppermute | solution.py:69
  171.9 14.5 %collective-permute-done.16 = bf16[128,2048]{1,0:T(8,128)(2,1)S(1)} collective-permute-done((bf16[128,2048]{1,0:T(8,128)(2,1)S(1)}, bf16[128,2048]{1,0:T(8,128)(2,1)S(1)}, u32[]{:S(2)}, u32[]{:S(2)}) %collective-permute-start.16) | collective-permute-done | bytes 524320 | tf_op jit(solution)/shard_map/ppermute | solution.py:69
  189.3 4.0 collective-permute-done.18
  200.2 3.4 fusion.96
  204.8 40.7 %feed.1 = (bf16[1024,2304]{1,0:T(8,128)(2,1)}, bf16[1024,4608]{1,0:T(8,128)(2,1)}, f32[3,1024,1]{2,1,0:T(8,128)}) custom-call(s32[1]{0:T(128)} %bitcast.31.chunk_ref.plane_ref, bf16[1024,2048]{1,0:T(8,128)(2,1)} %pad_maximum_fusion.rows_ref, bf16[4096,2048]{1,0:T(8,128)(2,1)} %all-gather.3.cloned.1.call-done.top_ref.part_ref, f32[1024,3]{1,0:T(8,128)} %copy.368.gates_ref, ...), custom_call_target="tpu_custom_call" | custom-call | flops 28991029248 | bytes 53477376 | tf_op jit(solution)/shard_map/feed/pallas_call | solution.py:494
  251.1 22.5 %add_convert_fusion = bf16[1024,2048]{1,0:T(8,128)(2,1)S(1)} fusion(f32[1024,2048]{1,0:T(8,128)S(1)} %fusion.57, bf16[1024,4608]{1,0:T(8,128)(2,1)S(1)} %copy-done.18, bf16[4608,2048]{1,0:T(8,128)(2,1)} %get-tuple-element.94.gu_ref), kind=kOutput, calls=%fused_computation | convolution fusion | flops 19331547136 | bytes 40894464 | tf_op jit(solution)/shard_map/dot_general | solution.py:26
  279.3 4.3 collective-permute-done.19
  291.8 14.2 %convolution_convert_fusion = bf16[1024,2048]{1,0:T(8,128)(2,1)} fusion(bf16[1024,2304]{1,0:T(8,128)(2,1)S(1)} %bitcast.280, bf16[2304,2048]{1,0:T(8,128)(2,1)} %get-tuple-element.95.down_ref), kind=kOutput, calls=%fused_computation.10 | convolution fusion | flops 9665773568 | bytes 18350080 | tf_op jit(solution)/shard_map/dot_general | solution.py:26
  306.0 5.4 fusion.9.gu_in
  311.4 3.9 collective-permute-done.22
  315.3 11.9 %collective-permute-done.21 = bf16[128,2048]{1,0:T(8,128)(2,1)} collective-permute-done((bf16[128,2048]{1,0:T(8,128)(2,1)}, bf16[128,2048]{1,0:T(8,128)(2,1)}, u32[]{:S(2)}, u32[]{:S(2)}) %collective-permute-start.21) | collective-permute-done | bytes 524320 | tf_op jit(solution)/shard_map/ppermute | solution.py:99
  329.3 3.3 multiply_reduce_fusion
  338.6 6.4 turn.2.top_t_ref
  349.8 3.6 fusion.5.gu_in
  355.5 3.5 fusion.7.gu_in
  359.0 2.9 collective-permute-done.25
  366.3 3.1 collective-permute-done.27
  369.4 2.8 broadcast_select_fusion.1
  372.2 3.5 fusion.30
  375.8 14.0 %attend_back.1 = (f32[1024,256]{1,0:T(8,128)S(1)}, f32[1024,256]{1,0:T(8,128)S(1)}, f32[1024,256]{1,0:T(8,128)S(1)}, f32[1024,256]{1,0:T(8,128)S(1)}, f32[1024,256]{1,0:T(8,128)}) custom-call(bf16[1024,256]{1,0:T(8,128)(2,1)S(1)} %copy.397.q_ref, bf16[1024,512]{1,0:T(8,128)(2,1)} %copy-done.4, bf16[1024,512]{1,0:T(8,128)(2,1)} %copy-done.4, ...), custom_call_target="tpu_custom_call" | custom-call | flops 2684354560 | bytes 8388608 | tf_op jit(solution)/shard_map/attend_back/pallas_call | solution.py:272
  392.7 2.7 copy.371
  397.9 12.1 %turn.3 = (bf16[512,4096]{1,0:T(8,128)(2,1)S(1)}, f32[4096,128]{1,0:T(8,128)S(1)}) custom-call(s32[1]{0:T(128)} %bitcast.31.chunk_ref.plane_ref, bf16[4096,2048]{1,0:T(8,128)(2,1)} %all-gather.5.cloned.1.call-done.part_ref.rows_ref, bf16[4096,2048]{1,0:T(8,128)(2,1)} %all-gather.5.cloned.1.call-done.part_ref.rows_ref, ...), custom_call_target="tpu_custom_call" | custom-call | bytes 16777216 | tf_op jit(solution)/shard_map/turn/pallas_call | solution.py:461
  417.1 50.4 %weight_grads.3 = (bf16[4,128,768]{2,1,0:T(8,128)(2,1)}, bf16[4,128,768]{2,1,0:T(8,128)(2,1)}, bf16[4,768,128]{2,1,0:T(8,128)(2,1)}) custom-call(s32[1]{0:T(128)} %bitcast.31.chunk_ref.plane_ref, bf16[4096,2048]{1,0:T(8,128)(2,1)} %all-gather.5.cloned.1.call-done.part_ref.rows_ref, bf16[4096,2048]{1,0:T(8,128)(2,1)} %all-gather.3.cloned.1.call-done.top_ref.part_ref, ...), custom_call_target="tpu_custom_call" | custom-call | flops 36238786560 | bytes 42991616 | tf_op jit(solution)/shard_map/weight_grads/pallas_call | solution.py:553
  476.2 4.1 convolution_convert_fusion.1
  486.5 4.5 fusion.13
  491.0 3.6 all-to-all-start.3
  499.3 3.8 convolution_convert_fusion.2
  505.4 3.0 convert_add_fusion
  515.2 3.7 all-to-all-start.2
  518.9 52.1 %weight_grads.4 = (f32[2,704,512]{2,1,0:T(8,128)}, f32[2,704,512]{2,1,0:T(8,128)}, f32[2,704,512]{2,1,0:T(8,128)}) custom-call(s32[1]{0:T(128)} %bitcast.31.chunk_ref.plane_ref, bf16[4096,2048]{1,0:T(8,128)(2,1)} %all-gather.5.cloned.1.call-done.part_ref.rows_ref, bf16[4096,2048]{1,0:T(8,128)(2,1)} %all-gather.3.cloned.1.call-done.top_ref.part_ref, ...), custom_call_target="tpu_custom_call" | custom-call | flops 36238786560 | bytes 42991616 | tf_op jit(solution)/shard_map/weight_grads/pallas_call | solution.py:553
  576.1 3.3 fusion.41
  580.2 5.8 all-to-all-start
  586.1 6.6 all-to-all-done
  592.7 4.1 collective-permute-start.34
  596.9 3.3 fusion.37
  611.1 3.7 all-to-all-start.1
  614.8 52.0 %weight_grads.5 = (f32[2,704,512]{2,1,0:T(8,128)}, f32[2,704,512]{2,1,0:T(8,128)}, f32[2,704,512]{2,1,0:T(8,128)}) custom-call(s32[1]{0:T(128)} %bitcast.31.chunk_ref.plane_ref, bf16[4096,2048]{1,0:T(8,128)(2,1)} %all-gather.5.cloned.1.call-done.part_ref.rows_ref, ...), custom_call_target="tpu_custom_call", output_to_operand_aliasing={{0}: (10, {}), {1}: (11, {}), {2}: (12, {})} | custom-call | flops 36238786560 | bytes 42991616 | tf_op jit(solution)/shard_map/weight_grads/pallas_call | solution.py:553
  (417 shorter events, 169.3 us)
Async XLA Ops:
  7.2 197.6 %all-gather.3.cloned.1.call-start = ((), (), s32[]{:S(2)}) async-start(), calls=%async_computation.6 | async-start | bytes 17301504 | tf_op jit(solution)/shard_map/all_gather | solution.py:648
  9.2 388.6 %all-gather.5.cloned.1.call-start = ((), (), s32[]{:S(2)}) async-start(), calls=%async_computation.8 | async-start | bytes 17301504 | tf_op jit(solution)/shard_map/all_gather | solution.py:693
  12.5 26.4 %collective-permute-start.2 = (bf16[128,2048]{1,0:T(8,128)(2,1)}, bf16[128,2048]{1,0:T(8,128)(2,1)S(1)}, u32[]{:S(2)}, u32[]{:S(2)}) collective-permute-start(bf16[128,2048]{1,0:T(8,128)(2,1)} %get-tuple-element.296), channel_id=1, source_target_pairs={{0,6},{2,4},{4,2},{6,0},{1,7},{3,5},{5,3},{7,1},{8,14},{10,12},{12... | collective-permute-start | bytes 1572872 | tf_op jit(solution)/shard_map/ppermute | solution.py:69
  15.5 27.7 %collective-permute-start.1 = (bf16[128,2048]{1,0:T(8,128)(2,1)}, bf16[128,2048]{1,0:T(8,128)(2,1)S(1)}, u32[]{:S(2)}, u32[]{:S(2)}) collective-permute-start(bf16[128,2048]{1,0:T(8,128)(2,1)} %get-tuple-element.296), channel_id=1, source_target_pairs={{0,4},{2,6},{4,0},{6,2},{1,5},{3,7},{5,1},{7,3},{8,12},{10,14},{12... | collective-permute-start | bytes 1572872 | tf_op jit(solution)/shard_map/ppermute | solution.py:69
  15.7 27.5 %collective-permute-start = (bf16[128,2048]{1,0:T(8,128)(2,1)}, bf16[128,2048]{1,0:T(8,128)(2,1)}, u32[]{:S(2)}, u32[]{:S(2)}) collective-permute-start(bf16[128,2048]{1,0:T(8,128)(2,1)} %get-tuple-element.296), channel_id=1, source_target_pairs={{0,2},{2,0},{4,6},{6,4},{1,3},{3,1},{5,7},{7,5},{8,10},{10,8},{12,... | collective-permute-start | bytes 1572872 | tf_op jit(solution)/shard_map/ppermute | solution.py:69
  44.4 7.8 %collective-permute-start.3 = (bf16[512,2048]{1,0:T(8,128)(2,1)S(1)}, bf16[512,2048]{1,0:T(8,128)(2,1)}, u32[]{:S(2)}, u32[]{:S(2)}) collective-permute-start(bf16[512,2048]{1,0:T(8,128)(2,1)S(1)} %constant_dynamic-update-slice_fusion.10), channel_id=1, source_target_pairs={{0,1},{1,0},{2,3},{3,2},{4,5},{5,4},{6,7},{7,6},{8,9},{9,8},{10,11... | collective-permute-start | bytes 6291464 | tf_op jit(solution)/shard_map/ppermute | solution.py:73
  64.1 48.9 %copy-start.45 = (bf16[1024,2,64]{0,2,1:T(8,128)(2,1)S(1)}, bf16[1024,2,64]{0,2,1:T(8,128)(2,1)}, u32[]{:S(2)}) copy-start(bf16[1024,2,64]{0,2,1:T(8,128)(2,1)} %get-tuple-element.346) | copy-start | bytes 786436
  64.2 51.0 %copy-start = (bf16[1024,512]{1,0:T(8,128)(2,1)}, bf16[1024,512]{1,0:T(8,128)(2,1)S(1)}, u32[]{:S(2)}) copy-start(bf16[1024,512]{1,0:T(8,128)(2,1)S(1)} %pad_maximum_fusion.17.ko_ref.vo_ref) | copy-start | bytes 3145732
  64.2 50.9 %collective-permute-start.4 = (bf16[1024,512]{1,0:T(8,128)(2,1)S(1)}, bf16[1024,512]{1,0:T(8,128)(2,1)S(1)}, u32[]{:S(2)}, u32[]{:S(2)}) collective-permute-start(bf16[1024,512]{1,0:T(8,128)(2,1)S(1)} %pad_maximum_fusion.17.ko_ref.vo_ref), channel_id=1, source_target_pairs={{0,8},{8,16},{16,24},{1,9},{9,17},{17,25},{2,10},{10,18},{18,26},{... | collective-permute-start | bytes 3145736 | tf_op jit(solution)/shard_map/ppermute | solution.py:676
  67.8 3.5 collective-permute-start.7
  69.0 2.9 collective-permute-start.6
  70.3 2.9 collective-permute-start.5
  73.5 35.3 %collective-permute-start.10 = (bf16[16,1024]{1,0:T(8,128)(2,1)S(1)}, bf16[16,1024]{1,0:T(8,128)(2,1)S(1)}, u32[]{:S(2)}, u32[]{:S(2)}) collective-permute-start(bf16[16,1024]{1,0:T(8,128)(2,1)S(1)} %bitcast.265), channel_id=1, source_target_pairs={{0,24},{8,0},{16,8},{24,16},{1,25},{9,1},{17,9},{25,17},{2,26},{10... | collective-permute-start | bytes 98312 | tf_op jit(solution)/shard_map/ppermute | solution.py:643
  74.8 35.4 %collective-permute-start.9 = (bf16[16,1024]{1,0:T(8,128)(2,1)S(1)}, bf16[16,1024]{1,0:T(8,128)(2,1)S(1)}, u32[]{:S(2)}, u32[]{:S(2)}) collective-permute-start(bf16[16,1024]{1,0:T(8,128)(2,1)S(1)} %bitcast.266), channel_id=1, source_target_pairs={{0,16},{8,24},{16,0},{24,8},{1,17},{9,25},{17,1},{25,9},{2,18},{10... | collective-permute-start | bytes 98312 | tf_op jit(solution)/shard_map/ppermute | solution.py:643
  75.9 35.7 %collective-permute-start.8 = (bf16[16,1024]{1,0:T(8,128)(2,1)S(1)}, bf16[16,1024]{1,0:T(8,128)(2,1)S(1)}, u32[]{:S(2)}, u32[]{:S(2)}) collective-permute-start(bf16[16,1024]{1,0:T(8,128)(2,1)S(1)} %bitcast.267), channel_id=1, source_target_pairs={{0,8},{8,16},{16,24},{24,0},{1,9},{9,17},{17,25},{25,1},{2,10},{10... | collective-permute-start | bytes 98312 | tf_op jit(solution)/shard_map/ppermute | solution.py:643
  124.5 4.9 collective-permute-start.11
  132.4 12.9 %collective-permute-start.12 = (bf16[128,2048]{1,0:T(8,128)(2,1)S(1)}, bf16[128,2048]{1,0:T(8,128)(2,1)S(1)}, u32[]{:S(2)}, u32[]{:S(2)}) collective-permute-start(bf16[128,2048]{1,0:T(8,128)(2,1)S(1)} %get-tuple-element.307), channel_id=1, source_target_pairs={{0,2},{2,0},{4,6},{6,4},{1,3},{3,1},{5,7},{7,5},{8,10},{10,8},{12,... | collective-permute-start | bytes 1572872 | tf_op jit(solution)/shard_map/ppermute | solution.py:99
  132.4 24.7 %collective-permute-start.14 = (bf16[128,2048]{1,0:T(8,128)(2,1)S(1)}, bf16[128,2048]{1,0:T(8,128)(2,1)S(1)}, u32[]{:S(2)}, u32[]{:S(2)}) collective-permute-start(bf16[128,2048]{1,0:T(8,128)(2,1)S(1)} %get-tuple-element.308), channel_id=1, source_target_pairs={{0,6},{2,4},{4,2},{6,0},{1,7},{3,5},{5,3},{7,1},{8,14},{10,12},{12... | collective-permute-start | bytes 1572872 | tf_op jit(solution)/shard_map/ppermute | solution.py:99
  134.5 22.7 %collective-permute-start.13 = (bf16[128,2048]{1,0:T(8,128)(2,1)S(1)}, bf16[128,2048]{1,0:T(8,128)(2,1)S(1)}, u32[]{:S(2)}, u32[]{:S(2)}) collective-permute-start(bf16[128,2048]{1,0:T(8,128)(2,1)S(1)} %get-tuple-element.309), channel_id=1, source_target_pairs={{0,4},{2,6},{4,0},{6,2},{1,5},{3,7},{5,1},{7,3},{8,12},{10,14},{12... | collective-permute-start | bytes 1572872 | tf_op jit(solution)/shard_map/ppermute | solution.py:99
  135.1 199.1 %copy-start.56 = (f32[2048]{0:T(1024)}, f32[2048]{0:T(1024)S(1)}, u32[]{:S(2)}) copy-start(f32[2048]{0:T(1024)S(1)} %convert_element_type.343) | copy-start | bytes 24580
  157.7 176.4 %copy-start.12 = (f32[128,2048]{1,0:T(8,128)}, f32[128,2048]{1,0:T(8,128)S(1)}, u32[]{:S(2)}) copy-start(f32[128,2048]{1,0:T(8,128)S(1)} %get-tuple-element.294) | copy-start | bytes 3145732
  157.7 176.4 %copy-start.67 = (f32[128]{0:T(128)}, f32[128]{0:T(128)S(1)}, u32[]{:S(2)}) copy-start(f32[128]{0:T(128)S(1)} %add_rsqrt_fusion) | copy-start | bytes 1540
  160.4 11.5 %collective-permute-start.17 = (bf16[128,2048]{1,0:T(8,128)(2,1)S(1)}, bf16[128,2048]{1,0:T(8,128)(2,1)S(1)}, u32[]{:S(2)}, u32[]{:S(2)}) collective-permute-start(bf16[128,2048]{1,0:T(8,128)(2,1)S(1)} %get-tuple-element.122), channel_id=1, source_target_pairs={{0,6},{2,4},{4,2},{6,0},{1,7},{3,5},{5,3},{7,1},{8,14},{10,12},{12... | collective-permute-start | bytes 1572872 | tf_op jit(solution)/shard_map/ppermute | solution.py:69
  161.8 24.5 %collective-permute-start.16 = (bf16[128,2048]{1,0:T(8,128)(2,1)S(1)}, bf16[128,2048]{1,0:T(8,128)(2,1)S(1)}, u32[]{:S(2)}, u32[]{:S(2)}) collective-permute-start(bf16[128,2048]{1,0:T(8,128)(2,1)S(1)} %get-tuple-element.122), channel_id=1, source_target_pairs={{0,4},{2,6},{4,0},{6,2},{1,5},{3,7},{5,1},{7,3},{8,12},{10,14},{12... | collective-permute-start | bytes 1572872 | tf_op jit(solution)/shard_map/ppermute | solution.py:69
  162.7 23.6 %collective-permute-start.15 = (bf16[128,2048]{1,0:T(8,128)(2,1)S(1)}, bf16[128,2048]{1,0:T(8,128)(2,1)S(1)}, u32[]{:S(2)}, u32[]{:S(2)}) collective-permute-start(bf16[128,2048]{1,0:T(8,128)(2,1)S(1)} %get-tuple-element.122), channel_id=1, source_target_pairs={{0,2},{2,0},{4,6},{6,4},{1,3},{3,1},{5,7},{7,5},{8,10},{10,8},{12,... | collective-permute-start | bytes 1572872 | tf_op jit(solution)/shard_map/ppermute | solution.py:69
  188.8 4.5 collective-permute-start.18
  199.8 397.0 %reduce-scatter.3.cloned.1.call-start = ((), (), s32[]{:S(2)}) async-start(), calls=%async_computation.7 | async-start | bytes 4718592 | tf_op jit(solution)/shard_map/reduce_scatter | solution.py:728
  277.0 6.6 collective-permute-start.19
  289.2 26.1 %collective-permute-start.22 = (bf16[128,2048]{1,0:T(8,128)(2,1)}, bf16[128,2048]{1,0:T(8,128)(2,1)}, u32[]{:S(2)}, u32[]{:S(2)}) collective-permute-start(bf16[128,2048]{1,0:T(8,128)(2,1)} %get-tuple-element.302), channel_id=1, source_target_pairs={{0,6},{2,4},{4,2},{6,0},{1,7},{3,5},{5,3},{7,1},{8,14},{10,12},{12... | collective-permute-start | bytes 1572872 | tf_op jit(solution)/shard_map/ppermute | solution.py:99
  291.0 36.2 %collective-permute-start.21 = (bf16[128,2048]{1,0:T(8,128)(2,1)}, bf16[128,2048]{1,0:T(8,128)(2,1)}, u32[]{:S(2)}, u32[]{:S(2)}) collective-permute-start(bf16[128,2048]{1,0:T(8,128)(2,1)} %get-tuple-element.303), channel_id=1, source_target_pairs={{0,4},{2,6},{4,0},{6,2},{1,5},{3,7},{5,1},{7,3},{8,12},{10,14},{12... | collective-permute-start | bytes 1572872 | tf_op jit(solution)/shard_map/ppermute | solution.py:99
  291.6 37.6 %collective-permute-start.20 = (bf16[128,2048]{1,0:T(8,128)(2,1)}, bf16[128,2048]{1,0:T(8,128)(2,1)}, u32[]{:S(2)}, u32[]{:S(2)}) collective-permute-start(bf16[128,2048]{1,0:T(8,128)(2,1)} %get-tuple-element.304), channel_id=1, source_target_pairs={{0,2},{2,0},{4,6},{6,4},{1,3},{3,1},{5,7},{7,5},{8,10},{10,8},{12,... | collective-permute-start | bytes 1572872 | tf_op jit(solution)/shard_map/ppermute | solution.py:99
  335.8 23.2 %collective-permute-start.26 = (bf16[128,2048]{1,0:T(8,128)(2,1)S(1)}, bf16[128,2048]{1,0:T(8,128)(2,1)S(1)}, u32[]{:S(2)}, u32[]{:S(2)}) collective-permute-start(bf16[128,2048]{1,0:T(8,128)(2,1)S(1)} %get-tuple-element.289), channel_id=1, source_target_pairs={{0,6},{2,4},{4,2},{6,0},{1,7},{3,5},{5,3},{7,1},{8,14},{10,12},{12... | collective-permute-start | bytes 1572872 | tf_op jit(solution)/shard_map/ppermute | solution.py:69
  337.0 24.8 %collective-permute-start.25 = (bf16[128,2048]{1,0:T(8,128)(2,1)S(1)}, bf16[128,2048]{1,0:T(8,128)(2,1)S(1)}, u32[]{:S(2)}, u32[]{:S(2)}) collective-permute-start(bf16[128,2048]{1,0:T(8,128)(2,1)S(1)} %get-tuple-element.289), channel_id=1, source_target_pairs={{0,4},{2,6},{4,0},{6,2},{1,5},{3,7},{5,1},{7,3},{8,12},{10,14},{12... | collective-permute-start | bytes 1572872 | tf_op jit(solution)/shard_map/ppermute | solution.py:69
  337.5 24.4 %collective-permute-start.24 = (bf16[128,2048]{1,0:T(8,128)(2,1)S(1)}, bf16[128,2048]{1,0:T(8,128)(2,1)S(1)}, u32[]{:S(2)}, u32[]{:S(2)}) collective-permute-start(bf16[128,2048]{1,0:T(8,128)(2,1)S(1)} %get-tuple-element.289), channel_id=1, source_target_pairs={{0,2},{2,0},{4,6},{6,4},{1,3},{3,1},{5,7},{7,5},{8,10},{10,8},{12,... | collective-permute-start | bytes 1572872 | tf_op jit(solution)/shard_map/ppermute | solution.py:69
  364.4 5.0 collective-permute-start.27
  396.6 71.0 %collective-permute-start.28 = (bf16[1024,512]{1,0:T(8,128)(2,1)}, bf16[1024,512]{1,0:T(8,128)(2,1)S(1)}, u32[]{:S(2)}, u32[]{:S(2)}) collective-permute-start(bf16[1024,512]{1,0:T(8,128)(2,1)} %pad_maximum_fusion.19), channel_id=1, source_target_pairs={{8,0},{16,8},{24,16},{9,1},{17,9},{25,17},{10,2},{18,10},{26,18},{... | collective-permute-start | bytes 3145736 | tf_op jit(solution)/shard_map/ppermute | solution.py:815
  483.4 22.0 %collective-permute-start.29 = (bf16[512,2048]{1,0:T(8,128)(2,1)}, bf16[512,2048]{1,0:T(8,128)(2,1)}, u32[]{:S(2)}, u32[]{:S(2)}) collective-permute-start(bf16[512,2048]{1,0:T(8,128)(2,1)} %constant_dynamic-slice_fusion.4), channel_id=1, source_target_pairs={{0,1},{1,0},{2,3},{3,2},{4,5},{5,4},{6,7},{7,6},{8,9},{9,8},{10,11... | collective-permute-start | bytes 6291464 | tf_op jit(solution)/shard_map/ppermute | solution.py:91
  491.0 23.3 %all-to-all-start.3 = ((bf16[4,768,128]{2,1,0:T(8,128)(2,1)}), bf16[4,768,128]{2,1,0:T(8,128)(2,1)S(1)}, u32[]{:S(2)}, u32[]{:S(2)}) async-start(bf16[4,768,128]{2,1,0:T(8,128)(2,1)} %get-tuple-element.129), calls=%async_computation.5 | async-start | bytes 1572864 | tf_op jit(solution)/shard_map/all_to_all | solution.py:758
  494.6 113.9 %reduce-scatter.5.cloned.1.call-start = ((), (), s32[]{:S(2)}) async-start(), calls=%async_computation.9 | async-start | bytes 5242880 | tf_op jit(solution)/shard_map/reduce_scatter | solution.py:824
  511.7 64.4 %collective-permute-start.32 = (bf16[128,2048]{1,0:T(8,128)(2,1)}, bf16[128,2048]{1,0:T(8,128)(2,1)}, u32[]{:S(2)}, u32[]{:S(2)}) collective-permute-start(bf16[128,2048]{1,0:T(8,128)(2,1)} %get-tuple-element.297), channel_id=1, source_target_pairs={{0,6},{2,4},{4,2},{6,0},{1,7},{3,5},{5,3},{7,1},{8,14},{10,12},{12... | collective-permute-start | bytes 1572872 | tf_op jit(solution)/shard_map/ppermute | solution.py:99
  513.9 62.1 %collective-permute-start.31 = (bf16[128,2048]{1,0:T(8,128)(2,1)}, bf16[128,2048]{1,0:T(8,128)(2,1)}, u32[]{:S(2)}, u32[]{:S(2)}) collective-permute-start(bf16[128,2048]{1,0:T(8,128)(2,1)} %get-tuple-element.298), channel_id=1, source_target_pairs={{0,4},{2,6},{4,0},{6,2},{1,5},{3,7},{5,1},{7,3},{8,12},{10,14},{12... | collective-permute-start | bytes 1572872 | tf_op jit(solution)/shard_map/ppermute | solution.py:99
  514.2 61.9 %collective-permute-start.30 = (bf16[128,2048]{1,0:T(8,128)(2,1)}, bf16[128,2048]{1,0:T(8,128)(2,1)}, u32[]{:S(2)}, u32[]{:S(2)}) collective-permute-start(bf16[128,2048]{1,0:T(8,128)(2,1)} %get-tuple-element.299), channel_id=1, source_target_pairs={{0,2},{2,0},{4,6},{6,4},{1,3},{3,1},{5,7},{7,5},{8,10},{10,8},{12,... | collective-permute-start | bytes 1572872 | tf_op jit(solution)/shard_map/ppermute | solution.py:99
  515.2 55.8 %all-to-all-start.2 = ((bf16[4,2,128,768]{3,2,1,0:T(8,128)(2,1)}), bf16[4,2,128,768]{3,2,1,0:T(8,128)(2,1)S(1)}, u32[]{:S(2)}, u32[]{:S(2)}) async-start(bf16[4,2,128,768]{3,2,1,0:T(8,128)(2,1)} %copy.391), calls=%async_computation.4 | async-start | bytes 3145728 | tf_op jit(solution)/shard_map/all_to_all | solution.py:758
  580.2 12.4 %all-to-all-start = ((f32[16,1,1792]{2,1,0:T(1,128)}), f32[16,1,1792]{2,1,0:T(1,128)S(1)}, u32[]{:S(2)}, u32[]{:S(2)}) async-start(f32[16,1,1792]{2,1,0:T(1,128)} %copy.389), calls=%async_computation.1 | async-start | bytes 229376 | tf_op jit(solution)/shard_map/all_to_all | solution.py:876
  592.7 7.9 %collective-permute-start.34 = (f32[1,1792]{1,0:T(1,128)S(1)}, f32[1,1792]{1,0:T(1,128)S(1)}, u32[]{:S(2)}, u32[]{:S(2)}) collective-permute-start(f32[1,1792]{1,0:T(1,128)S(1)} %broadcast_in_dim.86), channel_id=1, source_target_pairs={{0,1},{1,0},{2,3},{3,2},{4,5},{5,4},{6,7},{7,6},{8,9},{9,8},{10,11... | collective-permute-start | bytes 21512 | tf_op jit(solution)/shard_map/ppermute | solution.py:877
  600.2 3.3 collective-permute-start.23
  600.2 5.5 collective-permute-start.33
  611.1 55.8 %all-to-all-start.1 = ((bf16[4,128,4,256]{1,3,2,0:T(8,128)(2,1)}), bf16[4,128,4,256]{1,3,2,0:T(8,128)(2,1)S(1)}, u32[]{:S(2)}, u32[]{:S(2)}) async-start(bf16[4,128,4,256]{1,3,2,0:T(8,128)(2,1)} %copy.390), calls=%async_computation.3 | async-start | bytes 2097152 | tf_op jit(solution)/shard_map/all_to_all | solution.py:854
  (78 other events, 503.4 us)
Sparse Core Ops, SparseCore 0:
  11.5 134.1 all-gather.2
  199.9 144.5 all-gather.4
  366.4 49.9 reduce-scatter.2
  505.5 77.7 reduce-scatter.4

commit v3 on v2

v3 whole, which is shorter than its diff:
```python
import functools

import jax
import jax.numpy as jnp
from jax import lax
from jax.experimental import pallas as pl
from jax.experimental.pallas import tpu as pltpu
from jax.sharding import PartitionSpec as P

HD = 128
SEQ_LEN = 4096
WINDOW = 1024
EPS = 1e-06
THETA = 1000000.0
NEG_LARGE = -1e30
QUERY_BLOCK = 256
FEED_BLOCK = 512
LANE = 128
FACT_ROWS = 16
GATHERED_PLANES = 4
F32 = jnp.float32
BF16 = jnp.bfloat16


def dot(left, right):
    return jnp.dot(left, right, preferred_element_type=F32)


def dot_nt(left, right):
    return lax.dot_general(left, right, (((1,), (1,)), ((), ())), preferred_element_type=F32)


def dot_tn(left, right):
    return lax.dot_general(left, right, (((0,), (0,)), ((), ())), preferred_element_type=F32)


def shift_pairs(count, step):
    if count & (count - 1) == 0:
        return [(source, source ^ step) for source in range(count)]
    return [(source, (source + step) % count) for source in range(count)]


def partner(index, count, step):
    if count & (count - 1) == 0:
        return index ^ step
    return (index + step) % count


def source(index, count, step):
    if count & (count - 1) == 0:
        return index ^ step
    return (index - step + count) % count


def gather_halves(own, meanwhile=()):
    groups, mine = lax.axis_size("expert"), lax.axis_index("expert")
    rows, width = own.shape
    pieces = jnp.zeros((groups * rows, width), own.dtype)
    pieces = lax.dynamic_update_slice(pieces, own, (mine * rows, 0))
    for step in range(1, groups):
        came = lax.ppermute(own, "expert", shift_pairs(groups, step))
        came = after(came, own, *meanwhile)
        pieces = lax.dynamic_update_slice(pieces, came, (source(mine, groups, step) * rows, 0))
    return pieces, swapped(pieces)


def swapped(values):
    return lax.ppermute(values, "tensor", [(0, 1), (1, 0)])


def scatter_halves(own, other, meanwhile=None):
    groups, mine = lax.axis_size("expert"), lax.axis_index("expert")
    held = own.astype(F32) + swapped(other.astype(BF16)).astype(F32)
    rows, width = held.shape[0] // groups, held.shape[1]

    def of_group(index):
        return lax.dynamic_slice(held, (index * rows, 0), (rows, width))

    sent = [of_group(partner(mine, groups, step)).astype(BF16) for step in range(1, groups)]
    came = [lax.ppermute(sent[step - 1], "expert", shift_pairs(groups, step)) for step in range(1, groups)]
    result = of_group(mine)
    if meanwhile is None:
        return functools.reduce(jnp.add, [part.astype(F32) for part in came], result)
    side = meanwhile(tuple(sent))
    came = lax.optimization_barrier((tuple(came), side))[0]
    return functools.reduce(jnp.add, [part.astype(F32) for part in came], result), side


def after(value, *others):
    return lax.optimization_barrier((value, *others))[0]


def both_cores(own):
    return joined(own, swapped(own))


def joined(own, other):
    core = lax.axis_index("tensor")
    return jnp.concatenate([jnp.where(core == 0, own, other), jnp.where(core == 0, other, own)], axis=0)


def token_order(own, other, groups):
    half, width = own.shape
    both = joined(own, other).reshape(2, groups, half // groups, width)
    return both.transpose(1, 0, 2, 3).reshape(2 * half, width)


def half_order(values, groups):
    total, width = values.shape
    core = lax.axis_index("tensor")
    split = values.reshape(groups, 2, total // (2 * groups), width)
    return tuple(
        lax.dynamic_slice(split, (0, index, 0, 0), (groups, 1, total // (2 * groups), width)).reshape(-1, width)
        for index in (core, 1 - core)
    )


def norm_back(values, inv_scale, gain_vec, grad_normed):
    weighted = grad_normed * gain_vec
    inner_mean = jnp.mean(weighted * values, axis=-1, keepdims=True)
    return inv_scale * weighted - values * inv_scale * inv_scale * inv_scale * inner_mean


def masked_scores(query, keys, seg_query, seg_keys, offset):
    scores = dot_nt(query, keys) * (HD ** (-0.5))
    rows, columns = scores.shape
    distance = (
        lax.broadcasted_iota(jnp.int32, (rows, columns), 0)
        - lax.broadcasted_iota(jnp.int32, (rows, columns), 1)
        + offset
    )
    allowed = (seg_query == seg_keys) & (distance >= 0) & (distance < WINDOW)
    return jnp.where(allowed, scores, NEG_LARGE)


def key_ranges(start, block, rows):
    first_before = min(rows, max(0, (start + rows - WINDOW + 1) // block * block))
    first_own = max(0, (start - WINDOW + 1) // block * block)
    return (first_before, rows), (first_own, start + block)


def probabilities(query, parts, seg_query):
    scores = [masked_scores(query, keys, seg_query, seg_keys, offset) for keys, seg_keys, offset in parts]
    top = functools.reduce(jnp.maximum, [jnp.max(part, axis=-1, keepdims=True) for part in scores])
    expo = [jnp.exp(part - top) for part in scores]
    total = functools.reduce(jnp.add, [jnp.sum(part, axis=-1, keepdims=True) for part in expo])
    inverse = 1.0 / total
    return [part * inverse for part in expo]


def key_parts(start, block, rows, before_ref, own_ref, seg_before, seg_own):
    (before, before_end), (own, own_end) = key_ranges(start, block, rows)
    ranges = []
    if before < before_end:
        ranges.append((before_ref, seg_before, before, before_end, start + rows - before))
    ranges.append((own_ref, seg_own, own, own_end, start - own))
    parts = [(ref[low:high, :HD], seg[:, low:high], offset) for ref, seg, low, high, offset in ranges]
    values = [ref[low:high, HD:] for ref, _, low, high, _ in ranges]
    return parts, values, [(low, high) for _, _, low, high, _ in ranges]


def attend_kernel(block, q_ref, before_ref, own_ref, sq_ref, sb_ref, so_ref, out_ref):
    rows = q_ref.shape[0]
    for start in range(0, rows, block):
        parts, values, _ = key_parts(start, block, rows, before_ref, own_ref, sb_ref, so_ref)
        probs = probabilities(q_ref[start : start + block, :], parts, sq_ref[start : start + block, :])
        total = functools.reduce(
            jnp.add, [dot(part.astype(BF16), value) for part, value in zip(probs, values, strict=True)]
        )
        out_ref[start : start + block, :] = total.astype(BF16)


def attend_back_kernel(
    block, q_ref, before_ref, own_ref, sq_ref, sb_ref, so_ref, grad_ref, gq_ref, gb_ref, go_ref, back_ref
):
    rows = q_ref.shape[0]
    back_ref[...] = jnp.zeros_like(back_ref)
    go_ref[...] = jnp.zeros_like(go_ref)
    scale = HD ** (-0.5)
    for start in range(0, rows, block):
        query = q_ref[start : start + block, :]
        grad = grad_ref[start : start + block, :]
        parts, values, ranges = key_parts(start, block, rows, before_ref, own_ref, sb_ref, so_ref)
        sinks = [back_ref, go_ref][-len(parts) :]
        probs = probabilities(query, parts, sq_ref[start : start + block, :])
        grad_probs = [dot_nt(grad, value) for value in values]
        delta = functools.reduce(
            jnp.add,
            [jnp.sum(p * g, axis=-1, keepdims=True) for p, g in zip(probs, grad_probs, strict=True)],
        )
        grad_query = None
        for p, g, part, sink, (low, high) in zip(probs, grad_probs, parts, sinks, ranges, strict=True):
            grad_scores = (p * (g - delta)).astype(BF16)
            term = dot(grad_scores, part[0])
            grad_query = term if grad_query is None else grad_query + term
            sink[low:high, :HD] += dot_tn(grad_scores, query) * scale
            sink[low:high, HD:] += dot_tn(p.astype(BF16), grad)
        gq_ref[start : start + block, :] = grad_query * scale
    gb_ref[...] = back_ref[...].astype(BF16)


def attention_specs(rows):
    column = pl.BlockSpec((rows, HD), lambda h: (0, h))
    pair = pl.BlockSpec((rows, 2 * HD), lambda h: (0, h))
    seg_rows = pl.BlockSpec((rows, 1), lambda h: (0, 0))
    seg_columns = pl.BlockSpec((1, rows), lambda h: (0, 0))
    return column, pair, [column, pair, pair, seg_rows, seg_columns, seg_columns]


def attend(query, before, own, seg_rows, seg_before, seg_own):
    rows, width = query.shape
    heads = width // HD
    column, _, specs = attention_specs(rows)
    return pl.pallas_call(
        functools.partial(attend_kernel, min(QUERY_BLOCK, rows)),
        grid=(heads,),
        in_specs=specs,
        out_specs=column,
        out_shape=jax.ShapeDtypeStruct((rows, width), BF16),
        compiler_params=pltpu.CompilerParams(vmem_limit_bytes=48 * 2**20),
        cost_estimate=pl.CostEstimate(
            flops=4 * rows * WINDOW * width, bytes_accessed=12 * rows * width, transcendentals=rows * WINDOW * heads
        ),
        name="attend",
    )(query, before, own, seg_rows, seg_before, seg_own)


def attend_back(query, before, own, seg_rows, seg_before, seg_own, grad_heads):
    rows, width = query.shape
    heads = width // HD
    column, pair, specs = attention_specs(rows)
    return pl.pallas_call(
        functools.partial(attend_back_kernel, min(QUERY_BLOCK, rows)),
        grid=(heads,),
        in_specs=specs + [column],
        out_specs=[column, pair, pair],
        out_shape=[
            jax.ShapeDtypeStruct((rows, width), F32),
            jax.ShapeDtypeStruct((rows, 2 * width), BF16),
            jax.ShapeDtypeStruct((rows, 2 * width), F32),
        ],
        scratch_shapes=[pltpu.VMEM((rows, 2 * HD), F32)],
        compiler_params=pltpu.CompilerParams(vmem_limit_bytes=48 * 2**20),
        cost_estimate=pl.CostEstimate(
            flops=10 * rows * WINDOW * width, bytes_accessed=32 * rows * width, transcendentals=rows * WINDOW * heads
        ),
        name="attend_back",
    )(query, before, own, seg_rows, seg_before, seg_own, grad_heads)


def turned(values, cosine, sines):
    return values * cosine + pltpu.roll(values, HD // 2, 1) * sines


def half_rows(index, group, rows, core):
    return pl.ds(pl.multiple_of(2 * group * rows + lax.rem(core + index, 2) * rows, rows), rows)


def project_kernel(
    groups, place_ref, own_ref, other_ref, wq_ref, wk_ref, wv_ref, bias_ref, cos_ref, sin_ref, q_ref, kv_ref
):
    core = place_ref[1]
    half, width = own_ref.shape[0], wq_ref.shape[1]
    rows = half // groups
    for index, ref in enumerate((own_ref, other_ref)):
        here = slice(index * half, (index + 1) * half)
        cosine, sines = cos_ref[here, :], sin_ref[here, :]
        normed = ref[...]
        for k, weight in enumerate((wq_ref, wk_ref, wv_ref)):
            product = dot(normed, weight[...]) + bias_ref[k : k + 1, :].astype(F32)
            for h in range(width // HD):
                values = product[:, h * HD : (h + 1) * HD]
                if k < 2:
                    values = turned(values, cosine, sines)
                values = values.astype(BF16)
                out, at = (q_ref, h * HD) if k == 0 else (kv_ref, (2 * h + k - 1) * HD)
                for group in range(groups):
                    out[half_rows(index, group, rows, core), at : at + HD] = values[group * rows : (group + 1) * rows]


def project(place, halves, weights, bias, cosine, sines, groups):
    half, model_width = halves[0].shape
    width = weights[0].shape[1] // groups
    whole = pl.BlockSpec((half, model_width), lambda i, p: (0, 0))
    weight_spec = pl.BlockSpec((model_width, width), lambda i, p: (0, p[0]))
    table = pl.BlockSpec((2 * half, HD), lambda i, p: (0, 0))
    return pl.pallas_call(
        functools.partial(project_kernel, groups),
        grid_spec=pltpu.PrefetchScalarGridSpec(
            num_scalar_prefetch=1,
            grid=(1,),
            in_specs=[whole, whole]
            + [weight_spec] * 3
            + [pl.BlockSpec((3, width), lambda i, p: (0, p[0])), table, table],
            out_specs=[
                pl.BlockSpec((2 * half, width), lambda i, p: (0, 0)),
                pl.BlockSpec((2 * half, 2 * width), lambda i, p: (0, 0)),
            ],
        ),
        out_shape=[
            jax.ShapeDtypeStruct((2 * half, width), BF16),
            jax.ShapeDtypeStruct((2 * half, 2 * width), BF16),
        ],
        compiler_params=pltpu.CompilerParams(vmem_limit_bytes=48 * 2**20),
        cost_estimate=pl.CostEstimate(
            flops=12 * half * model_width * width,
            bytes_accessed=4 * half * model_width + 6 * model_width * width,
            transcendentals=0,
        ),
        name="project",
    )(place, *halves, *weights, bias, cosine, sines)


def project_back_kernel(
    groups,
    place_ref,
    gq_ref,
    go_ref,
    came_ref,
    wq_ref,
    wk_ref,
    wv_ref,
    cos_ref,
    sin_ref,
    own_ref,
    other_ref,
    own_part,
    other_part,
    bias_ref,
):
    core = place_ref[1]
    half, width = own_ref.shape[0], gq_ref.shape[1]
    rows = half // groups
    columns = min(512, own_part.shape[1])
    bias_sum = jnp.zeros((1, 3 * width), F32)
    for index, (out, part) in enumerate(((own_ref, own_part), (other_ref, other_part))):
        here = slice(index * half, (index + 1) * half)
        cosine, sines = cos_ref[here, :], sin_ref[here, :]
        for k in range(3):
            for h in range(width // HD):
                pieces = []
                for group in range(groups):
                    at_rows = half_rows(index, group, rows, core)
                    if k == 0:
                        pieces.append(gq_ref[at_rows, h * HD : (h + 1) * HD])
                    else:
                        at = (2 * h + k - 1) * HD
                        pieces.append(go_ref[at_rows, at : at + HD] + came_ref[at_rows, at : at + HD].astype(F32))
                values = jnp.concatenate(pieces, axis=0)
                if k < 2:
                    values = turned(values, cosine, -sines)
                out[:, k * width + h * HD : k * width + (h + 1) * HD] = values.astype(BF16)
        grads = out[...]
        bias_sum = bias_sum + jnp.sum(grads.astype(F32), axis=0, keepdims=True)
        for at in range(0, part.shape[1], columns):
            total = dot_nt(grads[:, :width], wq_ref[at : at + columns, :])
            total = total + dot_nt(grads[:, width : 2 * width], wk_ref[at : at + columns, :])
            total = total + dot_nt(grads[:, 2 * width :], wv_ref[at : at + columns, :])
            part[:, at : at + columns] = total.astype(BF16)
    bias_ref[...] = jnp.broadcast_to(bias_sum, bias_ref.shape)


def project_back(place, grad_query, own_kv_grad, came_kv, weights, cosine, sines, groups):
    total, width = grad_query.shape
    half = total // 2
    model_width = weights[0].shape[0]
    weight_spec = pl.BlockSpec((model_width, width), lambda i, p: (0, p[0]))

    def full(*shape):
        return pl.BlockSpec(shape, lambda i, p: (0, 0))

    return pl.pallas_call(
        functools.partial(project_back_kernel, groups),
        grid_spec=pltpu.PrefetchScalarGridSpec(
            num_scalar_prefetch=1,
            grid=(1,),
            in_specs=[full(total, width), full(total, 2 * width), full(total, 2 * width)]
            + [weight_spec] * 3
            + [full(total, HD)] * 2,
            out_specs=[full(half, 3 * width)] * 2 + [full(half, model_width)] * 2 + [full(8, 3 * width)],
        ),
        out_shape=[jax.ShapeDtypeStruct((half, 3 * width), BF16)] * 2
        + [jax.ShapeDtypeStruct((half, model_width), BF16)] * 2
        + [jax.ShapeDtypeStruct((8, 3 * width), F32)],
        compiler_params=pltpu.CompilerParams(vmem_limit_bytes=48 * 2**20),
        cost_estimate=pl.CostEstimate(
            flops=12 * half * model_width * width,
            bytes_accessed=8 * half * model_width + 6 * model_width * width,
            transcendentals=0,
        ),
        name="project_back",
    )(place, grad_query, own_kv_grad, came_kv, *weights, cosine, sines)


def projection_grads_kernel(n0, n1, d0, d1, g0, g1, a0, a1, out_ref):
    width = g0.shape[1]
    out_ref[:, :width] = (dot_tn(n0[...], g0[...]) + dot_tn(n1[...], g1[...])).astype(BF16)
    out_ref[:, width:] = (dot_tn(d0[...], a0[...]) + dot_tn(d1[...], a1[...])).astype(BF16)


def projection_grads(normed, grads_after, grads, attended):
    half, model_width = normed[0].shape
    width = grads[0].shape[1] + attended[0].shape[1]
    tile = min(512, model_width)
    wide = pl.BlockSpec((half, tile), lambda i: (0, i))
    return pl.pallas_call(
        projection_grads_kernel,
        grid=(model_width // tile,),
        in_specs=[wide] * 4
        + [pl.BlockSpec(grads[0].shape, lambda i: (0, 0))] * 2
        + [pl.BlockSpec(attended[0].shape, lambda i: (0, 0))] * 2,
        out_specs=pl.BlockSpec((tile, width), lambda i: (i, 0)),
        out_shape=jax.ShapeDtypeStruct((model_width, width), BF16),
        compiler_params=pltpu.CompilerParams(vmem_limit_bytes=40 * 2**20),
        cost_estimate=pl.CostEstimate(
            flops=4 * half * model_width * width, bytes_accessed=8 * half * model_width, transcendentals=0
        ),
        name="projection_grads",
    )(*normed, *grads_after, *grads, *attended)


def hidden_grads(rows, top, gate, weight_gu, weight_down):
    hidden = weight_down.shape[0]
    both = dot_nt(rows, weight_gu)
    inner_grad = dot_nt(top, weight_down)
    gate_val, up_val = both[:, :hidden], both[:, hidden:]
    sigmoid_val = jax.nn.sigmoid(gate_val)
    silu_val = gate_val * sigmoid_val
    inner = silu_val * up_val
    slope = jnp.sum(inner * inner_grad, axis=-1, keepdims=True)
    inner_grad = inner_grad * gate
    gated = (inner * gate).astype(BF16)
    grad_gate_val = (inner_grad * up_val * (sigmoid_val + silu_val * (1.0 - sigmoid_val))).astype(BF16)
    grad_up_val = (inner_grad * silu_val).astype(BF16)
    return gated, grad_gate_val, grad_up_val, slope


def gate_of(gates, block):
    lane = lax.broadcasted_iota(jnp.int32, gates.shape, 1)
    return jnp.sum(jnp.where(lane == block, gates, 0.0), axis=1, keepdims=True)


def feed_kernel(first_ref, rows_ref, top_ref, gates_ref, gu_ref, down_ref, *refs):
    del first_ref
    gated_ref, grad_ref, slope_ref = refs[-3:]
    hidden = down_ref.shape[0]
    gate = gate_of(gates_ref[...], pl.program_id(0))
    gated, grad_gate_val, grad_up_val, slope = hidden_grads(
        rows_ref[...], top_ref[...], gate, gu_ref[...], down_ref[...]
    )
    gated_ref[...] = gated
    grad_ref[:, :hidden] = grad_gate_val
    grad_ref[:, hidden:] = grad_up_val
    slope_ref[0] = slope


def weight_kernel(
    routed,
    hidden_out,
    chunk_ref,
    rows_ref,
    top_ref,
    rows_t_ref,
    top_t_ref,
    gates_ref,
    gu_ref,
    down_ref,
    gu_in,
    down_in,
    *rest,
):
    del chunk_ref
    sums = rest[-3:]
    gate_sum, up_sum, down_sum = sums
    hidden = down_ref.shape[0]
    step = pl.program_id(0)

    @pl.when(step == 0)
    def _():
        gate_sum[...] = gu_in[:, :hidden]
        up_sum[...] = gu_in[:, hidden:]
        down_sum[...] = down_in[...]

    gate = gate_of(gates_ref[...], routed)
    gated, grad_gate_val, grad_up_val, _ = hidden_grads(
        rows_ref[...], top_ref[...], gate, gu_ref[...], down_ref[...]
    )
    gate_sum[...] += dot(rows_t_ref[...], grad_gate_val)
    up_sum[...] += dot(rows_t_ref[...], grad_up_val)
    down_sum[...] += dot(top_t_ref[...], gated)

    @pl.when(step == pl.num_programs(0) - 1)
    def _():
        if len(rest[-4].shape) == 3:
            for out, total in zip(rest[-6:-3], sums, strict=True):
                out[0] = total[...].T[:hidden_out]
        else:
            out = rest[-4]
            groups, _, part = out.shape[:3]
            for g in range(groups):
                for k, total in enumerate(sums):
                    out[g, k] = total[g * part : (g + 1) * part, :].astype(BF16)


def pack_kernel(local, hidden, units, window_ref, *refs):
    gate_ref, up_ref, down_ref = refs[:3]
    shared_gate, shared_up = refs[3 : 3 + units], refs[3 + units : 3 + 2 * units]
    shared_down = refs[3 + 2 * units : 3 + 3 * units]
    gu_out, down_out = refs[-2:]
    padded = units * LANE
    columns = down_out.shape[1]
    for e in range(local):
        for ref, out, at in ((gate_ref, gu_out, 2 * e), (up_ref, gu_out, 2 * e + 1), (down_ref, down_out, e)):
            out[at * padded : at * padded + hidden, :] = ref[e]
            if hidden < padded:
                out[at * padded + hidden : (at + 1) * padded, :] = jnp.zeros((padded - hidden, columns), BF16)
    skip = window_ref[1]
    for k in range(units):
        line = lax.broadcasted_iota(jnp.int32, (LANE, columns), 0) + k * LANE
        keep = (line >= skip) & (line < skip + hidden)
        for block, out, at in (
            (shared_gate[k][...].T, gu_out, 2 * local),
            (shared_up[k][...].T, gu_out, 2 * local + 1),
            (shared_down[k][...], down_out, local),
        ):
            out[at * padded + k * LANE : at * padded + (k + 1) * LANE, :] = jnp.where(
                keep, block.astype(F32), 0.0
            ).astype(BF16)


def pack_weights(window, expert_gate, expert_up, expert_down, shared_gate, shared_up, shared_down, padded):
    local, hidden, model_width = expert_down.shape
    units = padded // LANE
    blocks = local + 1
    tile = min(256, model_width)
    expert_spec = pl.BlockSpec((local, hidden, tile), lambda i, w: (0, 0, i))
    column_specs = [pl.BlockSpec((tile, LANE), lambda i, w, k=k: (i, w[0] + k)) for k in range(units)]
    row_specs = [pl.BlockSpec((LANE, tile), lambda i, w, k=k: (w[0] + k, i)) for k in range(units)]
    return pl.pallas_call(
        functools.partial(pack_kernel, local, hidden, units),
        grid_spec=pltpu.PrefetchScalarGridSpec(
            num_scalar_prefetch=1,
            grid=(model_width // tile,),
            in_specs=[expert_spec] * 3 + column_specs * 2 + row_specs,
            out_specs=[
                pl.BlockSpec((2 * blocks * padded, tile), lambda i, w: (0, i)),
                pl.BlockSpec((blocks * padded, tile), lambda i, w: (0, i)),
            ],
        ),
        out_shape=[
            jax.ShapeDtypeStruct((2 * blocks * padded, model_width), BF16),
            jax.ShapeDtypeStruct((blocks * padded, model_width), BF16),
        ],
        compiler_params=pltpu.CompilerParams(vmem_limit_bytes=40 * 2**20),
        cost_estimate=pl.CostEstimate(
            flops=0, bytes_accessed=12 * blocks * padded * model_width, transcendentals=0
        ),
        name="pack_weights",
    )(
        window,
        jnp.swapaxes(expert_gate, 1, 2),
        jnp.swapaxes(expert_up, 1, 2),
        expert_down,
        *([shared_gate] * units),
        *([shared_up] * units),
        *([shared_down] * units),
    )


def turn_kernel(plane_ref, part_ref, out_ref):
    del plane_ref
    out_ref[...] = part_ref[...].T


def turn(plane, values, part):
    total = values.shape[0]
    tile = min(1024, total)
    return pl.pallas_call(
        turn_kernel,
        grid_spec=pltpu.PrefetchScalarGridSpec(
            num_scalar_prefetch=1,
            grid=(total // tile,),
            in_specs=[pl.BlockSpec((tile, part), lambda i, p: (i, p[0]))],
            out_specs=pl.BlockSpec((part, tile), lambda i, p: (0, i)),
        ),
        out_shape=jax.ShapeDtypeStruct((part, total), BF16),
        compiler_params=pltpu.CompilerParams(vmem_limit_bytes=40 * 2**20),
        cost_estimate=pl.CostEstimate(flops=0, bytes_accessed=4 * total * part, transcendentals=0),
        name="turn",
    )(plane, values)


def feed(first, index, rows, top_all, gates, weight_gu, weight_down, blocks, outs=None):
    count, model_width = rows.shape
    hidden = weight_down.shape[0] // blocks
    tile = min(FEED_BLOCK, count)
    steps = count // tile
    whole = 2 * count
    in_specs = [
        pl.BlockSpec((tile, model_width), lambda s, i, c: (i, 0)),
        pl.BlockSpec((tile, model_width), lambda s, i, c: (c[0] * steps + i, 0)),
        pl.BlockSpec((tile, gates.shape[1]), lambda s, i, c: (i, 0)),
        pl.BlockSpec((2 * hidden, model_width), lambda s, i, c: (s, 0)),
        pl.BlockSpec((hidden, model_width), lambda s, i, c: (s, 0)),
    ]
    args = [first, rows, top_all, gates, weight_gu, weight_down]
    aliases = {}
    if outs is not None:
        aliases = {len(args) + k: k for k in range(3)}
        in_specs += [pl.BlockSpec(memory_space=pl.ANY)] * 3
        args += list(outs)
    grid_spec = pltpu.PrefetchScalarGridSpec(
        num_scalar_prefetch=1,
        grid=(blocks, steps),
        in_specs=in_specs,
        out_specs=[
            pl.BlockSpec((tile, hidden), lambda s, i, c: (index * steps + i, s)),
            pl.BlockSpec((tile, 2 * hidden), lambda s, i, c: (index * steps + i, s)),
            pl.BlockSpec((1, tile, 1), lambda s, i, c: (s, index * steps + i, 0)),
        ],
    )
    return pl.pallas_call(
        feed_kernel,
        grid_spec=grid_spec,
        out_shape=[
            jax.ShapeDtypeStruct((whole, blocks * hidden), BF16),
            jax.ShapeDtypeStruct((whole, 2 * blocks * hidden), BF16),
            jax.ShapeDtypeStruct((blocks, whole, 1), F32),
        ],
        input_output_aliases=aliases,
        compiler_params=pltpu.CompilerParams(vmem_limit_bytes=56 * 2**20),
        cost_estimate=pl.CostEstimate(
            flops=6 * count * model_width * hidden * blocks,
            bytes_accessed=6 * model_width * hidden * blocks + 4 * count * model_width * blocks,
            transcendentals=count * hidden * blocks,
        ),
        name="feed",
    )(*args)


def weight_grads(plane, planes, block, rows_all, top_all, rows_t, top_t, gates, packed, sums, outs, groups, hidden):
    weight_gu, weight_down = packed
    total, model_width = rows_all.shape
    count = total // planes
    part = rows_t.shape[0]
    padded = sums[1].shape[1]
    tile = min(FEED_BLOCK, count // 2)
    steps = count // tile
    local = outs[0] if isinstance(outs[0], int) else outs[0].shape[0]

    half_steps = max(1, steps // 2)

    def at(i, c):
        place = lax.rem(i, steps)
        half = lax.rem(place // half_steps + c[1], 2)
        return lax.rem(c[0] + 1 + i // steps, planes) * steps + half * half_steps + lax.rem(place, half_steps)

    tokens = pl.BlockSpec((tile, model_width), lambda i, c: (at(i, c), 0))
    turned = pl.BlockSpec((part, tile), lambda i, c: (0, at(i, c)))
    in_specs = [
        tokens,
        tokens,
        turned,
        turned,
        pl.BlockSpec((tile, gates.shape[1]), lambda i, c: (i, 0)),
        pl.BlockSpec((2 * padded, model_width), lambda i, c: (block, 0)),
        pl.BlockSpec((padded, model_width), lambda i, c: (block, 0)),
        pl.BlockSpec((part, 2 * padded), lambda i, c: (0, 0)),
        pl.BlockSpec((part, padded), lambda i, c: (0, 0)),
    ]
    args = [rows_all, top_all, rows_t, top_t, gates, weight_gu, weight_down, *sums]
    aliases = {}
    if block < local:
        out_shape = [jax.ShapeDtypeStruct((local, hidden, part), F32)] * 3
        out_specs = [pl.BlockSpec((1, hidden, part), lambda i, c: (block, 0, 0))] * 3
        if not isinstance(outs[0], int):
            in_specs += [pl.BlockSpec(memory_space=pl.ANY)] * 3
            aliases = {len(args) + 1 + k: k for k in range(3)}
            args += list(outs)
    else:
        out_shape = [jax.ShapeDtypeStruct((groups, 3, part // groups, padded), BF16)]
        out_specs = [pl.BlockSpec(out_shape[0].shape, lambda i, c: (0, 0, 0, 0))]
    return pl.pallas_call(
        functools.partial(weight_kernel, block, hidden),
        grid_spec=pltpu.PrefetchScalarGridSpec(
            num_scalar_prefetch=1,
            grid=((planes - 1) * steps,),
            in_specs=in_specs,
            out_specs=out_specs,
            scratch_shapes=[pltpu.VMEM((part, padded), F32)] * 3,
        ),
        out_shape=out_shape,
        input_output_aliases=aliases,
        compiler_params=pltpu.CompilerParams(vmem_limit_bytes=62 * 2**20),
        cost_estimate=pl.CostEstimate(
            flops=6 * (total - count) * (model_width + part) * padded,
            bytes_accessed=6 * model_width * padded + 4 * total * model_width,
            transcendentals=total * padded,
        ),
        name="weight_grads",
    )(plane, *args)


def per_device(
    tokens,
    segments,
    routes,
    attn_gain,
    query_weight,
    query_bias,
    key_weight,
    key_bias,
    value_weight,
    value_bias,
    out_weight,
    mlp_gain,
    router_weight,
    shared_router,
    shared_gate,
    shared_up,
    shared_down,
    expert_gate,
    expert_up,
    expert_down,
    grad_out,
):
    tok_rows, model_width = tokens.shape
    groups, cores = lax.axis_size("expert"), lax.axis_size("tensor")
    planes = lax.axis_size("dp")
    mine, core, plane = lax.axis_index("expert"), lax.axis_index("tensor"), lax.axis_index("dp")
    rows = tok_rows // cores
    plane_rows = tok_rows * groups
    heads_here = query_weight.shape[1] // HD
    width = query_weight.shape[1] // groups
    heads = width // HD
    local_experts, _, hidden = expert_gate.shape
    expert_count = local_experts * groups
    blocks = local_experts + 1
    gathered = planes <= GATHERED_PLANES
    padded = -(-hidden // LANE) * LANE
    part_rows = model_width // planes

    first_unit = mine * hidden // LANE
    window = jnp.stack([first_unit, mine * hidden - first_unit * LANE]).astype(jnp.int32)
    weight_gu, weight_down = pack_weights(
        window, expert_gate, expert_up, expert_down, shared_gate, shared_up, shared_down, padded
    )

    own_tokens = lax.dynamic_slice(tokens, (core * rows, 0), (rows, model_width))
    inputs = own_tokens.astype(F32)
    gain_one = attn_gain.astype(F32)
    scale_one = lax.rsqrt(jnp.mean(inputs * inputs, axis=-1, keepdims=True) + EPS)
    normed_one = gather_halves((inputs * scale_one * gain_one).astype(BF16), (weight_gu, weight_down))
    grad_top_own = lax.dynamic_slice(grad_out, (core * rows, 0), (rows, model_width))
    top_axes = ("dp", "tensor", "expert") if gathered else ("tensor", "expert")
    grad_top_all = lax.all_gather(grad_top_own, top_axes, axis=0, tiled=True)

    picks = jnp.sum(1 << routes, axis=1)
    facts_own = jnp.zeros((FACT_ROWS, tok_rows), BF16)
    facts_own = facts_own.at[0].set(segments.astype(BF16)).at[1].set(picks.astype(BF16))
    facts = jnp.zeros((groups, FACT_ROWS, tok_rows), BF16)
    facts = lax.dynamic_update_slice(facts, facts_own[None], (mine, 0, 0))
    for step in range(1, groups):
        came = lax.ppermute(facts_own, "expert", shift_pairs(groups, step))
        facts = lax.dynamic_update_slice(facts, came[None], (source(mine, groups, step), 0, 0))
    facts = facts.transpose(1, 0, 2).reshape(FACT_ROWS, plane_rows)
    upward = [(i, i + 1) for i in range(planes - 1)]
    seg_own = facts[:1].astype(F32)
    seg_before = jnp.where(plane > 0, lax.ppermute(facts, "dp", upward)[:1].astype(F32), -1.0)
    seg_rows = seg_own.reshape(plane_rows, 1)
    bits = jnp.concatenate(half_order(facts[1].reshape(plane_rows, 1), groups), axis=0).astype(jnp.int32)

    half = plane_rows // 2
    slot = jnp.arange(plane_rows, dtype=jnp.int32)
    half_core = (core + slot // half) % 2
    row_index = plane * plane_rows + slot % half // rows * tok_rows + half_core * rows + slot % rows
    places = (row_index % SEQ_LEN).astype(F32)
    frequency = THETA ** (-2.0 * jnp.arange(HD // 2, dtype=F32) / HD)
    angles = places[:, None] * jnp.concatenate([frequency, frequency])[None, :]
    cosine = jnp.cos(angles)
    sines = jnp.sin(angles) * jnp.where(jnp.arange(HD) < HD // 2, -1.0, 1.0)[None, :]
    place = jnp.stack([mine, core]).astype(jnp.int32)
    weights_in = (query_weight, key_weight, value_weight)
    bias_in = jnp.stack([bias.reshape(-1) for bias in (query_bias, key_bias, value_bias)])
    query_rot, own_kv = project(place, normed_one, weights_in, bias_in, cosine, sines, groups)
    before_kv = lax.ppermute(own_kv, "dp", upward)
    attended = half_order(attend(query_rot, before_kv, own_kv, seg_rows, seg_before, seg_own), groups)
    out_rows = lax.dynamic_slice(out_weight, (mine * width, 0), (width, model_width))
    after_attn = inputs + scatter_halves(*(dot(half, out_rows) for half in attended))

    gain_two = mlp_gain.astype(F32)
    scale_two = lax.rsqrt(jnp.mean(after_attn * after_attn, axis=-1, keepdims=True) + EPS)
    normed_own = (after_attn * scale_two * gain_two).astype(BF16)
    normed_two = gather_halves(normed_own)
    if gathered:
        normed_all = lax.all_gather(after(normed_own, normed_two[0]), ("dp", "tensor", "expert"), axis=0, tiled=True)
    gate_columns = jnp.concatenate([router_weight, shared_router[:, None]], axis=1)
    first_tile = 2 * plane if gathered else jnp.zeros_like(plane)
    outs, half_gates, half_probs = None, [], []
    for index in range(2):
        logits = dot(normed_two[index], gate_columns)
        chosen = (
            (bits[index * half : (index + 1) * half] >> jnp.arange(expert_count, dtype=jnp.int32)[None, :]) & 1
        ).astype(F32)
        probs = jax.nn.softmax(logits[:, :expert_count], axis=-1)
        named = lax.dynamic_slice(probs * chosen, (0, mine * local_experts), (half, local_experts))
        half_gates.append(jnp.concatenate([named, jax.nn.sigmoid(logits[:, expert_count:])], axis=1))
        half_probs.append((probs, chosen))
        first = (first_tile + (core + index) % 2).reshape(1).astype(jnp.int32)
        outs = feed(
            first, index, normed_two[index], grad_top_all, half_gates[index], weight_gu, weight_down, blocks, outs
        )
    gated, grad_hidden, slopes = outs
    gates = jnp.concatenate(half_gates, axis=0)
    router_probs, chosen = (jnp.concatenate(parts, axis=0) for parts in zip(*half_probs, strict=True))

    shared_mix = gates[:, local_experts:]
    own_slopes = jnp.concatenate([slopes[e] for e in range(local_experts)], axis=1)
    all_slopes = lax.dynamic_update_slice(
        jnp.zeros((plane_rows, expert_count), F32), own_slopes, (0, mine * local_experts)
    ) * chosen
    grad_logits = router_probs * (all_slopes - jnp.sum(router_probs * all_slopes, axis=-1, keepdims=True))
    grad_shared_logit = slopes[local_experts] * shared_mix * (1.0 - shared_mix)
    grad_small = jnp.concatenate([grad_logits, grad_shared_logit], axis=1).astype(BF16)
    grad_normed_part = (dot(grad_hidden, weight_gu) + dot_nt(grad_small, gate_columns)).astype(BF16)
    own_part = jnp.concatenate(
        [lax.dynamic_slice(part, (0, plane * part_rows), (half, part_rows)) for part in normed_two], axis=0
    )

    def mix_meanwhile(token):
        values, grads = after((gated, grad_hidden), token)
        in_order = [lax.dynamic_slice(values, ((core + k) % 2 * half, 0), (half, values.shape[1])) for k in range(2)]
        mixed_part = dot(jnp.concatenate(in_order, axis=0), weight_down).astype(BF16)
        first_sums = [dot_tn(own_part, block_grads(grads, b)) for b in range(1, blocks)] if gathered else []
        return mixed_part, first_sums

    def block_grads(grads, block):
        return grads[:, 2 * block * padded : 2 * (block + 1) * padded]

    grad_normed_two, (mixed_part, first_sums) = scatter_halves(
        grad_normed_part[:half], grad_normed_part[half:], mix_meanwhile
    )
    mixed = lax.psum_scatter(
        after(mixed_part, grad_normed_two), ("tensor", "expert"), scatter_dimension=0, tiled=True
    )
    out = both_cores((after_attn + mixed.astype(F32)).astype(BF16))
    grad_columns = functools.reduce(
        jnp.add, [dot_tn(normed_two[k], grad_small[k * half : (k + 1) * half]) for k in range(2)]
    )

    grad_mlp_gain = jnp.sum(grad_normed_two * after_attn * scale_two, axis=0)
    grad_after = grad_top_own.astype(F32) + norm_back(after_attn, scale_two, gain_two, grad_normed_two)

    plane_number = jnp.stack([plane, core]).astype(jnp.int32)
    grad_sent = grad_after.astype(BF16)
    values, grads, top_all = after((gated, grad_hidden, grad_top_all), grad_sent)
    own_sums = []
    if gathered:
        top_t = turn(plane_number, top_all, part_rows)
        own_top_t = jnp.concatenate(
            [
                lax.dynamic_slice(top_t, (0, (2 * plane + (core + k) % 2) * half), (part_rows, half))
                for k in range(2)
            ],
            axis=1,
        )
        first_sums = [dot_tn(own_part, block_grads(grads, 0)), *first_sums]
        own_sums = [
            (first_sums[b], dot(own_top_t, values[:, b * padded : (b + 1) * padded])) for b in range(blocks)
        ]
    grad_attended = gather_halves(grad_sent, tuple(own_sums))
    grad_heads = token_order(*(dot_nt(part, out_rows).astype(BF16) for part in grad_attended), groups)
    grad_query_rot, back_kv, own_kv_grad = attend_back(
        query_rot, before_kv, own_kv, seg_rows, seg_before, seg_own, grad_heads
    )

    small_rows = part_rows // groups

    def to_owners(values):
        return lax.all_to_all(values, "expert", 0, 0)

    def placed(pieces):
        total = None
        for j in range(groups):
            at = j * hidden // LANE * LANE
            piece = jnp.pad(pieces[j].astype(F32), [(0, 0), (at, groups * hidden - at - padded)])
            total = piece if total is None else total + piece
        return total

    if gathered:
        gates_sent = after(
            jnp.pad(gates.T, [(0, -gates.shape[1] % 8), (0, 0)]), back_kv
        )
        gates_came = [
            lax.ppermute(gates_sent, "dp", [((i + step) % planes, i) for i in range(planes)])
            for step in range(1, planes)
        ]
        normed_all = after(normed_all, back_kv)
        rows_t = turn(plane_number, normed_all, part_rows)
        gates_all = jnp.concatenate(gates_came, axis=1).T

        def weight_sums(block, outs, *tokens):
            return weight_grads(
                plane_number,
                planes,
                block,
                after(normed_all, *tokens),
                grad_top_all,
                rows_t,
                top_t,
                gates_all,
                (weight_gu, weight_down),
                own_sums[block],
                outs,
                groups,
                hidden,
            )

        shared_grads = weight_sums(local_experts, (local_experts,), back_kv)[0]
        shared_grads_token = shared_grads
    else:
        top_half = grad_top_all.reshape(2, half, model_width)
        top_here = jnp.concatenate(
            [lax.dynamic_slice(top_half, ((core + k) % 2, 0, 0), (1, half, model_width))[0] for k in range(2)], axis=0
        )
        gu_part = lax.psum_scatter(
            dot_tn(jnp.concatenate(normed_two, axis=0), grad_hidden).astype(BF16),
            "dp",
            scatter_dimension=0,
            tiled=True,
        )
        down_part = lax.psum_scatter(dot_tn(top_here, gated).astype(BF16), "dp", scatter_dimension=0, tiled=True)

        def block_of(values, index, size):
            return values[:, index * padded : index * padded + size]

        shared_grads = jnp.stack(
            [
                block_of(values, index, padded).reshape(groups, small_rows, padded)
                for values, index in (
                    (gu_part, 2 * local_experts),
                    (gu_part, 2 * local_experts + 1),
                    (down_part, local_experts),
                )
            ],
            axis=1,
        )
    shared_grads = to_owners(shared_grads)
    came_kv = lax.ppermute(back_kv, "dp", [(i + 1, i) for i in range(planes - 1)])
    if gathered:
        came_kv = after(came_kv, shared_grads_token)
    *grad_qkv, own_one_part, other_one_part, bias_sums = project_back(
        place, grad_query_rot, own_kv_grad, came_kv, weights_in, cosine, sines, groups
    )
    grad_part = projection_grads(normed_one, grad_attended, grad_qkv, attended)
    weight_sum = lax.psum_scatter(grad_part, "dp", scatter_dimension=0, tiled=True)
    weight_sum = weight_sum.reshape(groups, small_rows, 4, width)
    if gathered:
        expert_grads = (local_experts,)
        for e in range(local_experts - 2):
            expert_grads = weight_sums(e, expert_grads, grad_part)
        grad_normed_one, expert_grads = scatter_halves(
            own_one_part,
            other_one_part,
            lambda token: weight_sums(local_experts - 2, expert_grads, token, grad_part),
        )
        shared_grads = after(shared_grads, expert_grads)
    else:
        grad_normed_one = scatter_halves(own_one_part, other_one_part)
    grad_shared_gate = placed(shared_grads[:, 0])
    grad_shared_up = placed(shared_grads[:, 1])
    grad_shared_down = placed(shared_grads[:, 2]).T
    grad_attn_gain = jnp.sum(grad_normed_one * inputs * scale_one, axis=0)
    grad_own = grad_after + norm_back(inputs, scale_one, gain_one, grad_normed_one)
    if gathered:
        expert_grads = weight_sums(local_experts - 1, expert_grads, grad_own, weight_sum)
    else:
        expert_grads = [
            jnp.stack([block_of(values, first + stride * e, hidden).T for e in range(local_experts)]).astype(F32)
            for values, first, stride in ((gu_part, 0, 2), (gu_part, 1, 2), (down_part, 0, 1))
        ]
    grad_expert_gate, grad_expert_up = (jnp.swapaxes(grad, 1, 2) for grad in expert_grads[:2])
    grad_expert_down = expert_grads[2]
    grad_tokens = both_cores(grad_own)

    weight_rows = (
        to_owners(weight_sum).transpose(2, 1, 0, 3).reshape(4, small_rows, groups * width).astype(F32)
    )
    qkv_rows = weight_rows[:3]
    grad_out_weight = weight_rows[3].T

    bias_sums = bias_sums[0].reshape(1, 3, heads, HD)
    bias_table = lax.dynamic_update_slice(
        jnp.zeros((cores, 3, heads_here, HD), F32), bias_sums, (core, 0, mine * heads, 0)
    )
    devices = planes * groups
    spread = jnp.concatenate(
        [
            grad_attn_gain.reshape(devices, -1),
            grad_mlp_gain.reshape(devices, -1),
            grad_columns.reshape(devices, -1),
            bias_table.reshape(cores * 3 * heads_here, devices, HD // devices).transpose(1, 0, 2).reshape(devices, -1),
        ],
        axis=1,
    )
    sums = jnp.sum(lax.all_to_all(spread, ("dp", "expert"), 0, 0, tiled=True), axis=0, keepdims=True)
    sums = lax.psum(sums, "tensor")[0] if cores != 2 else (sums + lax.ppermute(sums, "tensor", [(0, 1), (1, 0)]))[0]
    gain_part = model_width // devices
    grad_attn_gain, grad_mlp_gain = sums[:gain_part], sums[gain_part : 2 * gain_part]
    table = sums[2 * gain_part :]
    column_size = gain_part * (expert_count + 1)
    column_sums = table[:column_size].reshape(gain_part, expert_count + 1)
    bias_sums = table[column_size:].reshape(cores, 3, heads_here, HD // devices)
    bias_sums = lax.dynamic_slice(bias_sums, (core, 0, 0, 0), (1, 3, heads_here, HD // devices))[0]
    return (
        out,
        grad_tokens,
        grad_attn_gain,
        qkv_rows[0],
        bias_sums[0],
        qkv_rows[1],
        bias_sums[1],
        qkv_rows[2],
        bias_sums[2],
        grad_out_weight,
        grad_mlp_gain,
        column_sums[:, :expert_count],
        column_sums[:, expert_count],
        grad_shared_gate,
        grad_shared_up,
        grad_shared_down,
        grad_expert_gate,
        grad_expert_up,
        grad_expert_down,
    )


def solution(mesh):
    tokens = ("dp", "expert")
    return jax.shard_map(
        per_device,
        mesh=mesh,
        in_specs=(
            P(tokens, None),
            P(tokens),
            P(tokens, None),
            P(),
            P(None, "tensor"),
            P("tensor", None),
            P(None, "tensor"),
            P("tensor", None),
            P(None, "tensor"),
            P("tensor", None),
            P("tensor", None),
            P(),
            P(),
            P(),
            P(None, "tensor"),
            P(None, "tensor"),
            P("tensor", None),
            P("expert", None, "tensor"),
            P("expert", None, "tensor"),
            P("expert", "tensor", None),
            P(tokens, None),
        ),
        out_specs=(
            P(tokens, None),
            P(tokens, None),
            P(tokens),
            P(tokens, "tensor"),
            P("tensor", tokens),
            P(tokens, "tensor"),
            P("tensor", tokens),
            P(tokens, "tensor"),
            P("tensor", tokens),
            P("tensor", tokens),
            P(tokens),
            P(tokens, None),
            P(tokens),
            P(tokens, "tensor"),
            P(tokens, "tensor"),
            P("tensor", tokens),
            P("expert", "dp", "tensor"),
            P("expert", "dp", "tensor"),
            P("expert", "tensor", "dp"),
        ),
        check_vma=False,
    )
```

time: 687 us -> 646 us (0.940)
  other arithmetic: 61.9 us -> 31.9 us
  Pallas kernels: 252 us -> 277 us
  waiting for transfers between devices: 128 us -> 113 us
  matrix products: 86.3 us -> 73.3 us
  local copies, waits for them, and re-layouts: 79.3 us -> 68.7 us
    ppermute x30 -> x31, waiting for transfers between devices: 119 us -> 103 us  [the longest x9 32.2 us: gather_halves(): came = lax.ppermute(own, 'expert', shift_pairs(groups, step))]
    pallas_call x2 -> x5, Pallas kernels: 18.4 us -> 33.4 us  [the longest x2 9.3 us: turn(): pl.pallas_call(turn_kernel, grid_spec=pltpu.PrefetchScalarGridSpec(num_sc...]
    concatenate x15 -> x6, other arithmetic: 13.5 us -> 2.61 us  [the longest x3 2.58 us: joined(): jnp.concatenate([jnp.where(core == 0, own, other), jnp.where(core == 0, o...]
    ppermute x30 -> x31, starting transfers between devices: 28.6 us -> 38.1 us  [the longest x9 8.79 us: gather_halves(): came = lax.ppermute(own, 'expert', shift_pairs(groups, step))]
    dot_general x10 -> x9, matrix products: 55.3 us -> 47.4 us  [dot(): return jnp.dot(left, right, preferred_element_type=F32)]
    select_n x6 -> x4, other arithmetic: 9.8 us -> 2.56 us  [the longest x2 2.48 us: joined(): jnp.where(core == 0, own, other)]
    pallas_call x1 -> x2, Pallas kernels: 40.7 us -> 47 us  [feed(): pl.pallas_call(feed_kernel, grid_spec=grid_spec, out_shape=[jax.ShapeDtyp...]
    unnamed x178 -> x134, local copies, waits for them, and re-layouts: 34.2 us -> 29.1 us
  transfers between devices with their start and end apart: 43 -> 43, of which waited for: 20 -> 19; matrix products, arithmetic and copies ran while one was open for 28% -> 22% of each run, Pallas kernels for 37% -> 43%
where the time goes in v3:
time: 646 us; the launch traced here: 638 us
  Pallas kernels  277 us (43%)
  waiting for transfers between devices  113 us (17%)
  matrix products  73.3 us (11%)
  local copies, waits for them, and re-layouts  68.7 us (11%)
  starting transfers between devices  58.6 us (9%)
  other arithmetic  31.9 us (5%)
  between operations  15.5 us (2%)
    pallas_call x3, Pallas kernels, weight_grads(): pl.pallas_call(functools.partial(weight_kernel, block, hidden), grid_spec...  157 us
    dot_general x9, matrix products, dot(): return jnp.dot(left, right, preferred_element_type=F32)  47.4 us
    pallas_call x2, Pallas kernels, feed(): pl.pallas_call(feed_kernel, grid_spec=grid_spec, out_shape=[jax.ShapeDtyp...  47 us
    ppermute x9, waiting for transfers between devices, gather_halves(): came = lax.ppermute(own, 'expert', shift_pairs(groups, step))  32.2 us
    ppermute x1, waiting for transfers between devices, per_device(): lax.ppermute(facts, 'dp', upward)[:1].astype(F32)  29.9 us
    unnamed x134, local copies, waits for them, and re-layouts  29.1 us
    ppermute x9, waiting for transfers between devices, scatter_halves(): lax.ppermute(sent[step - 1], 'expert', shift_pairs(groups, step))  27.3 us
    dot_general x5, matrix products, dot_tn(): lax.dot_general(left, right, (((0,), (0,)), ((), ())), preferred_element_...  20.1 us
  transfers between devices with their start and end apart: 43, of which 19 were waited for; matrix products, arithmetic and copies ran while one was open for 22% of the time, Pallas kernels for 43%

profile of v3, /device:TPU:1, one launch (start us, length us, event | category | flops | bytes accessed | tf_op | source)
XLA Modules:
  0.0 637.8 jit_solution(3534384266098585554)
XLA Ops:
  12.7 3.1 collective-permute-start.2
  16.2 2.6 copy-done.3
  18.8 2.6 copy-done.4
  21.4 17.6 %pack_weights.1 = (bf16[4608,2048]{1,0:T(8,128)(2,1)}, bf16[2304,2048]{1,0:T(8,128)(2,1)}) custom-call(s32[2]{0:T(128)S(1)} %pad_add_fusion.1.window_ref, bf16[2,704,2048]{2,1,0:T(8,128)(2,1)S(1)} %bitcast.134, bf16[2,704,2048]{2,1,0:T(8,128)(2,1)S(1)} %bitcast.135, bf16[2,704,2048]{2,1,0:T(8,128)(2,1)} %refs_2_.1, bf16[2048,2816]{1,0:T(8,128)(2,1)} %refs_8_.1, ...), custom_call_target="tpu_custom_call" | custom-call | bytes 56623104 | tf_op jit(solution)/shard_map/pack_weights/pallas_call | solution.py:539
  39.0 4.2 collective-permute-done.1
  50.2 7.6 %project.1 = (bf16[1024,256]{1,0:T(8,128)(2,1)S(1)}, bf16[1024,512]{1,0:T(8,128)(2,1)}) custom-call(s32[2]{0:T(128)S(1)} %pad_add_fusion.place_ref, bf16[512,2048]{1,0:T(8,128)(2,1)S(1)} %constant_dynamic-update-slice_fusion.10.own_ref.n0, bf16[512,2048]{1,0:T(8,128)(2,1)} %collective-permute-done.3.other_ref.n1, bf16[2048,1024]{1,0:T(8,128)(2,1)} %wq_ref.3, ...), custom_call_target="tpu_custom_call" | custom-call | flops 3221225472 | bytes 7340032 | tf_op jit(solution)/shard_map/project/pallas_call | solution.py:287
  57.8 3.3 collective-permute-start.4
  67.3 3.6 collective-permute-start.8
  71.1 29.9 %collective-permute-done.8 = bf16[16,1024]{1,0:T(8,128)(2,1)S(1)} collective-permute-done((bf16[16,1024]{1,0:T(8,128)(2,1)S(1)}, bf16[16,1024]{1,0:T(8,128)(2,1)S(1)}, u32[]{:S(2)}, u32[]{:S(2)}) %collective-permute-start.8) | collective-permute-done | bytes 32800 | tf_op jit(solution)/shard_map/ppermute | solution.py:769
  101.0 8.2 %attend.1 = bf16[1024,256]{1,0:T(8,128)(2,1)S(1)} custom-call(bf16[1024,256]{1,0:T(8,128)(2,1)S(1)} %get-tuple-element.101.q_ref, bf16[1024,512]{1,0:T(8,128)(2,1)S(1)} %collective-permute-done.4.before_ref, bf16[1024,512]{1,0:T(8,128)(2,1)} %get-tuple-element.102.own_ref, f32[1024,1]{1,0:T(8,128)S(1)} %bitcast.141, ...), custom_call_target="tpu_custom_call" | custom-call | flops 1073741824 | bytes 3145728 | tf_op jit(solution)/shard_map/attend/pallas_call | solution.py:214
  111.0 3.8 collective-permute-done.9
  118.6 15.2 %collective-permute-done.10 = bf16[128,2048]{1,0:T(8,128)(2,1)S(1)} collective-permute-done((bf16[128,2048]{1,0:T(8,128)(2,1)S(1)}, bf16[128,2048]{1,0:T(8,128)(2,1)S(1)}, u32[]{:S(2)}, u32[]{:S(2)}) %collective-permute-start.10) | collective-permute-done | bytes 524320 | tf_op jit(solution)/shard_map/ppermute | solution.py:80
  133.9 12.0 %collective-permute-done.12 = bf16[128,2048]{1,0:T(8,128)(2,1)S(1)} collective-permute-done((bf16[128,2048]{1,0:T(8,128)(2,1)S(1)}, bf16[128,2048]{1,0:T(8,128)(2,1)S(1)}, u32[]{:S(2)}, u32[]{:S(2)}) %collective-permute-start.12) | collective-permute-done | bytes 524320 | tf_op jit(solution)/shard_map/ppermute | solution.py:80
  151.7 11.1 %collective-permute-done.15 = bf16[128,2048]{1,0:T(8,128)(2,1)S(1)} collective-permute-done((bf16[128,2048]{1,0:T(8,128)(2,1)S(1)}, bf16[128,2048]{1,0:T(8,128)(2,1)S(1)}, u32[]{:S(2)}, u32[]{:S(2)}) %collective-permute-start.15) | collective-permute-done | bytes 524320 | tf_op jit(solution)/shard_map/ppermute | solution.py:61
  162.8 10.5 %collective-permute-done.14 = bf16[128,2048]{1,0:T(8,128)(2,1)S(1)} collective-permute-done((bf16[128,2048]{1,0:T(8,128)(2,1)S(1)}, bf16[128,2048]{1,0:T(8,128)(2,1)S(1)}, u32[]{:S(2)}, u32[]{:S(2)}) %collective-permute-start.14) | collective-permute-done | bytes 524320 | tf_op jit(solution)/shard_map/ppermute | solution.py:61
  184.9 23.7 %feed.2 = (bf16[1024,2304]{1,0:T(8,128)(2,1)}, bf16[1024,4608]{1,0:T(8,128)(2,1)}, f32[3,1024,1]{2,1,0:T(8,128)}) custom-call(s32[1]{0:T(128)} %bitcast.18.first_ref, bf16[512,2048]{1,0:T(8,128)(2,1)} %constant_dynamic-update-slice_fusion.6.rows_ref, bf16[4096,2048]{1,0:T(8,128)(2,1)} %all-gather.3.cloned.1.call-done.top_ref.part_ref, ...), custom_call_target="tpu_custom_call" | custom-call | flops 14495514624 | bytes 40894464 | tf_op jit(solution)/shard_map/feed/pallas_call | solution.py:622
  208.6 23.3 %feed.3 = (bf16[1024,2304]{1,0:T(8,128)(2,1)}, bf16[1024,4608]{1,0:T(8,128)(2,1)}, f32[3,1024,1]{2,1,0:T(8,128)}) custom-call(s32[1]{0:T(128)} %bitcast.14.first_ref, bf16[512,2048]{1,0:T(8,128)(2,1)} %collective-permute-done.16.rows_ref, ...), custom_call_target="tpu_custom_call", output_to_operand_aliasing={{0}: (6, {}), {1}: (7, {}), {2}: (8, {})} | custom-call | flops 14495514624 | bytes 40894464 | tf_op jit(solution)/shard_map/feed/pallas_call | solution.py:622
  235.1 2.4 copy-done.25
  237.5 22.6 %add_convert_fusion = bf16[1024,2048]{1,0:T(8,128)(2,1)S(1)} fusion(f32[1024,2048]{1,0:T(8,128)S(1)} %fusion.35, bf16[1024,4608]{1,0:T(8,128)(2,1)S(1)} %copy-done.25, bf16[4608,2048]{1,0:T(8,128)(2,1)} %get-tuple-element.96.gu_ref), kind=kOutput, calls=%fused_computation | convolution fusion | flops 19331547136 | bytes 40894464 | tf_op jit(solution)/shard_map/dot_general | solution.py:26
  267.4 3.2 convert_add_fusion.1
  277.7 12.2 %fusion.4 = bf16[1024,2048]{1,0:T(8,128)(2,1)} fusion(bf16[2304,2048]{1,0:T(8,128)(2,1)S(1)} %bitcast.152, bf16[512,2304]{1,0:T(8,128)(2,1)S(1)} %get-tuple-element.262, bf16[512,2304]{1,0:T(8,128)(2,1)S(1)} %get-tuple-element.261), kind=kOutput, calls=%fused_computation.8 | convolution fusion | flops 9675210752 | bytes 18350080 | tf_op jit(solution)/shard_map/dot_general | solution.py:26
  289.9 5.4 fusion.9.gu_in
  295.4 5.4 fusion.11.gu_in
  300.8 2.3 multiply_reduce_fusion
  308.1 4.8 turn.2.top_t_ref
  313.0 2.4 fusion.13.down_in
  319.7 5.3 fusion.7.gu_in
  325.0 6.4 %collective-permute-done.23 = bf16[128,2048]{1,0:T(8,128)(2,1)S(1)} collective-permute-done((bf16[128,2048]{1,0:T(8,128)(2,1)S(1)}, bf16[128,2048]{1,0:T(8,128)(2,1)S(1)}, u32[]{:S(2)}, u32[]{:S(2)}) %collective-permute-start.23) | collective-permute-done | bytes 524320 | tf_op jit(solution)/shard_map/ppermute | solution.py:61
  332.4 3.9 collective-permute-done.25.d1
  336.3 2.6 convolution_convert_fusion.1
  342.1 13.7 %attend_back.1 = (f32[1024,256]{1,0:T(8,128)S(1)}, bf16[1024,512]{1,0:T(8,128)(2,1)}, f32[1024,512]{1,0:T(8,128)}) custom-call(bf16[1024,256]{1,0:T(8,128)(2,1)S(1)} %get-tuple-element.101.q_ref, bf16[1024,512]{1,0:T(8,128)(2,1)S(1)} %copy-done.22, bf16[1024,512]{1,0:T(8,128)(2,1)} %get-tuple-element.102.own_ref, f32[1024,1]{1,0:T(8,128)S(1)} %bitcast.142, ...), custom_call_target="tpu_custom_call" | custom-call | flops 2684354560 | bytes 8388608 | tf_op jit(solution)/shard_map/attend_back/pallas_call | solution.py:232
  356.8 6.4 collective-permute-start.27
  369.4 4.5 turn.3.rows_t_ref
  375.9 51.7 %weight_grads.3 = bf16[4,3,128,768]{3,2,1,0:T(8,128)(2,1)} custom-call(s32[2]{0:T(128)} %copy-done.20, bf16[4096,2048]{1,0:T(8,128)(2,1)} %all-gather.5.cloned.1.call-done.part_ref.rows_ref, bf16[4096,2048]{1,0:T(8,128)(2,1)} %all-gather.3.cloned.1.call-done.top_ref.part_ref, bf16[512,4096]{1,0:T(8,128)(2,1)} %copy-done.9, bf16[512,4096]{1,0:T(8,128)(2,1)} %copy-done.2, ...), custom_call_target="tpu_custom_call" | custom-call | flops 36238786560 | bytes 42991616 | tf_op jit(solution)/shard_map/weight_grads/pallas_call | solution.py:683
  428.9 8.5 %project_back.1 = (bf16[512,768]{1,0:T(8,128)(2,1)S(1)}, bf16[512,768]{1,0:T(8,128)(2,1)S(1)}, bf16[512,2048]{1,0:T(8,128)(2,1)}, bf16[512,2048]{1,0:T(8,128)(2,1)}, f32[8,768]{1,0:T(8,128)S(1)}) custom-call(s32[2]{0:T(128)S(1)} %copy-done.19, f32[1024,256]{1,0:T(8,128)S(1)} %copy-done.17, f32[1024,512]{1,0:T(8,128)} %get-tuple-element.125.go_ref, ...), custom_call_target="tpu_custom_call" | custom-call | flops 3221225472 | bytes 11534336 | tf_op jit(solution)/shard_map/project_back/pallas_call | solution.py:372
  444.8 4.7 all-to-all-start.2
  456.1 8.0 %projection_grads.1 = bf16[2048,1024]{1,0:T(8,128)(2,1)} custom-call(bf16[512,2048]{1,0:T(8,128)(2,1)S(1)} %copy-done.1, bf16[512,2048]{1,0:T(8,128)(2,1)} %collective-permute-done.3.other_ref.n1, bf16[512,2048]{1,0:T(8,128)(2,1)S(1)} %copy-done.11, bf16[512,2048]{1,0:T(8,128)(2,1)} %collective-permute-done.25.d1, ...), custom_call_target="tpu_custom_call" | custom-call | flops 4294967296 | bytes 8388608 | tf_op jit(solution)/shard_map/projection_grads/pallas_call | solution.py:406
  465.7 4.3 convert_add_fusion
  470.0 3.3 dynamic-slice_convert_fusion
  476.0 52.8 %weight_grads.4 = (f32[2,704,512]{2,1,0:T(8,128)}, f32[2,704,512]{2,1,0:T(8,128)}, f32[2,704,512]{2,1,0:T(8,128)}) custom-call(s32[2]{0:T(128)} %copy-done.20, bf16[4096,2048]{1,0:T(8,128)(2,1)} %all-gather.5.cloned.1.call-done.part_ref.rows_ref, bf16[4096,2048]{1,0:T(8,128)(2,1)} %all-gather.3.cloned.1.call-done.top_ref.part_ref, ...), custom_call_target="tpu_custom_call" | custom-call | flops 36238786560 | bytes 42991616 | tf_op jit(solution)/shard_map/weight_grads/pallas_call | solution.py:683
  534.8 3.2 fusion.29
  538.8 5.5 all-to-all-start
  544.3 6.5 %all-to-all-done = f32[16,1,1792]{2,1,0:T(1,128)S(1)} async-done(((f32[16,1,1792]{2,1,0:T(1,128)}), f32[16,1,1792]{2,1,0:T(1,128)S(1)}, u32[]{:S(2)}, u32[]{:S(2)}) %all-to-all-start) | async-done | bytes 114720 | tf_op jit(solution)/shard_map/all_to_all | solution.py:1006
  550.9 2.5 collective-permute-start.35
  553.5 3.3 fusion.25
  565.4 2.6 reshape.405
  568.1 3.5 all-to-all-start.1
  571.6 52.7 %weight_grads.5 = (f32[2,704,512]{2,1,0:T(8,128)}, f32[2,704,512]{2,1,0:T(8,128)}, f32[2,704,512]{2,1,0:T(8,128)}) custom-call(s32[2]{0:T(128)} %copy-done.20, bf16[4096,2048]{1,0:T(8,128)(2,1)} %all-gather.5.cloned.1.call-done.part_ref.rows_ref, ...), custom_call_target="tpu_custom_call", output_to_operand_aliasing={{0}: (10, {}), {1}: (11, {}), {2}: (12, {})} | custom-call | flops 36238786560 | bytes 42991616 | tf_op jit(solution)/shard_map/weight_grads/pallas_call | solution.py:683
  (341 shorter events, 123.4 us)
Async XLA Ops:
  7.2 177.7 %all-gather.3.cloned.1.call-start = ((), (), s32[]{:S(2)}) async-start(), calls=%async_computation.5 | async-start | bytes 17301504 | tf_op jit(solution)/shard_map/all_gather | solution.py:756
  9.2 360.2 %all-gather.5.cloned.1.call-start = ((), (), s32[]{:S(2)}) async-start(), calls=%async_computation.7 | async-start | bytes 17301504 | tf_op jit(solution)/shard_map/all_gather | solution.py:796
  12.7 26.4 %collective-permute-start.2 = (bf16[128,2048]{1,0:T(8,128)(2,1)S(1)}, bf16[128,2048]{1,0:T(8,128)(2,1)S(1)}, u32[]{:S(2)}, u32[]{:S(2)}) collective-permute-start(bf16[128,2048]{1,0:T(8,128)(2,1)S(1)} %get-tuple-element.260), channel_id=1, source_target_pairs={{0,6},{2,4},{4,2},{6,0},{1,7},{3,5},{5,3},{7,1},{8,14},{10,12},{12... | collective-permute-start | bytes 1572872 | tf_op jit(solution)/shard_map/ppermute | solution.py:61
  15.7 27.5 %collective-permute-start.1 = (bf16[128,2048]{1,0:T(8,128)(2,1)S(1)}, bf16[128,2048]{1,0:T(8,128)(2,1)}, u32[]{:S(2)}, u32[]{:S(2)}) collective-permute-start(bf16[128,2048]{1,0:T(8,128)(2,1)S(1)} %get-tuple-element.260), channel_id=1, source_target_pairs={{0,4},{2,6},{4,0},{6,2},{1,5},{3,7},{5,1},{7,3},{8,12},{10,14},{12... | collective-permute-start | bytes 1572872 | tf_op jit(solution)/shard_map/ppermute | solution.py:61
  15.9 27.3 %collective-permute-start = (bf16[128,2048]{1,0:T(8,128)(2,1)S(1)}, bf16[128,2048]{1,0:T(8,128)(2,1)}, u32[]{:S(2)}, u32[]{:S(2)}) collective-permute-start(bf16[128,2048]{1,0:T(8,128)(2,1)S(1)} %get-tuple-element.260), channel_id=1, source_target_pairs={{0,2},{2,0},{4,6},{6,4},{1,3},{3,1},{5,7},{7,5},{8,10},{10,8},{12,... | collective-permute-start | bytes 1572872 | tf_op jit(solution)/shard_map/ppermute | solution.py:61
  45.4 4.8 collective-permute-start.3
  57.8 43.2 %collective-permute-start.4 = (bf16[1024,512]{1,0:T(8,128)(2,1)}, bf16[1024,512]{1,0:T(8,128)(2,1)S(1)}, u32[]{:S(2)}, u32[]{:S(2)}) collective-permute-start(bf16[1024,512]{1,0:T(8,128)(2,1)} %get-tuple-element.102.own_ref), channel_id=1, source_target_pairs={{0,8},{8,16},{16,24},{1,9},{9,17},{17,25},{2,10},{10,18},{18,26},{... | collective-permute-start | bytes 3145736 | tf_op jit(solution)/shard_map/ppermute | solution.py:786
  61.3 3.1 collective-permute-start.5
  62.5 2.9 collective-permute-start.6
  63.4 3.6 collective-permute-start.7
  67.3 33.7 %collective-permute-start.8 = (bf16[16,1024]{1,0:T(8,128)(2,1)S(1)}, bf16[16,1024]{1,0:T(8,128)(2,1)S(1)}, u32[]{:S(2)}, u32[]{:S(2)}) collective-permute-start(bf16[16,1024]{1,0:T(8,128)(2,1)S(1)} %bitcast.172), channel_id=1, source_target_pairs={{0,8},{8,16},{16,24},{1,9},{9,17},{17,25},{2,10},{10,18},{18,26},{... | collective-permute-start | bytes 98312 | tf_op jit(solution)/shard_map/ppermute | solution.py:769
  110.0 4.7 collective-permute-start.9
  115.8 18.1 %collective-permute-start.10 = (bf16[128,2048]{1,0:T(8,128)(2,1)S(1)}, bf16[128,2048]{1,0:T(8,128)(2,1)S(1)}, u32[]{:S(2)}, u32[]{:S(2)}) collective-permute-start(bf16[128,2048]{1,0:T(8,128)(2,1)S(1)} %get-tuple-element.271), channel_id=1, source_target_pairs={{0,2},{2,0},{4,6},{6,4},{1,3},{3,1},{5,7},{7,5},{8,10},{10,8},{12,... | collective-permute-start | bytes 1572872 | tf_op jit(solution)/shard_map/ppermute | solution.py:80
  117.4 16.5 %collective-permute-start.11 = (bf16[128,2048]{1,0:T(8,128)(2,1)S(1)}, bf16[128,2048]{1,0:T(8,128)(2,1)S(1)}, u32[]{:S(2)}, u32[]{:S(2)}) collective-permute-start(bf16[128,2048]{1,0:T(8,128)(2,1)S(1)} %get-tuple-element.273), channel_id=1, source_target_pairs={{0,4},{2,6},{4,0},{6,2},{1,5},{3,7},{5,1},{7,3},{8,12},{10,14},{12... | collective-permute-start | bytes 1572872 | tf_op jit(solution)/shard_map/ppermute | solution.py:80
  118.6 27.3 %collective-permute-start.12 = (bf16[128,2048]{1,0:T(8,128)(2,1)S(1)}, bf16[128,2048]{1,0:T(8,128)(2,1)S(1)}, u32[]{:S(2)}, u32[]{:S(2)}) collective-permute-start(bf16[128,2048]{1,0:T(8,128)(2,1)S(1)} %get-tuple-element.272), channel_id=1, source_target_pairs={{0,6},{2,4},{4,2},{6,0},{1,7},{3,5},{5,3},{7,1},{8,14},{10,12},{12... | collective-permute-start | bytes 1572872 | tf_op jit(solution)/shard_map/ppermute | solution.py:80
  146.4 154.3 %copy-start.26 = (f32[128,2048]{1,0:T(8,128)}, f32[128,2048]{1,0:T(8,128)S(1)}, u32[]{:S(2)}) copy-start(f32[128,2048]{1,0:T(8,128)S(1)} %get-tuple-element.258) | copy-start | bytes 3145732
  149.1 13.8 %collective-permute-start.15 = (bf16[128,2048]{1,0:T(8,128)(2,1)S(1)}, bf16[128,2048]{1,0:T(8,128)(2,1)S(1)}, u32[]{:S(2)}, u32[]{:S(2)}) collective-permute-start(bf16[128,2048]{1,0:T(8,128)(2,1)S(1)} %get-tuple-element.127), channel_id=1, source_target_pairs={{0,6},{2,4},{4,2},{6,0},{1,7},{3,5},{5,3},{7,1},{8,14},{10,12},{12... | collective-permute-start | bytes 1572872 | tf_op jit(solution)/shard_map/ppermute | solution.py:61
  149.1 24.2 %collective-permute-start.14 = (bf16[128,2048]{1,0:T(8,128)(2,1)S(1)}, bf16[128,2048]{1,0:T(8,128)(2,1)S(1)}, u32[]{:S(2)}, u32[]{:S(2)}) collective-permute-start(bf16[128,2048]{1,0:T(8,128)(2,1)S(1)} %get-tuple-element.127), channel_id=1, source_target_pairs={{0,4},{2,6},{4,0},{6,2},{1,5},{3,7},{5,1},{7,3},{8,12},{10,14},{12... | collective-permute-start | bytes 1572872 | tf_op jit(solution)/shard_map/ppermute | solution.py:61
  150.5 22.8 %collective-permute-start.13 = (bf16[128,2048]{1,0:T(8,128)(2,1)S(1)}, bf16[128,2048]{1,0:T(8,128)(2,1)S(1)}, u32[]{:S(2)}, u32[]{:S(2)}) collective-permute-start(bf16[128,2048]{1,0:T(8,128)(2,1)S(1)} %get-tuple-element.127), channel_id=1, source_target_pairs={{0,2},{2,0},{4,6},{6,4},{1,3},{3,1},{5,7},{7,5},{8,10},{10,8},{12,... | collective-permute-start | bytes 1572872 | tf_op jit(solution)/shard_map/ppermute | solution.py:61
  175.8 377.6 %reduce-scatter.3.cloned.1.call-start = ((), (), s32[]{:S(2)}) async-start(), calls=%async_computation.6 | async-start | bytes 4718592 | tf_op jit(solution)/shard_map/reduce_scatter | solution.py:843
  176.1 5.6 collective-permute-start.16
  262.9 4.5 collective-permute-start.17
  263.3 106.1 %copy-start.20 = (s32[2]{0:T(128)}, s32[2]{0:T(128)S(1)}, u32[]{:S(2)}) copy-start(s32[2]{0:T(128)S(1)} %pad_add_fusion.2.plane_ref.chunk_ref) | copy-start | bytes 28
  273.9 26.9 %collective-permute-start.18 = (bf16[128,2048]{1,0:T(8,128)(2,1)}, bf16[128,2048]{1,0:T(8,128)(2,1)}, u32[]{:S(2)}, u32[]{:S(2)}) collective-permute-start(bf16[128,2048]{1,0:T(8,128)(2,1)} %get-tuple-element.270), channel_id=1, source_target_pairs={{0,2},{2,0},{4,6},{6,4},{1,3},{3,1},{5,7},{7,5},{8,10},{10,8},{12,... | collective-permute-start | bytes 1572872 | tf_op jit(solution)/shard_map/ppermute | solution.py:80
  275.2 25.6 %collective-permute-start.19 = (bf16[128,2048]{1,0:T(8,128)(2,1)}, bf16[128,2048]{1,0:T(8,128)(2,1)}, u32[]{:S(2)}, u32[]{:S(2)}) collective-permute-start(bf16[128,2048]{1,0:T(8,128)(2,1)} %get-tuple-element.269), channel_id=1, source_target_pairs={{0,4},{2,6},{4,0},{6,2},{1,5},{3,7},{5,1},{7,3},{8,12},{10,14},{12... | collective-permute-start | bytes 1572872 | tf_op jit(solution)/shard_map/ppermute | solution.py:80
  275.4 25.3 %collective-permute-start.20 = (bf16[128,2048]{1,0:T(8,128)(2,1)}, bf16[128,2048]{1,0:T(8,128)(2,1)}, u32[]{:S(2)}, u32[]{:S(2)}) collective-permute-start(bf16[128,2048]{1,0:T(8,128)(2,1)} %get-tuple-element.268), channel_id=1, source_target_pairs={{0,6},{2,4},{4,2},{6,0},{1,7},{3,5},{5,3},{7,1},{8,14},{10,12},{12... | collective-permute-start | bytes 1572872 | tf_op jit(solution)/shard_map/ppermute | solution.py:80
  305.4 19.6 %collective-permute-start.24 = (bf16[128,2048]{1,0:T(8,128)(2,1)S(1)}, bf16[128,2048]{1,0:T(8,128)(2,1)S(1)}, u32[]{:S(2)}, u32[]{:S(2)}) collective-permute-start(bf16[128,2048]{1,0:T(8,128)(2,1)S(1)} %get-tuple-element.253), channel_id=1, source_target_pairs={{0,6},{2,4},{4,2},{6,0},{1,7},{3,5},{5,3},{7,1},{8,14},{10,12},{12... | collective-permute-start | bytes 1572872 | tf_op jit(solution)/shard_map/ppermute | solution.py:61
  306.7 24.7 %collective-permute-start.23 = (bf16[128,2048]{1,0:T(8,128)(2,1)S(1)}, bf16[128,2048]{1,0:T(8,128)(2,1)S(1)}, u32[]{:S(2)}, u32[]{:S(2)}) collective-permute-start(bf16[128,2048]{1,0:T(8,128)(2,1)S(1)} %get-tuple-element.253), channel_id=1, source_target_pairs={{0,4},{2,6},{4,0},{6,2},{1,5},{3,7},{5,1},{7,3},{8,12},{10,14},{12... | collective-permute-start | bytes 1572872 | tf_op jit(solution)/shard_map/ppermute | solution.py:61
  308.1 23.3 %collective-permute-start.22 = (bf16[128,2048]{1,0:T(8,128)(2,1)S(1)}, bf16[128,2048]{1,0:T(8,128)(2,1)S(1)}, u32[]{:S(2)}, u32[]{:S(2)}) collective-permute-start(bf16[128,2048]{1,0:T(8,128)(2,1)S(1)} %get-tuple-element.253), channel_id=1, source_target_pairs={{0,2},{2,0},{4,6},{6,4},{1,3},{3,1},{5,7},{7,5},{8,10},{10,8},{12,... | collective-permute-start | bytes 1572872 | tf_op jit(solution)/shard_map/ppermute | solution.py:61
  331.6 4.7 collective-permute-start.25
  356.8 9.1 %collective-permute-start.27 = (f32[8,1024]{1,0:T(8,128)S(1)}, f32[8,1024]{1,0:T(8,128)S(1)}, u32[]{:S(2)}, u32[]{:S(2)}) collective-permute-start(f32[8,1024]{1,0:T(8,128)S(1)} %pad.85), channel_id=1, source_target_pairs={{8,0},{16,8},{24,16},{0,24},{9,1},{17,9},{25,17},{1,25},{10,2},{18... | collective-permute-start | bytes 98312 | tf_op jit(solution)/shard_map/ppermute | solution.py:895
  363.2 4.1 collective-permute-start.28
  363.2 4.6 collective-permute-start.29
  364.6 63.1 %collective-permute-start.26 = (bf16[1024,512]{1,0:T(8,128)(2,1)}, bf16[1024,512]{1,0:T(8,128)(2,1)}, u32[]{:S(2)}, u32[]{:S(2)}) collective-permute-start(bf16[1024,512]{1,0:T(8,128)(2,1)} %get-tuple-element.126), channel_id=1, source_target_pairs={{8,0},{16,8},{24,16},{9,1},{17,9},{25,17},{10,2},{18,10},{26,18},{... | collective-permute-start | bytes 3145736 | tf_op jit(solution)/shard_map/ppermute | solution.py:949
  375.9 51.7 %copy-start.6 = (f32[1024,128]{1,0:T(8,128)S(1)}, f32[1024,128]{1,0:T(8,128)}, u32[]{:S(2)}) copy-start(f32[1024,128]{1,0:T(8,128)} %copy-done.5) | copy-start | bytes 1572868
  375.9 51.7 %copy-start.8 = (f32[1024,128]{1,0:T(8,128)S(1)}, f32[1024,128]{1,0:T(8,128)}, u32[]{:S(2)}) copy-start(f32[1024,128]{1,0:T(8,128)} %copy-done.7) | copy-start | bytes 1572868
  375.9 51.8 %copy-start.19 = (s32[2]{0:T(128)S(1)}, s32[2]{0:T(128)}, u32[]{:S(2)}) copy-start(s32[2]{0:T(128)} %copy-done.18) | copy-start | bytes 28
  438.3 25.8 %collective-permute-start.30 = (bf16[512,2048]{1,0:T(8,128)(2,1)}, bf16[512,2048]{1,0:T(8,128)(2,1)}, u32[]{:S(2)}, u32[]{:S(2)}) collective-permute-start(bf16[512,2048]{1,0:T(8,128)(2,1)} %get-tuple-element.133), channel_id=1, source_target_pairs={{0,1},{1,0},{2,3},{3,2},{4,5},{5,4},{6,7},{7,6},{8,9},{9,8},{10,11... | collective-permute-start | bytes 6291464 | tf_op jit(solution)/shard_map/ppermute | solution.py:68
  444.8 84.1 %all-to-all-start.2 = ((bf16[4,3,128,768]{3,2,1,0:T(8,128)(2,1)}), bf16[4,3,128,768]{3,2,1,0:T(8,128)(2,1)}, u32[]{:S(2)}, u32[]{:S(2)}) async-start(bf16[4,3,128,768]{3,2,1,0:T(8,128)(2,1)} %weight_grads.3), calls=%async_computation.4 | async-start | bytes 4718592 | tf_op jit(solution)/shard_map/all_to_all | solution.py:880
  449.4 116.0 %reduce-scatter.5.cloned.1.call-start = ((), (), s32[]{:S(2)}) async-start(), calls=%async_computation.8 | async-start | bytes 5242880 | tf_op jit(solution)/shard_map/reduce_scatter | solution.py:956
  473.4 61.4 %collective-permute-start.31 = (bf16[128,2048]{1,0:T(8,128)(2,1)}, bf16[128,2048]{1,0:T(8,128)(2,1)}, u32[]{:S(2)}, u32[]{:S(2)}) collective-permute-start(bf16[128,2048]{1,0:T(8,128)(2,1)} %get-tuple-element.265), channel_id=1, source_target_pairs={{0,2},{2,0},{4,6},{6,4},{1,3},{3,1},{5,7},{7,5},{8,10},{10,8},{12,... | collective-permute-start | bytes 1572872 | tf_op jit(solution)/shard_map/ppermute | solution.py:80
  474.8 60.0 %collective-permute-start.32 = (bf16[128,2048]{1,0:T(8,128)(2,1)}, bf16[128,2048]{1,0:T(8,128)(2,1)}, u32[]{:S(2)}, u32[]{:S(2)}) collective-permute-start(bf16[128,2048]{1,0:T(8,128)(2,1)} %get-tuple-element.264), channel_id=1, source_target_pairs={{0,4},{2,6},{4,0},{6,2},{1,5},{3,7},{5,1},{7,3},{8,12},{10,14},{12... | collective-permute-start | bytes 1572872 | tf_op jit(solution)/shard_map/ppermute | solution.py:80
  475.9 58.8 %collective-permute-start.33 = (bf16[128,2048]{1,0:T(8,128)(2,1)}, bf16[128,2048]{1,0:T(8,128)(2,1)}, u32[]{:S(2)}, u32[]{:S(2)}) collective-permute-start(bf16[128,2048]{1,0:T(8,128)(2,1)} %get-tuple-element.263), channel_id=1, source_target_pairs={{0,6},{2,4},{4,2},{6,0},{1,7},{3,5},{5,3},{7,1},{8,14},{10,12},{12... | collective-permute-start | bytes 1572872 | tf_op jit(solution)/shard_map/ppermute | solution.py:80
  538.8 12.0 %all-to-all-start = ((f32[16,1,1792]{2,1,0:T(1,128)}), f32[16,1,1792]{2,1,0:T(1,128)S(1)}, u32[]{:S(2)}, u32[]{:S(2)}) async-start(f32[16,1,1792]{2,1,0:T(1,128)} %copy.142), calls=%async_computation.1 | async-start | bytes 229376 | tf_op jit(solution)/shard_map/all_to_all | solution.py:1006
  550.9 6.3 collective-permute-start.35
  556.7 5.8 collective-permute-start.34
  556.8 3.6 collective-permute-start.21
  568.1 56.3 %all-to-all-start.1 = ((bf16[4,128,4,256]{3,2,1,0:T(4,128)(2,1)}), bf16[4,128,4,256]{3,2,1,0:T(4,128)(2,1)S(1)}, u32[]{:S(2)}, u32[]{:S(2)}) async-start(bf16[4,128,4,256]{3,2,1,0:T(4,128)(2,1)} %reshape.405), calls=%async_computation.3 | async-start | bytes 2097152 | tf_op jit(solution)/shard_map/all_to_all | solution.py:880
  (57 other events, 469.0 us)
Sparse Core Ops, SparseCore 0:
  11.5 132.7 all-gather.2
  176.0 118.4 all-gather.4
  332.5 53.8 reduce-scatter.2
  464.3 75.9 reduce-scatter.4

commit v4 on v3

--- a/solution.py
+++ b/solution.py
@@ -440,18 +440,20 @@
     return jnp.sum(jnp.where(lane == block, gates, 0.0), axis=1, keepdims=True)
 
 
-def feed_kernel(first_ref, rows_ref, top_ref, gates_ref, gu_ref, down_ref, *refs):
+def feed_kernel(
+    first_ref, own_ref, other_ref, top_own, top_other, gates_ref, gu_ref, down_ref, gated_ref, grad_ref, slope_ref
+):
     del first_ref
-    gated_ref, grad_ref, slope_ref = refs[-3:]
     hidden = down_ref.shape[0]
-    gate = gate_of(gates_ref[...], pl.program_id(0))
-    gated, grad_gate_val, grad_up_val, slope = hidden_grads(
-        rows_ref[...], top_ref[...], gate, gu_ref[...], down_ref[...]
-    )
-    gated_ref[...] = gated
-    grad_ref[:, :hidden] = grad_gate_val
-    grad_ref[:, hidden:] = grad_up_val
-    slope_ref[0] = slope
+    half = own_ref.shape[0]
+    for index, (rows, top) in enumerate(((own_ref, top_own), (other_ref, top_other))):
+        here = slice(index * half, (index + 1) * half)
+        gate = gate_of(gates_ref[here, :], pl.program_id(0))
+        gated, grad_gate_val, grad_up_val, slope = hidden_grads(rows[...], top[...], gate, gu_ref[...], down_ref[...])
+        gated_ref[here, :] = gated
+        grad_ref[here, :hidden] = grad_gate_val
+        grad_ref[here, hidden:] = grad_up_val
+        slope_ref[0, here] = slope
 
 
 def weight_kernel(
@@ -590,33 +592,25 @@
     )(plane, values)
 
 
-def feed(first, index, rows, top_all, gates, weight_gu, weight_down, blocks, outs=None):
-    count, model_width = rows.shape
+def feed(first_tiles, halves, top_all, gates, weight_gu, weight_down, blocks):
+    half, model_width = halves[0].shape
     hidden = weight_down.shape[0] // blocks
-    tile = min(FEED_BLOCK, count)
-    steps = count // tile
-    whole = 2 * count
-    in_specs = [
-        pl.BlockSpec((tile, model_width), lambda s, i, c: (i, 0)),
-        pl.BlockSpec((tile, model_width), lambda s, i, c: (c[0] * steps + i, 0)),
-        pl.BlockSpec((tile, gates.shape[1]), lambda s, i, c: (i, 0)),
-        pl.BlockSpec((2 * hidden, model_width), lambda s, i, c: (s, 0)),
-        pl.BlockSpec((hidden, model_width), lambda s, i, c: (s, 0)),
-    ]
-    args = [first, rows, top_all, gates, weight_gu, weight_down]
-    aliases = {}
-    if outs is not None:
-        aliases = {len(args) + k: k for k in range(3)}
-        in_specs += [pl.BlockSpec(memory_space=pl.ANY)] * 3
-        args += list(outs)
+    whole = 2 * half
+    rows = pl.BlockSpec((half, model_width), lambda s, c: (0, 0))
     grid_spec = pltpu.PrefetchScalarGridSpec(
         num_scalar_prefetch=1,
-        grid=(blocks, steps),
-        in_specs=in_specs,
+        grid=(blocks,),
+        in_specs=[rows, rows]
+        + [pl.BlockSpec((half, model_width), lambda s, c, k=k: (c[k], 0)) for k in range(2)]
+        + [
+            pl.BlockSpec(gates.shape, lambda s, c: (0, 0)),
+            pl.BlockSpec((2 * hidden, model_width), lambda s, c: (s, 0)),
+            pl.BlockSpec((hidden, model_width), lambda s, c: (s, 0)),
+        ],
         out_specs=[
-            pl.BlockSpec((tile, hidden), lambda s, i, c: (index * steps + i, s)),
-            pl.BlockSpec((tile, 2 * hidden), lambda s, i, c: (index * steps + i, s)),
-            pl.BlockSpec((1, tile, 1), lambda s, i, c: (s, index * steps + i, 0)),
+            pl.BlockSpec((whole, hidden), lambda s, c: (0, s)),
+            pl.BlockSpec((whole, 2 * hidden), lambda s, c: (0, s)),
+            pl.BlockSpec((1, whole, 1), lambda s, c: (s, 0, 0)),
         ],
     )
     return pl.pallas_call(
@@ -627,15 +621,14 @@
             jax.ShapeDtypeStruct((whole, 2 * blocks * hidden), BF16),
             jax.ShapeDtypeStruct((blocks, whole, 1), F32),
         ],
-        input_output_aliases=aliases,
-        compiler_params=pltpu.CompilerParams(vmem_limit_bytes=56 * 2**20),
+        compiler_params=pltpu.CompilerParams(vmem_limit_bytes=62 * 2**20),
         cost_estimate=pl.CostEstimate(
-            flops=6 * count * model_width * hidden * blocks,
-            bytes_accessed=6 * model_width * hidden * blocks + 4 * count * model_width * blocks,
-            transcendentals=count * hidden * blocks,
+            flops=6 * whole * model_width * hidden * blocks,
+            bytes_accessed=6 * model_width * hidden * blocks + 4 * whole * model_width,
+            transcendentals=whole * hidden * blocks,
         ),
         name="feed",
-    )(*args)
+    )(first_tiles, *halves, top_all, top_all, gates, weight_gu, weight_down)
 
 
 def weight_grads(plane, planes, block, rows_all, top_all, rows_t, top_t, gates, packed, sums, outs, groups, hidden):
@@ -796,7 +789,8 @@
         normed_all = lax.all_gather(after(normed_own, normed_two[0]), ("dp", "tensor", "expert"), axis=0, tiled=True)
     gate_columns = jnp.concatenate([router_weight, shared_router[:, None]], axis=1)
     first_tile = 2 * plane if gathered else jnp.zeros_like(plane)
-    outs, half_gates, half_probs = None, [], []
+    top_tiles = jnp.stack([first_tile + (core + k) % 2 for k in range(2)]).astype(jnp.int32)
+    half_gates, half_probs = [], []
     for index in range(2):
         logits = dot(normed_two[index], gate_columns)
         chosen = (
@@ -806,12 +800,10 @@
         named = lax.dynamic_slice(probs * chosen, (0, mine * local_experts), (half, local_experts))
         half_gates.append(jnp.concatenate([named, jax.nn.sigmoid(logits[:, expert_count:])], axis=1))
         half_probs.append((probs, chosen))
-        first = (first_tile + (core + index) % 2).reshape(1).astype(jnp.int32)
-        outs = feed(
-            first, index, normed_two[index], grad_top_all, half_gates[index], weight_gu, weight_down, blocks, outs
-        )
-    gated, grad_hidden, slopes = outs
     gates = jnp.concatenate(half_gates, axis=0)
+    gated, grad_hidden, slopes = feed(
+        top_tiles, normed_two, grad_top_all, gates, weight_gu, weight_down, blocks
+    )
     router_probs, chosen = (jnp.concatenate(parts, axis=0) for parts in zip(*half_probs, strict=True))
 
     shared_mix = gates[:, local_experts:]
@@ -953,6 +945,9 @@
         place, grad_query_rot, own_kv_grad, came_kv, weights_in, cosine, sines, groups
     )
     grad_part = projection_grads(normed_one, grad_attended, grad_qkv, attended)
+    def attn_gain_of(grads):
+        return jnp.sum(grads * inputs * scale_one, axis=0)
+
     weight_sum = lax.psum_scatter(grad_part, "dp", scatter_dimension=0, tiled=True)
     weight_sum = weight_sum.reshape(groups, small_rows, 4, width)
     if gathered:
@@ -964,13 +959,13 @@
             other_one_part,
             lambda token: weight_sums(local_experts - 2, expert_grads, token, grad_part),
         )
-        shared_grads = after(shared_grads, expert_grads)
+        shared_grads, grad_attn_gain = after((shared_grads, attn_gain_of(grad_normed_one)), expert_grads)
     else:
         grad_normed_one = scatter_halves(own_one_part, other_one_part)
+        grad_attn_gain = attn_gain_of(grad_normed_one)
     grad_shared_gate = placed(shared_grads[:, 0])
     grad_shared_up = placed(shared_grads[:, 1])
     grad_shared_down = placed(shared_grads[:, 2]).T
-    grad_attn_gain = jnp.sum(grad_normed_one * inputs * scale_one, axis=0)
     grad_own = grad_after + norm_back(inputs, scale_one, gain_one, grad_normed_one)
     if gathered:
         expert_grads = weight_sums(local_experts - 1, expert_grads, grad_own, weight_sum)

time: 646 us -> 628 us (0.972)
    all_to_all x1, waiting for transfers between devices: 6.55 us -> 0.01 us  [per_device(): lax.all_to_all(spread, ('dp', 'expert'), 0, 0, tiled=True)]
    pallas_call x2 -> x1, Pallas kernels: 47 us -> 41.9 us  [feed(): pl.pallas_call(feed_kernel, grid_spec=grid_spec, out_shape=[jax.ShapeDtyp...]
    unnamed x134 -> x138, local copies, waits for them, and re-layouts: 29.1 us -> 30.2 us
  transfers between devices with their start and end apart: 43 -> 43, of which waited for: 19 -> 16; matrix products, arithmetic and copies ran while one was open for 22% -> 21% of each run, Pallas kernels for 43% -> 44%
where the time goes in v4:
time: 628 us; the launch traced here: 620 us
  Pallas kernels  272 us (43%)
  waiting for transfers between devices  108 us (17%)
  matrix products  70.8 us (11%)
  local copies, waits for them, and re-layouts  64 us (10%)
  starting transfers between devices  57 us (9%)
  other arithmetic  32.3 us (5%)
  between operations  15.6 us (2%)
    pallas_call x3, Pallas kernels, weight_grads(): pl.pallas_call(functools.partial(weight_kernel, block, hidden), grid_spec...  157 us
    dot_general x9, matrix products, dot(): return jnp.dot(left, right, preferred_element_type=F32)  45.7 us
    pallas_call x1, Pallas kernels, feed(): pl.pallas_call(feed_kernel, grid_spec=grid_spec, out_shape=[jax.ShapeDtyp...  41.9 us
    ppermute x9, waiting for transfers between devices, gather_halves(): came = lax.ppermute(own, 'expert', shift_pairs(groups, step))  32.6 us
    unnamed x138, local copies, waits for them, and re-layouts  30.2 us
    ppermute x9, waiting for transfers between devices, scatter_halves(): lax.ppermute(sent[step - 1], 'expert', shift_pairs(groups, step))  29.5 us
    ppermute x1, waiting for transfers between devices, per_device(): lax.ppermute(facts, 'dp', upward)[:1].astype(F32)  29.3 us
    dot_general x5, matrix products, dot_tn(): lax.dot_general(left, right, (((0,), (0,)), ((), ())), preferred_element_...  18.8 us
  transfers between devices with their start and end apart: 43, of which 16 were waited for; matrix products, arithmetic and copies ran while one was open for 21% of the time, Pallas kernels for 44%

profile of v4, /device:TPU:1, one launch (start us, length us, event | category | flops | bytes accessed | tf_op | source)
XLA Modules:
  0.0 620.4 jit_solution(6221284046123200845)
XLA Ops:
  12.5 3.0 collective-permute-start.2
  16.0 2.6 copy-done.3
  18.6 2.6 copy-done.4
  21.2 17.5 %pack_weights.1 = (bf16[4608,2048]{1,0:T(8,128)(2,1)}, bf16[2304,2048]{1,0:T(8,128)(2,1)}) custom-call(s32[2]{0:T(128)S(1)} %pad_add_fusion.1.window_ref, bf16[2,704,2048]{2,1,0:T(8,128)(2,1)S(1)} %bitcast.134, bf16[2,704,2048]{2,1,0:T(8,128)(2,1)S(1)} %bitcast.135, bf16[2,704,2048]{2,1,0:T(8,128)(2,1)} %refs_2_.1, bf16[2048,2816]{1,0:T(8,128)(2,1)} %refs_8_.1, ...), custom_call_target="tpu_custom_call" | custom-call | bytes 56623104 | tf_op jit(solution)/shard_map/pack_weights/pallas_call | solution.py:541
  38.8 4.4 collective-permute-done.1
  49.2 8.0 %project.1 = (bf16[1024,256]{1,0:T(8,128)(2,1)S(1)}, bf16[1024,512]{1,0:T(8,128)(2,1)}) custom-call(s32[2]{0:T(128)S(1)} %pad_add_fusion.place_ref, bf16[512,2048]{1,0:T(8,128)(2,1)S(1)} %constant_dynamic-update-slice_fusion.10.own_ref.n0, bf16[512,2048]{1,0:T(8,128)(2,1)} %collective-permute-done.3.other_ref.n1, bf16[2048,1024]{1,0:T(8,128)(2,1)} %wq_ref.3, ...), custom_call_target="tpu_custom_call" | custom-call | flops 3221225472 | bytes 7340032 | tf_op jit(solution)/shard_map/project/pallas_call | solution.py:287
  57.2 3.3 collective-permute-start.4
  66.4 3.6 collective-permute-start.8
  70.3 29.3 %collective-permute-done.8 = bf16[16,1024]{1,0:T(8,128)(2,1)S(1)} collective-permute-done((bf16[16,1024]{1,0:T(8,128)(2,1)S(1)}, bf16[16,1024]{1,0:T(8,128)(2,1)S(1)}, u32[]{:S(2)}, u32[]{:S(2)}) %collective-permute-start.8) | collective-permute-done | bytes 32800 | tf_op jit(solution)/shard_map/ppermute | solution.py:762
  99.7 8.1 %attend.1 = bf16[1024,256]{1,0:T(8,128)(2,1)S(1)} custom-call(bf16[1024,256]{1,0:T(8,128)(2,1)S(1)} %get-tuple-element.99.q_ref, bf16[1024,512]{1,0:T(8,128)(2,1)S(1)} %collective-permute-done.4.before_ref, bf16[1024,512]{1,0:T(8,128)(2,1)} %get-tuple-element.100.own_ref, f32[1024,1]{1,0:T(8,128)S(1)} %bitcast.141, ...), custom_call_target="tpu_custom_call" | custom-call | flops 1073741824 | bytes 3145728 | tf_op jit(solution)/shard_map/attend/pallas_call | solution.py:214
  109.9 3.9 collective-permute-done.9
  117.5 17.5 %collective-permute-done.10 = bf16[128,2048]{1,0:T(8,128)(2,1)S(1)} collective-permute-done((bf16[128,2048]{1,0:T(8,128)(2,1)S(1)}, bf16[128,2048]{1,0:T(8,128)(2,1)S(1)}, u32[]{:S(2)}, u32[]{:S(2)}) %collective-permute-start.10) | collective-permute-done | bytes 524320 | tf_op jit(solution)/shard_map/ppermute | solution.py:80
  135.0 12.0 %collective-permute-done.12 = bf16[128,2048]{1,0:T(8,128)(2,1)S(1)} collective-permute-done((bf16[128,2048]{1,0:T(8,128)(2,1)S(1)}, bf16[128,2048]{1,0:T(8,128)(2,1)S(1)}, u32[]{:S(2)}, u32[]{:S(2)}) %collective-permute-start.12) | collective-permute-done | bytes 524320 | tf_op jit(solution)/shard_map/ppermute | solution.py:80
  151.5 11.4 %collective-permute-done.15 = bf16[128,2048]{1,0:T(8,128)(2,1)S(1)} collective-permute-done((bf16[128,2048]{1,0:T(8,128)(2,1)}, bf16[128,2048]{1,0:T(8,128)(2,1)S(1)}, u32[]{:S(2)}, u32[]{:S(2)}) %collective-permute-start.15) | collective-permute-done | bytes 524320 | tf_op jit(solution)/shard_map/ppermute | solution.py:61
  162.9 10.4 %collective-permute-done.14 = bf16[128,2048]{1,0:T(8,128)(2,1)S(1)} collective-permute-done((bf16[128,2048]{1,0:T(8,128)(2,1)}, bf16[128,2048]{1,0:T(8,128)(2,1)S(1)}, u32[]{:S(2)}, u32[]{:S(2)}) %collective-permute-start.14) | collective-permute-done | bytes 524320 | tf_op jit(solution)/shard_map/ppermute | solution.py:61
  176.5 2.5 collective-permute-done.16.other_ref
  178.9 2.2 fusion.100
  182.3 41.9 %feed.1 = (bf16[1024,2304]{1,0:T(8,128)(2,1)}, bf16[1024,4608]{1,0:T(8,128)(2,1)}, f32[3,1024,1]{2,1,0:T(8,128)}) custom-call(s32[2]{0:T(128)} %get-tuple-element.311.first_ref, bf16[512,2048]{1,0:T(8,128)(2,1)} %copy-done.28, bf16[512,2048]{1,0:T(8,128)(2,1)} %collective-permute-done.16.other_ref, ...), custom_call_target="tpu_custom_call" | custom-call | flops 28991029248 | bytes 36700160 | tf_op jit(solution)/shard_map/feed/pallas_call | solution.py:616
  227.4 2.4 copy-done.31
  229.8 22.7 %add_convert_fusion = bf16[1024,2048]{1,0:T(8,128)(2,1)S(1)} fusion(f32[1024,2048]{1,0:T(8,128)S(1)} %fusion.35, bf16[1024,4608]{1,0:T(8,128)(2,1)S(1)} %copy-done.31, bf16[4608,2048]{1,0:T(8,128)(2,1)} %get-tuple-element.94.gu_ref), kind=kOutput, calls=%fused_computation | convolution fusion | flops 19331547136 | bytes 40894464 | tf_op jit(solution)/shard_map/dot_general | solution.py:26
  260.4 3.2 convert_add_fusion.1
  270.9 12.1 %fusion.4 = bf16[1024,2048]{1,0:T(8,128)(2,1)} fusion(bf16[2304,2048]{1,0:T(8,128)(2,1)S(1)} %bitcast.185, bf16[512,2304]{1,0:T(8,128)(2,1)S(1)} %get-tuple-element.258, bf16[512,2304]{1,0:T(8,128)(2,1)S(1)} %get-tuple-element.257), kind=kOutput, calls=%fused_computation.8 | convolution fusion | flops 9675210752 | bytes 18350080 | tf_op jit(solution)/shard_map/dot_general | solution.py:26
  283.0 5.6 fusion.9.gu_in
  288.7 5.4 fusion.11.gu_in
  294.1 2.3 multiply_reduce_fusion
  301.1 4.8 turn.2.top_t_ref
  306.1 2.3 fusion.15.down_in
  312.6 5.4 fusion.7.gu_in
  318.0 6.4 %collective-permute-done.23 = bf16[128,2048]{1,0:T(8,128)(2,1)S(1)} collective-permute-done((bf16[128,2048]{1,0:T(8,128)(2,1)S(1)}, bf16[128,2048]{1,0:T(8,128)(2,1)S(1)}, u32[]{:S(2)}, u32[]{:S(2)}) %collective-permute-start.23) | collective-permute-done | bytes 524320 | tf_op jit(solution)/shard_map/ppermute | solution.py:61
  325.3 3.9 collective-permute-done.25.d1
  329.2 2.9 convolution_convert_fusion.1
  335.6 13.7 %attend_back.1 = (f32[1024,256]{1,0:T(8,128)S(1)}, bf16[1024,512]{1,0:T(8,128)(2,1)}, f32[1024,512]{1,0:T(8,128)}) custom-call(bf16[1024,256]{1,0:T(8,128)(2,1)S(1)} %get-tuple-element.99.q_ref, bf16[1024,512]{1,0:T(8,128)(2,1)S(1)} %copy-done.22, bf16[1024,512]{1,0:T(8,128)(2,1)} %get-tuple-element.100.own_ref, f32[1024,1]{1,0:T(8,128)S(1)} %bitcast.142, ...), custom_call_target="tpu_custom_call" | custom-call | flops 2684354560 | bytes 8388608 | tf_op jit(solution)/shard_map/attend_back/pallas_call | solution.py:232
  350.9 2.3 collective-permute-start.28
  358.4 4.6 turn.3.rows_t_ref
  365.1 51.6 %weight_grads.3 = bf16[4,3,128,768]{3,2,1,0:T(8,128)(2,1)} custom-call(s32[2]{0:T(128)} %copy-done.18, bf16[4096,2048]{1,0:T(8,128)(2,1)} %all-gather.5.cloned.1.call-done.part_ref.rows_ref, bf16[4096,2048]{1,0:T(8,128)(2,1)} %all-gather.3.cloned.1.call-done.top_own.top_other.part_ref.top_ref, bf16[512,4096]{1,0:T(8,128)(2,1)} %copy-done.9, ...), custom_call_target="tpu_custom_call" | custom-call | flops 36238786560 | bytes 42991616 | tf_op jit(solution)/shard_map/weight_grads/pallas_call | solution.py:676
  417.9 8.6 %project_back.1 = (bf16[512,768]{1,0:T(8,128)(2,1)S(1)}, bf16[512,768]{1,0:T(8,128)(2,1)S(1)}, bf16[512,2048]{1,0:T(8,128)(2,1)}, bf16[512,2048]{1,0:T(8,128)(2,1)}, f32[8,768]{1,0:T(8,128)S(1)}) custom-call(s32[2]{0:T(128)S(1)} %copy-done.20, f32[1024,256]{1,0:T(8,128)S(1)} %copy-done.17, f32[1024,512]{1,0:T(8,128)} %get-tuple-element.120.go_ref, ...), custom_call_target="tpu_custom_call" | custom-call | flops 3221225472 | bytes 11534336 | tf_op jit(solution)/shard_map/project_back/pallas_call | solution.py:372
  431.9 4.7 all-to-all-start
  443.3 8.0 %projection_grads.1 = bf16[2048,1024]{1,0:T(8,128)(2,1)} custom-call(bf16[512,2048]{1,0:T(8,128)(2,1)S(1)} %copy-done.1, bf16[512,2048]{1,0:T(8,128)(2,1)} %collective-permute-done.3.other_ref.n1, bf16[512,2048]{1,0:T(8,128)(2,1)S(1)} %copy-done.11, bf16[512,2048]{1,0:T(8,128)(2,1)} %collective-permute-done.25.d1, ...), custom_call_target="tpu_custom_call" | custom-call | flops 4294967296 | bytes 8388608 | tf_op jit(solution)/shard_map/projection_grads/pallas_call | solution.py:406
  452.9 4.3 convert_add_fusion
  457.2 3.1 dynamic-slice_convert_fusion
  460.3 2.2 collective-permute-start.33
  463.0 52.9 %weight_grads.4 = (f32[2,704,512]{2,1,0:T(8,128)}, f32[2,704,512]{2,1,0:T(8,128)}, f32[2,704,512]{2,1,0:T(8,128)}) custom-call(s32[2]{0:T(128)} %copy-done.18, bf16[4096,2048]{1,0:T(8,128)(2,1)} %all-gather.5.cloned.1.call-done.part_ref.rows_ref, bf16[4096,2048]{1,0:T(8,128)(2,1)} %all-gather.3.cloned.1.call-done.top_own.top_other.part_ref.top_ref, ...), custom_call_target="tpu_custom_call" | custom-call | flops 36238786560 | bytes 42991616 | tf_op jit(solution)/shard_map/weight_grads/pallas_call | solution.py:676
  516.0 3.2 fusion.29
  520.0 7.0 %all-to-all-start.1 = ((f32[16,1,1792]{2,1,0:T(1,128)}), f32[16,1,1792]{2,1,0:T(1,128)S(1)}, u32[]{:S(2)}, u32[]{:S(2)}) async-start(f32[16,1,1792]{2,1,0:T(1,128)} %copy.137), calls=%async_computation.2 | async-start | bytes 229376 | tf_op jit(solution)/shard_map/all_to_all | solution.py:1001
  527.0 3.3 fusion.25
  547.4 2.6 reshape.397
  550.0 3.8 all-to-all-start.2
  553.8 52.8 %weight_grads.5 = (f32[2,704,512]{2,1,0:T(8,128)}, f32[2,704,512]{2,1,0:T(8,128)}, f32[2,704,512]{2,1,0:T(8,128)}) custom-call(s32[2]{0:T(128)} %copy-done.18, bf16[4096,2048]{1,0:T(8,128)(2,1)} %all-gather.5.cloned.1.call-done.part_ref.rows_ref, ...), custom_call_target="tpu_custom_call", output_to_operand_aliasing={{0}: (10, {}), {1}: (11, {}), {2}: (12, {})} | custom-call | flops 36238786560 | bytes 42991616 | tf_op jit(solution)/shard_map/weight_grads/pallas_call | solution.py:676
  (341 shorter events, 112.4 us)
Async XLA Ops:
  7.2 175.1 %all-gather.3.cloned.1.call-start = ((), (), s32[]{:S(2)}) async-start(), calls=%async_computation.5 | async-start | bytes 17301504 | tf_op jit(solution)/shard_map/all_gather | solution.py:749
  9.2 349.1 %all-gather.5.cloned.1.call-start = ((), (), s32[]{:S(2)}) async-start(), calls=%async_computation.7 | async-start | bytes 17301504 | tf_op jit(solution)/shard_map/all_gather | solution.py:789
  12.5 26.3 %collective-permute-start.2 = (bf16[128,2048]{1,0:T(8,128)(2,1)}, bf16[128,2048]{1,0:T(8,128)(2,1)S(1)}, u32[]{:S(2)}, u32[]{:S(2)}) collective-permute-start(bf16[128,2048]{1,0:T(8,128)(2,1)} %get-tuple-element.256), channel_id=1, source_target_pairs={{0,6},{2,4},{4,2},{6,0},{1,7},{3,5},{5,3},{7,1},{8,14},{10,12},{12... | collective-permute-start | bytes 1572872 | tf_op jit(solution)/shard_map/ppermute | solution.py:61
  15.5 27.7 %collective-permute-start.1 = (bf16[128,2048]{1,0:T(8,128)(2,1)}, bf16[128,2048]{1,0:T(8,128)(2,1)S(1)}, u32[]{:S(2)}, u32[]{:S(2)}) collective-permute-start(bf16[128,2048]{1,0:T(8,128)(2,1)} %get-tuple-element.256), channel_id=1, source_target_pairs={{0,4},{2,6},{4,0},{6,2},{1,5},{3,7},{5,1},{7,3},{8,12},{10,14},{12... | collective-permute-start | bytes 1572872 | tf_op jit(solution)/shard_map/ppermute | solution.py:61
  15.7 27.5 %collective-permute-start = (bf16[128,2048]{1,0:T(8,128)(2,1)}, bf16[128,2048]{1,0:T(8,128)(2,1)}, u32[]{:S(2)}, u32[]{:S(2)}) collective-permute-start(bf16[128,2048]{1,0:T(8,128)(2,1)} %get-tuple-element.256), channel_id=1, source_target_pairs={{0,2},{2,0},{4,6},{6,4},{1,3},{3,1},{5,7},{7,5},{8,10},{10,8},{12,... | collective-permute-start | bytes 1572872 | tf_op jit(solution)/shard_map/ppermute | solution.py:61
  44.4 4.8 collective-permute-start.3
  57.2 42.4 %collective-permute-start.4 = (bf16[1024,512]{1,0:T(8,128)(2,1)}, bf16[1024,512]{1,0:T(8,128)(2,1)S(1)}, u32[]{:S(2)}, u32[]{:S(2)}) collective-permute-start(bf16[1024,512]{1,0:T(8,128)(2,1)} %get-tuple-element.100.own_ref), channel_id=1, source_target_pairs={{0,8},{8,16},{16,24},{1,9},{9,17},{17,25},{2,10},{10,18},{18,26},{... | collective-permute-start | bytes 3145736 | tf_op jit(solution)/shard_map/ppermute | solution.py:779
  60.6 4.0 collective-permute-start.7
  62.0 2.9 collective-permute-start.6
  63.1 3.0 collective-permute-start.5
  66.4 33.2 %collective-permute-start.8 = (bf16[16,1024]{1,0:T(8,128)(2,1)S(1)}, bf16[16,1024]{1,0:T(8,128)(2,1)S(1)}, u32[]{:S(2)}, u32[]{:S(2)}) collective-permute-start(bf16[16,1024]{1,0:T(8,128)(2,1)S(1)} %bitcast.170), channel_id=1, source_target_pairs={{0,8},{8,16},{16,24},{1,9},{9,17},{17,25},{2,10},{10,18},{18,26},{... | collective-permute-start | bytes 98312 | tf_op jit(solution)/shard_map/ppermute | solution.py:762
  108.6 5.2 collective-permute-start.9
  114.8 20.2 %collective-permute-start.10 = (bf16[128,2048]{1,0:T(8,128)(2,1)S(1)}, bf16[128,2048]{1,0:T(8,128)(2,1)S(1)}, u32[]{:S(2)}, u32[]{:S(2)}) collective-permute-start(bf16[128,2048]{1,0:T(8,128)(2,1)S(1)} %get-tuple-element.267), channel_id=1, source_target_pairs={{0,2},{2,0},{4,6},{6,4},{1,3},{3,1},{5,7},{7,5},{8,10},{10,8},{12,... | collective-permute-start | bytes 1572872 | tf_op jit(solution)/shard_map/ppermute | solution.py:80
  116.3 30.8 %collective-permute-start.12 = (bf16[128,2048]{1,0:T(8,128)(2,1)S(1)}, bf16[128,2048]{1,0:T(8,128)(2,1)S(1)}, u32[]{:S(2)}, u32[]{:S(2)}) collective-permute-start(bf16[128,2048]{1,0:T(8,128)(2,1)S(1)} %get-tuple-element.268), channel_id=1, source_target_pairs={{0,6},{2,4},{4,2},{6,0},{1,7},{3,5},{5,3},{7,1},{8,14},{10,12},{12... | collective-permute-start | bytes 1572872 | tf_op jit(solution)/shard_map/ppermute | solution.py:80
  117.5 29.6 %collective-permute-start.11 = (bf16[128,2048]{1,0:T(8,128)(2,1)S(1)}, bf16[128,2048]{1,0:T(8,128)(2,1)S(1)}, u32[]{:S(2)}, u32[]{:S(2)}) collective-permute-start(bf16[128,2048]{1,0:T(8,128)(2,1)S(1)} %get-tuple-element.269), channel_id=1, source_target_pairs={{0,4},{2,6},{4,0},{6,2},{1,5},{3,7},{5,1},{7,3},{8,12},{10,14},{12... | collective-permute-start | bytes 1572872 | tf_op jit(solution)/shard_map/ppermute | solution.py:80
  148.8 14.0 %collective-permute-start.15 = (bf16[128,2048]{1,0:T(8,128)(2,1)}, bf16[128,2048]{1,0:T(8,128)(2,1)S(1)}, u32[]{:S(2)}, u32[]{:S(2)}) collective-permute-start(bf16[128,2048]{1,0:T(8,128)(2,1)} %get-tuple-element.122), channel_id=1, source_target_pairs={{0,6},{2,4},{4,2},{6,0},{1,7},{3,5},{5,3},{7,1},{8,14},{10,12},{12... | collective-permute-start | bytes 1572872 | tf_op jit(solution)/shard_map/ppermute | solution.py:61
  148.9 24.4 %collective-permute-start.14 = (bf16[128,2048]{1,0:T(8,128)(2,1)}, bf16[128,2048]{1,0:T(8,128)(2,1)S(1)}, u32[]{:S(2)}, u32[]{:S(2)}) collective-permute-start(bf16[128,2048]{1,0:T(8,128)(2,1)} %get-tuple-element.122), channel_id=1, source_target_pairs={{0,4},{2,6},{4,0},{6,2},{1,5},{3,7},{5,1},{7,3},{8,12},{10,14},{12... | collective-permute-start | bytes 1572872 | tf_op jit(solution)/shard_map/ppermute | solution.py:61
  150.2 23.1 %collective-permute-start.13 = (bf16[128,2048]{1,0:T(8,128)(2,1)}, bf16[128,2048]{1,0:T(8,128)(2,1)S(1)}, u32[]{:S(2)}, u32[]{:S(2)}) collective-permute-start(bf16[128,2048]{1,0:T(8,128)(2,1)} %get-tuple-element.122), channel_id=1, source_target_pairs={{0,2},{2,0},{4,6},{6,4},{1,3},{3,1},{5,7},{7,5},{8,10},{10,8},{12,... | collective-permute-start | bytes 1572872 | tf_op jit(solution)/shard_map/ppermute | solution.py:61
  173.5 353.5 %reduce-scatter.3.cloned.1.call-start = ((), (), s32[]{:S(2)}) async-start(), calls=%async_computation.6 | async-start | bytes 4718592 | tf_op jit(solution)/shard_map/reduce_scatter | solution.py:835
  173.6 5.4 collective-permute-start.16
  175.6 182.8 %copy-start.18 = (s32[2]{0:T(128)}, s32[2]{0:T(128)S(1)}, u32[]{:S(2)}) copy-start(s32[2]{0:T(128)S(1)} %get-tuple-element.312.plane_ref.chunk_ref) | copy-start | bytes 28
  255.9 4.5 collective-permute-start.17
  266.8 27.3 %collective-permute-start.20 = (bf16[128,2048]{1,0:T(8,128)(2,1)}, bf16[128,2048]{1,0:T(8,128)(2,1)}, u32[]{:S(2)}, u32[]{:S(2)}) collective-permute-start(bf16[128,2048]{1,0:T(8,128)(2,1)} %get-tuple-element.264), channel_id=1, source_target_pairs={{0,6},{2,4},{4,2},{6,0},{1,7},{3,5},{5,3},{7,1},{8,14},{10,12},{12... | collective-permute-start | bytes 1572872 | tf_op jit(solution)/shard_map/ppermute | solution.py:80
  268.1 26.0 %collective-permute-start.19 = (bf16[128,2048]{1,0:T(8,128)(2,1)S(1)}, bf16[128,2048]{1,0:T(8,128)(2,1)}, u32[]{:S(2)}, u32[]{:S(2)}) collective-permute-start(bf16[128,2048]{1,0:T(8,128)(2,1)S(1)} %get-tuple-element.265), channel_id=1, source_target_pairs={{0,4},{2,6},{4,0},{6,2},{1,5},{3,7},{5,1},{7,3},{8,12},{10,14},{12... | collective-permute-start | bytes 1572872 | tf_op jit(solution)/shard_map/ppermute | solution.py:80
  269.1 25.0 %collective-permute-start.18 = (bf16[128,2048]{1,0:T(8,128)(2,1)S(1)}, bf16[128,2048]{1,0:T(8,128)(2,1)}, u32[]{:S(2)}, u32[]{:S(2)}) collective-permute-start(bf16[128,2048]{1,0:T(8,128)(2,1)S(1)} %get-tuple-element.266), channel_id=1, source_target_pairs={{0,2},{2,0},{4,6},{6,4},{1,3},{3,1},{5,7},{7,5},{8,10},{10,8},{12,... | collective-permute-start | bytes 1572872 | tf_op jit(solution)/shard_map/ppermute | solution.py:80
  298.4 19.6 %collective-permute-start.24 = (bf16[128,2048]{1,0:T(8,128)(2,1)S(1)}, bf16[128,2048]{1,0:T(8,128)(2,1)S(1)}, u32[]{:S(2)}, u32[]{:S(2)}) collective-permute-start(bf16[128,2048]{1,0:T(8,128)(2,1)S(1)} %get-tuple-element.249), channel_id=1, source_target_pairs={{0,6},{2,4},{4,2},{6,0},{1,7},{3,5},{5,3},{7,1},{8,14},{10,12},{12... | collective-permute-start | bytes 1572872 | tf_op jit(solution)/shard_map/ppermute | solution.py:61
  299.7 24.7 %collective-permute-start.23 = (bf16[128,2048]{1,0:T(8,128)(2,1)S(1)}, bf16[128,2048]{1,0:T(8,128)(2,1)S(1)}, u32[]{:S(2)}, u32[]{:S(2)}) collective-permute-start(bf16[128,2048]{1,0:T(8,128)(2,1)S(1)} %get-tuple-element.249), channel_id=1, source_target_pairs={{0,4},{2,6},{4,0},{6,2},{1,5},{3,7},{5,1},{7,3},{8,12},{10,14},{12... | collective-permute-start | bytes 1572872 | tf_op jit(solution)/shard_map/ppermute | solution.py:61
  300.7 23.7 %collective-permute-start.22 = (bf16[128,2048]{1,0:T(8,128)(2,1)S(1)}, bf16[128,2048]{1,0:T(8,128)(2,1)S(1)}, u32[]{:S(2)}, u32[]{:S(2)}) collective-permute-start(bf16[128,2048]{1,0:T(8,128)(2,1)S(1)} %get-tuple-element.249), channel_id=1, source_target_pairs={{0,2},{2,0},{4,6},{6,4},{1,3},{3,1},{5,7},{7,5},{8,10},{10,8},{12,... | collective-permute-start | bytes 1572872 | tf_op jit(solution)/shard_map/ppermute | solution.py:61
  324.7 4.5 collective-permute-start.25
  350.2 6.1 collective-permute-start.29
  350.9 5.4 collective-permute-start.28
  353.2 3.5 collective-permute-start.27
  355.0 61.6 %collective-permute-start.26 = (bf16[1024,512]{1,0:T(8,128)(2,1)}, bf16[1024,512]{1,0:T(8,128)(2,1)}, u32[]{:S(2)}, u32[]{:S(2)}) collective-permute-start(bf16[1024,512]{1,0:T(8,128)(2,1)} %get-tuple-element.121), channel_id=1, source_target_pairs={{8,0},{16,8},{24,16},{9,1},{17,9},{25,17},{10,2},{18,10},{26,18},{... | collective-permute-start | bytes 3145736 | tf_op jit(solution)/shard_map/ppermute | solution.py:941
  365.1 51.6 %copy-start.20 = (s32[2]{0:T(128)S(1)}, s32[2]{0:T(128)}, u32[]{:S(2)}) copy-start(s32[2]{0:T(128)} %copy-done.19) | copy-start | bytes 28
  427.3 24.0 %collective-permute-start.30 = (bf16[512,2048]{1,0:T(8,128)(2,1)}, bf16[512,2048]{1,0:T(8,128)(2,1)}, u32[]{:S(2)}, u32[]{:S(2)}) collective-permute-start(bf16[512,2048]{1,0:T(8,128)(2,1)} %get-tuple-element.128), channel_id=1, source_target_pairs={{0,1},{1,0},{2,3},{3,2},{4,5},{5,4},{6,7},{7,6},{8,9},{9,8},{10,11... | collective-permute-start | bytes 6291464 | tf_op jit(solution)/shard_map/ppermute | solution.py:68
  431.9 87.3 %all-to-all-start = ((bf16[4,3,128,768]{3,2,1,0:T(8,128)(2,1)}), bf16[4,3,128,768]{3,2,1,0:T(8,128)(2,1)}, u32[]{:S(2)}, u32[]{:S(2)}) async-start(bf16[4,3,128,768]{3,2,1,0:T(8,128)(2,1)} %weight_grads.3), calls=%async_computation.1 | async-start | bytes 4718592 | tf_op jit(solution)/shard_map/all_to_all | solution.py:872
  436.6 110.8 %reduce-scatter.5.cloned.1.call-start = ((), (), s32[]{:S(2)}) async-start(), calls=%async_computation.8 | async-start | bytes 5242880 | tf_op jit(solution)/shard_map/reduce_scatter | solution.py:951
  460.3 55.6 %collective-permute-start.33 = (bf16[128,2048]{1,0:T(8,128)(2,1)}, bf16[128,2048]{1,0:T(8,128)(2,1)}, u32[]{:S(2)}, u32[]{:S(2)}) collective-permute-start(bf16[128,2048]{1,0:T(8,128)(2,1)} %get-tuple-element.259), channel_id=1, source_target_pairs={{0,6},{2,4},{4,2},{6,0},{1,7},{3,5},{5,3},{7,1},{8,14},{10,12},{12... | collective-permute-start | bytes 1572872 | tf_op jit(solution)/shard_map/ppermute | solution.py:80
  462.5 53.3 %collective-permute-start.32 = (bf16[128,2048]{1,0:T(8,128)(2,1)}, bf16[128,2048]{1,0:T(8,128)(2,1)}, u32[]{:S(2)}, u32[]{:S(2)}) collective-permute-start(bf16[128,2048]{1,0:T(8,128)(2,1)} %get-tuple-element.260), channel_id=1, source_target_pairs={{0,4},{2,6},{4,0},{6,2},{1,5},{3,7},{5,1},{7,3},{8,12},{10,14},{12... | collective-permute-start | bytes 1572872 | tf_op jit(solution)/shard_map/ppermute | solution.py:80
  462.8 53.1 %copy-start.40 = (bf16[256,2048]{1,0:T(8,128)(2,1)S(1)}, bf16[256,2048]{1,0:T(8,128)(2,1)}, u32[]{:S(2)}) copy-start(bf16[256,2048]{1,0:T(8,128)(2,1)} %param.25) | copy-start | bytes 3145732
  462.8 53.1 %copy-start.46 = (f32[2048]{0:T(1024)S(1)}, f32[2048]{0:T(1024)}, u32[]{:S(2)}) copy-start(f32[2048]{0:T(1024)} %copy-done.45) | copy-start | bytes 24580
  462.8 53.1 %copy-start.49 = (f32[128]{0:T(128)S(1)}, f32[128]{0:T(128)}, u32[]{:S(2)}) copy-start(f32[128]{0:T(128)} %copy-done.48) | copy-start | bytes 1540
  462.8 53.1 %collective-permute-start.31 = (bf16[128,2048]{1,0:T(8,128)(2,1)S(1)}, bf16[128,2048]{1,0:T(8,128)(2,1)}, u32[]{:S(2)}, u32[]{:S(2)}) collective-permute-start(bf16[128,2048]{1,0:T(8,128)(2,1)S(1)} %get-tuple-element.261), channel_id=1, source_target_pairs={{0,2},{2,0},{4,6},{6,4},{1,3},{3,1},{5,7},{7,5},{8,10},{10,8},{12,... | collective-permute-start | bytes 1572872 | tf_op jit(solution)/shard_map/ppermute | solution.py:80
  520.0 15.3 %all-to-all-start.1 = ((f32[16,1,1792]{2,1,0:T(1,128)}), f32[16,1,1792]{2,1,0:T(1,128)S(1)}, u32[]{:S(2)}, u32[]{:S(2)}) async-start(f32[16,1,1792]{2,1,0:T(1,128)} %copy.137), calls=%async_computation.2 | async-start | bytes 229376 | tf_op jit(solution)/shard_map/all_to_all | solution.py:1001
  530.3 11.9 %collective-permute-start.21 = (bf16[128,2048]{1,0:T(8,128)(2,1)}, bf16[128,2048]{1,0:T(8,128)(2,1)}, u32[]{:S(2)}, u32[]{:S(2)}) collective-permute-start(bf16[128,2048]{1,0:T(8,128)(2,1)} %get-tuple-element.289), channel_id=1, source_target_pairs={{0,1},{1,0},{2,3},{3,2},{4,5},{5,4},{6,7},{7,6},{8,9},{9,8},{10,11... | collective-permute-start | bytes 1572872 | tf_op jit(solution)/shard_map/ppermute | solution.py:68
  532.1 12.4 %collective-permute-start.34 = (f32[128,2048]{1,0:T(8,128)}, f32[128,2048]{1,0:T(8,128)S(1)}, u32[]{:S(2)}, u32[]{:S(2)}) collective-permute-start(f32[128,2048]{1,0:T(8,128)} %get-tuple-element.288), channel_id=1, source_target_pairs={{0,1},{1,0},{2,3},{3,2},{4,5},{5,4},{6,7},{7,6},{8,9},{9,8},{10,11... | collective-permute-start | bytes 3145736 | tf_op jit(solution)/shard_map/ppermute | solution.py:68
  535.4 4.0 collective-permute-start.35
  550.0 56.5 %all-to-all-start.2 = ((bf16[4,128,4,256]{3,2,1,0:T(4,128)(2,1)}), bf16[4,128,4,256]{3,2,1,0:T(4,128)(2,1)S(1)}, u32[]{:S(2)}, u32[]{:S(2)}) async-start(bf16[4,128,4,256]{3,2,1,0:T(4,128)(2,1)} %reshape.397), calls=%async_computation.4 | async-start | bytes 2097152 | tf_op jit(solution)/shard_map/all_to_all | solution.py:872
  (59 other events, 534.3 us)
Sparse Core Ops, SparseCore 0:
  11.5 134.0 all-gather.2
  173.6 116.6 all-gather.4
  325.4 50.7 reduce-scatter.2
  451.5 78.0 reduce-scatter.4

commit v5 on v4

--- a/solution.py
+++ b/solution.py
@@ -70,11 +70,12 @@
 
 def scatter_halves(own, other, meanwhile=None):
     groups, mine = lax.axis_size("expert"), lax.axis_index("expert")
-    held = own.astype(F32) + swapped(other.astype(BF16)).astype(F32)
-    rows, width = held.shape[0] // groups, held.shape[1]
+    crossed = swapped(other.astype(BF16))
+    rows, width = own.shape[0] // groups, own.shape[1]
 
     def of_group(index):
-        return lax.dynamic_slice(held, (index * rows, 0), (rows, width))
+        parts = [lax.dynamic_slice(values, (index * rows, 0), (rows, width)) for values in (own, crossed)]
+        return parts[0].astype(F32) + parts[1].astype(F32)
 
     sent = [of_group(partner(mine, groups, step)).astype(BF16) for step in range(1, groups)]
     came = [lax.ppermute(sent[step - 1], "expert", shift_pairs(groups, step)) for step in range(1, groups)]
@@ -655,7 +656,10 @@
         tokens,
         turned,
         turned,
-        pl.BlockSpec((tile, gates.shape[1]), lambda i, c: (i, 0)),
+        pl.BlockSpec(
+            (tile, gates.shape[1]),
+            lambda i, c: (lax.rem(c[0] + 1 + i // steps, planes) * steps + lax.rem(i, steps), 0),
+        ),
         pl.BlockSpec((2 * padded, model_width), lambda i, c: (block, 0)),
         pl.BlockSpec((padded, model_width), lambda i, c: (block, 0)),
         pl.BlockSpec((part, 2 * padded), lambda i, c: (0, 0)),
@@ -739,11 +743,21 @@
         window, expert_gate, expert_up, expert_down, shared_gate, shared_up, shared_down, padded
     )
 
+    half = plane_rows // 2
+    slot = jnp.arange(plane_rows, dtype=jnp.int32)
+    half_core = (core + slot // half) % 2
+    row_index = plane * plane_rows + slot % half // rows * tok_rows + half_core * rows + slot % rows
+    places = (row_index % SEQ_LEN).astype(F32)
+    frequency = THETA ** (-2.0 * jnp.arange(HD // 2, dtype=F32) / HD)
+    angles = places[:, None] * jnp.concatenate([frequency, frequency])[None, :]
+    cosine = jnp.cos(angles)
+    sines = jnp.sin(angles) * jnp.where(jnp.arange(HD) < HD // 2, -1.0, 1.0)[None, :]
+
     own_tokens = lax.dynamic_slice(tokens, (core * rows, 0), (rows, model_width))
     inputs = own_tokens.astype(F32)
     gain_one = attn_gain.astype(F32)
     scale_one = lax.rsqrt(jnp.mean(inputs * inputs, axis=-1, keepdims=True) + EPS)
-    normed_one = gather_halves((inputs * scale_one * gain_one).astype(BF16), (weight_gu, weight_down))
+    normed_one = gather_halves((inputs * scale_one * gain_one).astype(BF16), (weight_gu, weight_down, cosine, sines))
     grad_top_own = lax.dynamic_slice(grad_out, (core * rows, 0), (rows, model_width))
     top_axes = ("dp", "tensor", "expert") if gathered else ("tensor", "expert")
     grad_top_all = lax.all_gather(grad_top_own, top_axes, axis=0, tiled=True)
@@ -763,15 +777,6 @@
     seg_rows = seg_own.reshape(plane_rows, 1)
     bits = jnp.concatenate(half_order(facts[1].reshape(plane_rows, 1), groups), axis=0).astype(jnp.int32)
 
-    half = plane_rows // 2
-    slot = jnp.arange(plane_rows, dtype=jnp.int32)
-    half_core = (core + slot // half) % 2
-    row_index = plane * plane_rows + slot % half // rows * tok_rows + half_core * rows + slot % rows
-    places = (row_index % SEQ_LEN).astype(F32)
-    frequency = THETA ** (-2.0 * jnp.arange(HD // 2, dtype=F32) / HD)
-    angles = places[:, None] * jnp.concatenate([frequency, frequency])[None, :]
-    cosine = jnp.cos(angles)
-    sines = jnp.sin(angles) * jnp.where(jnp.arange(HD) < HD // 2, -1.0, 1.0)[None, :]
     place = jnp.stack([mine, core]).astype(jnp.int32)
     weights_in = (query_weight, key_weight, value_weight)
     bias_in = jnp.stack([bias.reshape(-1) for bias in (query_bias, key_bias, value_bias)])
@@ -883,13 +888,10 @@
         gates_sent = after(
             jnp.pad(gates.T, [(0, -gates.shape[1] % 8), (0, 0)]), back_kv
         )
-        gates_came = [
-            lax.ppermute(gates_sent, "dp", [((i + step) % planes, i) for i in range(planes)])
-            for step in range(1, planes)
-        ]
+        gates_came = lax.all_to_all(jnp.broadcast_to(gates_sent[None], (planes, *gates_sent.shape)), "dp", 0, 0)
         normed_all = after(normed_all, back_kv)
         rows_t = turn(plane_number, normed_all, part_rows)
-        gates_all = jnp.concatenate(gates_came, axis=1).T
+        gates_all = gates_came.transpose(0, 2, 1).reshape(planes * plane_rows, -1)
 
         def weight_sums(block, outs, *tokens):
             return weight_grads(

time: 628 us -> 628 us (level)
    add x2 -> x0, other arithmetic: 7.57 us -> none  [scatter_halves(): held = own.astype(F32) + swapped(other.astype(BF16)).astype(F32)]
    all_to_all x0 -> x1, starting transfers between devices: none -> 6.31 us  [per_device(): lax.all_to_all(jnp.broadcast_to(gates_sent[None], (planes, *gates_sent.sh...]
    unnamed x138 -> x132, local copies, waits for them, and re-layouts: 30.2 us -> 29.3 us
  transfers between devices with their start and end apart: 43 -> 41, of which waited for: 16 -> 19; matrix products, arithmetic and copies ran while one was open for 21% -> 21% of each run, Pallas kernels for 44% -> 44%
where the time goes in v5:
time: 628 us; the launch traced here: 620 us
  Pallas kernels  270 us (43%)
  waiting for transfers between devices  112 us (18%)
  matrix products  72.1 us (11%)
  local copies, waits for them, and re-layouts  63.1 us (10%)
  starting transfers between devices  56.3 us (9%)
  other arithmetic  30.8 us (5%)
  between operations  15.5 us (2%)
    pallas_call x3, Pallas kernels, weight_grads(): pl.pallas_call(functools.partial(weight_kernel, block, hidden), grid_spec...  155 us
    dot_general x9, matrix products, dot(): return jnp.dot(left, right, preferred_element_type=F32)  47.4 us
    pallas_call x1, Pallas kernels, feed(): pl.pallas_call(feed_kernel, grid_spec=grid_spec, out_shape=[jax.ShapeDtyp...  42.1 us
    ppermute x9, waiting for transfers between devices, gather_halves(): came = lax.ppermute(own, 'expert', shift_pairs(groups, step))  30.5 us
    ppermute x1, waiting for transfers between devices, per_device(): lax.ppermute(facts, 'dp', upward)[:1].astype(F32)  29.7 us
    unnamed x132, local copies, waits for them, and re-layouts  29.3 us
    ppermute x9, waiting for transfers between devices, scatter_halves(): lax.ppermute(sent[step - 1], 'expert', shift_pairs(groups, step))  29 us
    dot_general x5, matrix products, dot_tn(): lax.dot_general(left, right, (((0,), (0,)), ((), ())), preferred_element_...  18.6 us
  transfers between devices with their start and end apart: 41, of which 19 were waited for; matrix products, arithmetic and copies ran while one was open for 21% of the time, Pallas kernels for 44%

profile of v5, /device:TPU:1, one launch (start us, length us, event | category | flops | bytes accessed | tf_op | source)
XLA Modules:
  0.0 619.7 jit_solution(8206252795017051093)
XLA Ops:
  12.5 3.0 collective-permute-start.2
  16.0 2.6 copy-done.3
  18.6 2.6 copy-done.4
  21.3 17.5 %pack_weights.1 = (bf16[4608,2048]{1,0:T(8,128)(2,1)}, bf16[2304,2048]{1,0:T(8,128)(2,1)}) custom-call(s32[2]{0:T(128)S(1)} %pad_add_fusion.1.window_ref, bf16[2,704,2048]{2,1,0:T(8,128)(2,1)S(1)} %bitcast.135, bf16[2,704,2048]{2,1,0:T(8,128)(2,1)S(1)} %bitcast.136, bf16[2,704,2048]{2,1,0:T(8,128)(2,1)} %refs_2_.1, bf16[2048,2816]{1,0:T(8,128)(2,1)} %refs_8_.1, ...), custom_call_target="tpu_custom_call" | custom-call | bytes 56623104 | tf_op jit(solution)/shard_map/pack_weights/pallas_call | solution.py:542
  40.9 2.3 collective-permute-done.1
  45.4 3.6 collective-permute-done.3.other_ref.n1
  50.4 7.6 %project.1 = (bf16[1024,256]{1,0:T(8,128)(2,1)S(1)}, bf16[1024,512]{1,0:T(8,128)(2,1)}) custom-call(s32[2]{0:T(128)S(1)} %pad_add_fusion.place_ref, bf16[512,2048]{1,0:T(8,128)(2,1)S(1)} %constant_dynamic-update-slice_fusion.10.own_ref.n0, bf16[512,2048]{1,0:T(8,128)(2,1)} %copy-done.10, bf16[2048,1024]{1,0:T(8,128)(2,1)} %wq_ref.3, ...), custom_call_target="tpu_custom_call" | custom-call | flops 3221225472 | bytes 7340032 | tf_op jit(solution)/shard_map/project/pallas_call | solution.py:288
  58.4 3.3 collective-permute-start.4
  67.7 3.6 collective-permute-start.8
  71.5 29.7 %collective-permute-done.8 = bf16[16,1024]{1,0:T(8,128)(2,1)S(1)} collective-permute-done((bf16[16,1024]{1,0:T(8,128)(2,1)S(1)}, bf16[16,1024]{1,0:T(8,128)(2,1)S(1)}, u32[]{:S(2)}, u32[]{:S(2)}) %collective-permute-start.8) | collective-permute-done | bytes 32800 | tf_op jit(solution)/shard_map/ppermute | solution.py:776
  101.2 8.1 %attend.1 = bf16[1024,256]{1,0:T(8,128)(2,1)S(1)} custom-call(bf16[1024,256]{1,0:T(8,128)(2,1)S(1)} %get-tuple-element.99.q_ref, bf16[1024,512]{1,0:T(8,128)(2,1)S(1)} %collective-permute-done.4.before_ref, bf16[1024,512]{1,0:T(8,128)(2,1)} %get-tuple-element.100.own_ref, f32[1024,1]{1,0:T(8,128)S(1)} %bitcast.142, ...), custom_call_target="tpu_custom_call" | custom-call | flops 1073741824 | bytes 3145728 | tf_op jit(solution)/shard_map/attend/pallas_call | solution.py:215
  112.4 3.0 collective-permute-done.9
  118.6 14.7 %collective-permute-done.10 = bf16[128,2048]{1,0:T(8,128)(2,1)S(1)} collective-permute-done((bf16[128,2048]{1,0:T(8,128)(2,1)S(1)}, bf16[128,2048]{1,0:T(8,128)(2,1)S(1)}, u32[]{:S(2)}, u32[]{:S(2)}) %collective-permute-start.10) | collective-permute-done | bytes 524320 | tf_op jit(solution)/shard_map/ppermute | solution.py:81
  133.3 12.0 %collective-permute-done.12 = bf16[128,2048]{1,0:T(8,128)(2,1)S(1)} collective-permute-done((bf16[128,2048]{1,0:T(8,128)(2,1)S(1)}, bf16[128,2048]{1,0:T(8,128)(2,1)S(1)}, u32[]{:S(2)}, u32[]{:S(2)}) %collective-permute-start.12) | collective-permute-done | bytes 524320 | tf_op jit(solution)/shard_map/ppermute | solution.py:81
  149.9 11.3 %collective-permute-done.15 = bf16[128,2048]{1,0:T(8,128)(2,1)S(1)} collective-permute-done((bf16[128,2048]{1,0:T(8,128)(2,1)}, bf16[128,2048]{1,0:T(8,128)(2,1)S(1)}, u32[]{:S(2)}, u32[]{:S(2)}) %collective-permute-start.15) | collective-permute-done | bytes 524320 | tf_op jit(solution)/shard_map/ppermute | solution.py:61
  161.2 10.5 %collective-permute-done.14 = bf16[128,2048]{1,0:T(8,128)(2,1)S(1)} collective-permute-done((bf16[128,2048]{1,0:T(8,128)(2,1)}, bf16[128,2048]{1,0:T(8,128)(2,1)S(1)}, u32[]{:S(2)}, u32[]{:S(2)}) %collective-permute-start.14) | collective-permute-done | bytes 524320 | tf_op jit(solution)/shard_map/ppermute | solution.py:61
  174.9 2.5 collective-permute-done.16.other_ref
  180.7 42.1 %feed.1 = (bf16[1024,2304]{1,0:T(8,128)(2,1)}, bf16[1024,4608]{1,0:T(8,128)(2,1)}, f32[3,1024,1]{2,1,0:T(8,128)}) custom-call(s32[2]{0:T(128)} %get-tuple-element.313.first_ref, bf16[512,2048]{1,0:T(8,128)(2,1)} %copy-done.30, bf16[512,2048]{1,0:T(8,128)(2,1)} %collective-permute-done.16.other_ref, ...), custom_call_target="tpu_custom_call" | custom-call | flops 28991029248 | bytes 36700160 | tf_op jit(solution)/shard_map/feed/pallas_call | solution.py:617
  226.0 2.4 copy-done.32
  228.4 22.7 %add_convert_fusion = bf16[1024,2048]{1,0:T(8,128)(2,1)S(1)} fusion(f32[1024,2048]{1,0:T(8,128)S(1)} %fusion.36, bf16[1024,4608]{1,0:T(8,128)(2,1)S(1)} %copy-done.32, bf16[4608,2048]{1,0:T(8,128)(2,1)} %get-tuple-element.94.gu_ref), kind=kOutput, calls=%fused_computation | convolution fusion | flops 19331547136 | bytes 40894464 | tf_op jit(solution)/shard_map/dot_general | solution.py:26
  258.0 2.8 add_convert_fusion.5
  263.5 2.8 constant_dynamic-slice_fusion.7
  266.3 13.8 %fusion.4 = bf16[1024,2048]{1,0:T(8,128)(2,1)} fusion(bf16[2304,2048]{1,0:T(8,128)(2,1)} %get-tuple-element.95.down_ref, bf16[512,2304]{1,0:T(8,128)(2,1)S(1)} %get-tuple-element.261, bf16[512,2304]{1,0:T(8,128)(2,1)S(1)} %get-tuple-element.260), kind=kOutput, calls=%fused_computation.5 | convolution fusion | flops 9675210752 | bytes 18350080 | tf_op jit(solution)/shard_map/dot_general | solution.py:26
  280.1 5.4 fusion.9.gu_in
  285.5 5.4 fusion.11.gu_in
  300.0 4.8 turn.2.top_t_ref
  304.9 2.3 fusion.15.down_in
  311.6 5.4 fusion.7.gu_in
  317.0 6.4 %collective-permute-done.23 = bf16[128,2048]{1,0:T(8,128)(2,1)S(1)} collective-permute-done((bf16[128,2048]{1,0:T(8,128)(2,1)S(1)}, bf16[128,2048]{1,0:T(8,128)(2,1)S(1)}, u32[]{:S(2)}, u32[]{:S(2)}) %collective-permute-start.23) | collective-permute-done | bytes 524320 | tf_op jit(solution)/shard_map/ppermute | solution.py:61
  324.2 3.9 collective-permute-done.25.d1
  328.1 2.6 convolution_convert_fusion.1
  334.3 13.7 %attend_back.1 = (f32[1024,256]{1,0:T(8,128)S(1)}, bf16[1024,512]{1,0:T(8,128)(2,1)}, f32[1024,512]{1,0:T(8,128)}) custom-call(bf16[1024,256]{1,0:T(8,128)(2,1)S(1)} %get-tuple-element.99.q_ref, bf16[1024,512]{1,0:T(8,128)(2,1)S(1)} %copy-done.24, bf16[1024,512]{1,0:T(8,128)(2,1)} %get-tuple-element.100.own_ref, f32[1024,1]{1,0:T(8,128)S(1)} %bitcast.143, ...), custom_call_target="tpu_custom_call" | custom-call | flops 2684354560 | bytes 8388608 | tf_op jit(solution)/shard_map/attend_back/pallas_call | solution.py:233
  349.6 6.3 %all-to-all-start = ((f32[4,8,1024]{2,1,0:T(8,128)}), f32[4,8,1024]{2,1,0:T(8,128)S(1)}, u32[]{:S(2)}, u32[]{:S(2)}) async-start(f32[4,8,1024]{2,1,0:T(8,128)} %broadcast_in_dim.74), calls=%async_computation.1 | async-start | bytes 262144 | tf_op jit(solution)/shard_map/all_to_all | solution.py:891
  357.2 3.5 all-to-all-done
  362.6 4.5 turn.3.rows_t_ref
  369.3 50.7 %weight_grads.3 = bf16[4,3,128,768]{3,2,1,0:T(8,128)(2,1)} custom-call(s32[2]{0:T(128)} %copy-done.20, bf16[4096,2048]{1,0:T(8,128)(2,1)} %all-gather.5.cloned.1.call-done.part_ref.rows_ref, bf16[4096,2048]{1,0:T(8,128)(2,1)} %all-gather.3.cloned.1.call-done.top_own.top_other.part_ref.top_ref, bf16[512,4096]{1,0:T(8,128)(2,1)} %copy-done.9, ...), custom_call_target="tpu_custom_call" | custom-call | flops 36238786560 | bytes 42991616 | tf_op jit(solution)/shard_map/weight_grads/pallas_call | solution.py:680
  421.3 8.6 %project_back.1 = (bf16[512,768]{1,0:T(8,128)(2,1)S(1)}, bf16[512,768]{1,0:T(8,128)(2,1)S(1)}, bf16[512,2048]{1,0:T(8,128)(2,1)}, bf16[512,2048]{1,0:T(8,128)(2,1)}, f32[8,768]{1,0:T(8,128)S(1)}) custom-call(s32[2]{0:T(128)S(1)} %copy-done.22, f32[1024,256]{1,0:T(8,128)S(1)} %copy-done.19, f32[1024,512]{1,0:T(8,128)} %get-tuple-element.120.go_ref, ...), custom_call_target="tpu_custom_call" | custom-call | flops 3221225472 | bytes 11534336 | tf_op jit(solution)/shard_map/project_back/pallas_call | solution.py:373
  430.8 2.8 collective-permute-start.27
  436.8 4.6 all-to-all-start.1
  449.7 7.8 %projection_grads.1 = bf16[2048,1024]{1,0:T(8,128)(2,1)} custom-call(bf16[512,2048]{1,0:T(8,128)(2,1)S(1)} %copy-done.1, bf16[512,2048]{1,0:T(8,128)(2,1)S(1)} %copy-done.11, bf16[512,2048]{1,0:T(8,128)(2,1)S(1)} %copy-done.13, bf16[512,2048]{1,0:T(8,128)(2,1)} %collective-permute-done.25.d1, bf16[512,768]{1,0:T(8,128)(2,1)S(1)} %get-tuple-element.129.g0, ...), custom_call_target="tpu_custom_call" | custom-call | flops 4294967296 | bytes 8388608 | tf_op jit(solution)/shard_map/projection_grads/pallas_call | solution.py:407
  459.1 2.8 add_convert_fusion.1
  464.6 52.2 %weight_grads.4 = (f32[2,704,512]{2,1,0:T(8,128)}, f32[2,704,512]{2,1,0:T(8,128)}, f32[2,704,512]{2,1,0:T(8,128)}) custom-call(s32[2]{0:T(128)} %copy-done.20, bf16[4096,2048]{1,0:T(8,128)(2,1)} %all-gather.5.cloned.1.call-done.part_ref.rows_ref, bf16[4096,2048]{1,0:T(8,128)(2,1)} %all-gather.3.cloned.1.call-done.top_own.top_other.part_ref.top_ref, ...), custom_call_target="tpu_custom_call" | custom-call | flops 36238786560 | bytes 42991616 | tf_op jit(solution)/shard_map/weight_grads/pallas_call | solution.py:680
  517.6 3.3 fusion.29
  521.7 3.8 all-to-all-start.2
  525.5 3.3 fusion.25
  547.5 2.6 reshape.402
  550.1 3.8 all-to-all-start.3
  553.9 52.1 %weight_grads.5 = (f32[2,704,512]{2,1,0:T(8,128)}, f32[2,704,512]{2,1,0:T(8,128)}, f32[2,704,512]{2,1,0:T(8,128)}) custom-call(s32[2]{0:T(128)} %copy-done.20, bf16[4096,2048]{1,0:T(8,128)(2,1)} %all-gather.5.cloned.1.call-done.part_ref.rows_ref, ...), custom_call_target="tpu_custom_call", output_to_operand_aliasing={{0}: (10, {}), {1}: (11, {}), {2}: (12, {})} | custom-call | flops 36238786560 | bytes 42991616 | tf_op jit(solution)/shard_map/weight_grads/pallas_call | solution.py:680
  (327 shorter events, 117.0 us)
Async XLA Ops:
  7.2 173.5 %all-gather.3.cloned.1.call-start = ((), (), s32[]{:S(2)}) async-start(), calls=%async_computation.6 | async-start | bytes 17301504 | tf_op jit(solution)/shard_map/all_gather | solution.py:763
  9.2 353.4 %all-gather.5.cloned.1.call-start = ((), (), s32[]{:S(2)}) async-start(), calls=%async_computation.8 | async-start | bytes 17301504 | tf_op jit(solution)/shard_map/all_gather | solution.py:794
  12.5 28.4 %collective-permute-start.2 = (bf16[128,2048]{1,0:T(8,128)(2,1)}, bf16[128,2048]{1,0:T(8,128)(2,1)S(1)}, u32[]{:S(2)}, u32[]{:S(2)}) collective-permute-start(bf16[128,2048]{1,0:T(8,128)(2,1)} %get-tuple-element.256), channel_id=1, source_target_pairs={{0,6},{2,4},{4,2},{6,0},{1,7},{3,5},{5,3},{7,1},{8,14},{10,12},{12... | collective-permute-start | bytes 1572872 | tf_op jit(solution)/shard_map/ppermute | solution.py:61
  15.5 27.7 %collective-permute-start.1 = (bf16[128,2048]{1,0:T(8,128)(2,1)}, bf16[128,2048]{1,0:T(8,128)(2,1)S(1)}, u32[]{:S(2)}, u32[]{:S(2)}) collective-permute-start(bf16[128,2048]{1,0:T(8,128)(2,1)} %get-tuple-element.256), channel_id=1, source_target_pairs={{0,4},{2,6},{4,0},{6,2},{1,5},{3,7},{5,1},{7,3},{8,12},{10,14},{12... | collective-permute-start | bytes 1572872 | tf_op jit(solution)/shard_map/ppermute | solution.py:61
  15.7 27.5 %collective-permute-start = (bf16[128,2048]{1,0:T(8,128)(2,1)}, bf16[128,2048]{1,0:T(8,128)(2,1)}, u32[]{:S(2)}, u32[]{:S(2)}) collective-permute-start(bf16[128,2048]{1,0:T(8,128)(2,1)} %get-tuple-element.256), channel_id=1, source_target_pairs={{0,2},{2,0},{4,6},{6,4},{1,3},{3,1},{5,7},{7,5},{8,10},{10,8},{12,... | collective-permute-start | bytes 1572872 | tf_op jit(solution)/shard_map/ppermute | solution.py:61
  44.4 4.6 collective-permute-start.3
  58.4 42.7 %collective-permute-start.4 = (bf16[1024,512]{1,0:T(8,128)(2,1)}, bf16[1024,512]{1,0:T(8,128)(2,1)S(1)}, u32[]{:S(2)}, u32[]{:S(2)}) collective-permute-start(bf16[1024,512]{1,0:T(8,128)(2,1)} %get-tuple-element.100.own_ref), channel_id=1, source_target_pairs={{0,8},{8,16},{16,24},{1,9},{9,17},{17,25},{2,10},{10,18},{18,26},{... | collective-permute-start | bytes 3145736 | tf_op jit(solution)/shard_map/ppermute | solution.py:784
  61.9 4.0 collective-permute-start.7
  63.6 2.9 collective-permute-start.6
  64.3 3.0 collective-permute-start.5
  67.7 33.5 %collective-permute-start.8 = (bf16[16,1024]{1,0:T(8,128)(2,1)S(1)}, bf16[16,1024]{1,0:T(8,128)(2,1)S(1)}, u32[]{:S(2)}, u32[]{:S(2)}) collective-permute-start(bf16[16,1024]{1,0:T(8,128)(2,1)S(1)} %bitcast.170), channel_id=1, source_target_pairs={{0,8},{8,16},{16,24},{1,9},{9,17},{17,25},{2,10},{10,18},{18,26},{... | collective-permute-start | bytes 98312 | tf_op jit(solution)/shard_map/ppermute | solution.py:776
  110.1 5.3 collective-permute-start.9
  115.9 17.4 %collective-permute-start.10 = (bf16[128,2048]{1,0:T(8,128)(2,1)S(1)}, bf16[128,2048]{1,0:T(8,128)(2,1)S(1)}, u32[]{:S(2)}, u32[]{:S(2)}) collective-permute-start(bf16[128,2048]{1,0:T(8,128)(2,1)S(1)} %get-tuple-element.257), channel_id=1, source_target_pairs={{0,2},{2,0},{4,6},{6,4},{1,3},{3,1},{5,7},{7,5},{8,10},{10,8},{12,... | collective-permute-start | bytes 1572872 | tf_op jit(solution)/shard_map/ppermute | solution.py:81
  117.3 28.0 %collective-permute-start.12 = (bf16[128,2048]{1,0:T(8,128)(2,1)S(1)}, bf16[128,2048]{1,0:T(8,128)(2,1)S(1)}, u32[]{:S(2)}, u32[]{:S(2)}) collective-permute-start(bf16[128,2048]{1,0:T(8,128)(2,1)S(1)} %get-tuple-element.258), channel_id=1, source_target_pairs={{0,6},{2,4},{4,2},{6,0},{1,7},{3,5},{5,3},{7,1},{8,14},{10,12},{12... | collective-permute-start | bytes 1572872 | tf_op jit(solution)/shard_map/ppermute | solution.py:81
  118.5 26.9 %collective-permute-start.11 = (bf16[128,2048]{1,0:T(8,128)(2,1)S(1)}, bf16[128,2048]{1,0:T(8,128)(2,1)S(1)}, u32[]{:S(2)}, u32[]{:S(2)}) collective-permute-start(bf16[128,2048]{1,0:T(8,128)(2,1)S(1)} %get-tuple-element.259), channel_id=1, source_target_pairs={{0,4},{2,6},{4,0},{6,2},{1,5},{3,7},{5,1},{7,3},{8,12},{10,14},{12... | collective-permute-start | bytes 1572872 | tf_op jit(solution)/shard_map/ppermute | solution.py:81
  147.2 14.0 %collective-permute-start.15 = (bf16[128,2048]{1,0:T(8,128)(2,1)}, bf16[128,2048]{1,0:T(8,128)(2,1)S(1)}, u32[]{:S(2)}, u32[]{:S(2)}) collective-permute-start(bf16[128,2048]{1,0:T(8,128)(2,1)} %get-tuple-element.122), channel_id=1, source_target_pairs={{0,6},{2,4},{4,2},{6,0},{1,7},{3,5},{5,3},{7,1},{8,14},{10,12},{12... | collective-permute-start | bytes 1572872 | tf_op jit(solution)/shard_map/ppermute | solution.py:61
  147.3 24.4 %collective-permute-start.14 = (bf16[128,2048]{1,0:T(8,128)(2,1)}, bf16[128,2048]{1,0:T(8,128)(2,1)S(1)}, u32[]{:S(2)}, u32[]{:S(2)}) collective-permute-start(bf16[128,2048]{1,0:T(8,128)(2,1)} %get-tuple-element.122), channel_id=1, source_target_pairs={{0,4},{2,6},{4,0},{6,2},{1,5},{3,7},{5,1},{7,3},{8,12},{10,14},{12... | collective-permute-start | bytes 1572872 | tf_op jit(solution)/shard_map/ppermute | solution.py:61
  148.7 23.0 %collective-permute-start.13 = (bf16[128,2048]{1,0:T(8,128)(2,1)}, bf16[128,2048]{1,0:T(8,128)(2,1)S(1)}, u32[]{:S(2)}, u32[]{:S(2)}) collective-permute-start(bf16[128,2048]{1,0:T(8,128)(2,1)} %get-tuple-element.122), channel_id=1, source_target_pairs={{0,2},{2,0},{4,6},{6,4},{1,3},{3,1},{5,7},{7,5},{8,10},{10,8},{12,... | collective-permute-start | bytes 1572872 | tf_op jit(solution)/shard_map/ppermute | solution.py:61
  171.9 353.6 %reduce-scatter.3.cloned.1.call-start = ((), (), s32[]{:S(2)}) async-start(), calls=%async_computation.7 | async-start | bytes 4718592 | tf_op jit(solution)/shard_map/reduce_scatter | solution.py:840
  172.0 5.4 collective-permute-start.16
  174.0 188.6 %copy-start.20 = (s32[2]{0:T(128)}, s32[2]{0:T(128)S(1)}, u32[]{:S(2)}) copy-start(s32[2]{0:T(128)S(1)} %get-tuple-element.314.plane_ref.chunk_ref) | copy-start | bytes 28
  253.4 4.6 collective-permute-start.17
  260.8 30.2 %collective-permute-start.20 = (bf16[128,2048]{1,0:T(8,128)(2,1)}, bf16[128,2048]{1,0:T(8,128)(2,1)S(1)}, u32[]{:S(2)}, u32[]{:S(2)}) collective-permute-start(bf16[128,2048]{1,0:T(8,128)(2,1)} %get-tuple-element.267), channel_id=1, source_target_pairs={{0,6},{2,4},{4,2},{6,0},{1,7},{3,5},{5,3},{7,1},{8,14},{10,12},{12... | collective-permute-start | bytes 1572872 | tf_op jit(solution)/shard_map/ppermute | solution.py:81
  261.8 31.3 %collective-permute-start.19 = (bf16[128,2048]{1,0:T(8,128)(2,1)}, bf16[128,2048]{1,0:T(8,128)(2,1)S(1)}, u32[]{:S(2)}, u32[]{:S(2)}) collective-permute-start(bf16[128,2048]{1,0:T(8,128)(2,1)} %get-tuple-element.268), channel_id=1, source_target_pairs={{0,4},{2,6},{4,0},{6,2},{1,5},{3,7},{5,1},{7,3},{8,12},{10,14},{12... | collective-permute-start | bytes 1572872 | tf_op jit(solution)/shard_map/ppermute | solution.py:81
  263.0 30.2 %collective-permute-start.18 = (bf16[128,2048]{1,0:T(8,128)(2,1)}, bf16[128,2048]{1,0:T(8,128)(2,1)}, u32[]{:S(2)}, u32[]{:S(2)}) collective-permute-start(bf16[128,2048]{1,0:T(8,128)(2,1)} %get-tuple-element.269), channel_id=1, source_target_pairs={{0,2},{2,0},{4,6},{6,4},{1,3},{3,1},{5,7},{7,5},{8,10},{10,8},{12,... | collective-permute-start | bytes 1572872 | tf_op jit(solution)/shard_map/ppermute | solution.py:81
  297.3 19.7 %collective-permute-start.24 = (bf16[128,2048]{1,0:T(8,128)(2,1)S(1)}, bf16[128,2048]{1,0:T(8,128)(2,1)S(1)}, u32[]{:S(2)}, u32[]{:S(2)}) collective-permute-start(bf16[128,2048]{1,0:T(8,128)(2,1)S(1)} %get-tuple-element.249), channel_id=1, source_target_pairs={{0,6},{2,4},{4,2},{6,0},{1,7},{3,5},{5,3},{7,1},{8,14},{10,12},{12... | collective-permute-start | bytes 1572872 | tf_op jit(solution)/shard_map/ppermute | solution.py:61
  298.6 24.8 %collective-permute-start.23 = (bf16[128,2048]{1,0:T(8,128)(2,1)S(1)}, bf16[128,2048]{1,0:T(8,128)(2,1)S(1)}, u32[]{:S(2)}, u32[]{:S(2)}) collective-permute-start(bf16[128,2048]{1,0:T(8,128)(2,1)S(1)} %get-tuple-element.249), channel_id=1, source_target_pairs={{0,4},{2,6},{4,0},{6,2},{1,5},{3,7},{5,1},{7,3},{8,12},{10,14},{12... | collective-permute-start | bytes 1572872 | tf_op jit(solution)/shard_map/ppermute | solution.py:61
  299.7 23.7 %collective-permute-start.22 = (bf16[128,2048]{1,0:T(8,128)(2,1)S(1)}, bf16[128,2048]{1,0:T(8,128)(2,1)S(1)}, u32[]{:S(2)}, u32[]{:S(2)}) collective-permute-start(bf16[128,2048]{1,0:T(8,128)(2,1)S(1)} %get-tuple-element.249), channel_id=1, source_target_pairs={{0,2},{2,0},{4,6},{6,4},{1,3},{3,1},{5,7},{7,5},{8,10},{10,8},{12,... | collective-permute-start | bytes 1572872 | tf_op jit(solution)/shard_map/ppermute | solution.py:61
  323.5 4.6 collective-permute-start.25
  349.6 11.1 %all-to-all-start = ((f32[4,8,1024]{2,1,0:T(8,128)}), f32[4,8,1024]{2,1,0:T(8,128)S(1)}, u32[]{:S(2)}, u32[]{:S(2)}) async-start(f32[4,8,1024]{2,1,0:T(8,128)} %broadcast_in_dim.74), calls=%async_computation.1 | async-start | bytes 262144 | tf_op jit(solution)/shard_map/all_to_all | solution.py:891
  355.9 64.1 %collective-permute-start.26 = (bf16[1024,512]{1,0:T(8,128)(2,1)}, bf16[1024,512]{1,0:T(8,128)(2,1)}, u32[]{:S(2)}, u32[]{:S(2)}) collective-permute-start(bf16[1024,512]{1,0:T(8,128)(2,1)} %get-tuple-element.121), channel_id=1, source_target_pairs={{8,0},{16,8},{24,16},{9,1},{17,9},{25,17},{10,2},{18,10},{26,18},{... | collective-permute-start | bytes 3145736 | tf_op jit(solution)/shard_map/ppermute | solution.py:943
  369.3 50.7 %copy-start.6 = (f32[1024,128]{1,0:T(8,128)S(1)}, f32[1024,128]{1,0:T(8,128)}, u32[]{:S(2)}) copy-start(f32[1024,128]{1,0:T(8,128)} %copy-done.5) | copy-start | bytes 1572868
  369.3 50.7 %copy-start.8 = (f32[1024,128]{1,0:T(8,128)S(1)}, f32[1024,128]{1,0:T(8,128)}, u32[]{:S(2)}) copy-start(f32[1024,128]{1,0:T(8,128)} %copy-done.7) | copy-start | bytes 1572868
  369.3 50.8 %copy-start.22 = (s32[2]{0:T(128)S(1)}, s32[2]{0:T(128)}, u32[]{:S(2)}) copy-start(s32[2]{0:T(128)} %copy-done.21) | copy-start | bytes 28
  430.8 26.8 %collective-permute-start.27 = (bf16[512,2048]{1,0:T(8,128)(2,1)}, bf16[512,2048]{1,0:T(8,128)(2,1)}, u32[]{:S(2)}, u32[]{:S(2)}) collective-permute-start(bf16[512,2048]{1,0:T(8,128)(2,1)} %get-tuple-element.128), channel_id=1, source_target_pairs={{0,1},{1,0},{2,3},{3,2},{4,5},{5,4},{6,7},{7,6},{8,9},{9,8},{10,11... | collective-permute-start | bytes 6291464 | tf_op jit(solution)/shard_map/ppermute | solution.py:68
  436.8 84.1 %all-to-all-start.1 = ((bf16[4,3,128,768]{3,2,1,0:T(8,128)(2,1)}), bf16[4,3,128,768]{3,2,1,0:T(8,128)(2,1)}, u32[]{:S(2)}, u32[]{:S(2)}) async-start(bf16[4,3,128,768]{3,2,1,0:T(8,128)(2,1)} %weight_grads.3), calls=%async_computation.2 | async-start | bytes 4718592 | tf_op jit(solution)/shard_map/all_to_all | solution.py:877
  441.5 106.0 %reduce-scatter.5.cloned.1.call-start = ((), (), s32[]{:S(2)}) async-start(), calls=%async_computation.9 | async-start | bytes 5242880 | tf_op jit(solution)/shard_map/reduce_scatter | solution.py:953
  461.9 54.9 %collective-permute-start.30 = (bf16[128,2048]{1,0:T(8,128)(2,1)}, bf16[128,2048]{1,0:T(8,128)(2,1)S(1)}, u32[]{:S(2)}, u32[]{:S(2)}) collective-permute-start(bf16[128,2048]{1,0:T(8,128)(2,1)} %get-tuple-element.262), channel_id=1, source_target_pairs={{0,6},{2,4},{4,2},{6,0},{1,7},{3,5},{5,3},{7,1},{8,14},{10,12},{12... | collective-permute-start | bytes 1572872 | tf_op jit(solution)/shard_map/ppermute | solution.py:81
  464.2 52.7 %collective-permute-start.29 = (bf16[128,2048]{1,0:T(8,128)(2,1)}, bf16[128,2048]{1,0:T(8,128)(2,1)}, u32[]{:S(2)}, u32[]{:S(2)}) collective-permute-start(bf16[128,2048]{1,0:T(8,128)(2,1)} %get-tuple-element.263), channel_id=1, source_target_pairs={{0,4},{2,6},{4,0},{6,2},{1,5},{3,7},{5,1},{7,3},{8,12},{10,14},{12... | collective-permute-start | bytes 1572872 | tf_op jit(solution)/shard_map/ppermute | solution.py:81
  464.5 53.2 %copy-start.42 = (bf16[256,2048]{1,0:T(8,128)(2,1)S(1)}, bf16[256,2048]{1,0:T(8,128)(2,1)}, u32[]{:S(2)}) copy-start(bf16[256,2048]{1,0:T(8,128)(2,1)} %param.25) | copy-start | bytes 3145732
  464.5 53.2 %copy-start.48 = (f32[2048]{0:T(1024)S(1)}, f32[2048]{0:T(1024)}, u32[]{:S(2)}) copy-start(f32[2048]{0:T(1024)} %copy-done.47) | copy-start | bytes 24580
  464.5 53.2 %copy-start.51 = (f32[128]{0:T(128)S(1)}, f32[128]{0:T(128)}, u32[]{:S(2)}) copy-start(f32[128]{0:T(128)} %copy-done.50) | copy-start | bytes 1540
  464.5 52.4 %collective-permute-start.28 = (bf16[128,2048]{1,0:T(8,128)(2,1)}, bf16[128,2048]{1,0:T(8,128)(2,1)}, u32[]{:S(2)}, u32[]{:S(2)}) collective-permute-start(bf16[128,2048]{1,0:T(8,128)(2,1)} %get-tuple-element.264), channel_id=1, source_target_pairs={{0,2},{2,0},{4,6},{6,4},{1,3},{3,1},{5,7},{7,5},{8,10},{10,8},{12,... | collective-permute-start | bytes 1572872 | tf_op jit(solution)/shard_map/ppermute | solution.py:81
  521.7 14.1 %all-to-all-start.2 = ((f32[16,1,1792]{2,1,0:T(1,128)}), f32[16,1,1792]{2,1,0:T(1,128)S(1)}, u32[]{:S(2)}, u32[]{:S(2)}) async-start(f32[16,1,1792]{2,1,0:T(1,128)} %copy.137), calls=%async_computation.3 | async-start | bytes 229376 | tf_op jit(solution)/shard_map/all_to_all | solution.py:1003
  528.8 13.4 %collective-permute-start.21 = (bf16[128,2048]{1,0:T(8,128)(2,1)}, bf16[128,2048]{1,0:T(8,128)(2,1)}, u32[]{:S(2)}, u32[]{:S(2)}) collective-permute-start(bf16[128,2048]{1,0:T(8,128)(2,1)} %get-tuple-element.291), channel_id=1, source_target_pairs={{0,1},{1,0},{2,3},{3,2},{4,5},{5,4},{6,7},{7,6},{8,9},{9,8},{10,11... | collective-permute-start | bytes 1572872 | tf_op jit(solution)/shard_map/ppermute | solution.py:68
  530.4 14.3 %collective-permute-start.31 = (f32[128,2048]{1,0:T(8,128)}, f32[128,2048]{1,0:T(8,128)S(1)}, u32[]{:S(2)}, u32[]{:S(2)}) collective-permute-start(f32[128,2048]{1,0:T(8,128)} %get-tuple-element.290), channel_id=1, source_target_pairs={{0,1},{1,0},{2,3},{3,2},{4,5},{5,4},{6,7},{7,6},{8,9},{9,8},{10,11... | collective-permute-start | bytes 3145736 | tf_op jit(solution)/shard_map/ppermute | solution.py:68
  535.8 3.6 collective-permute-start.32
  550.1 55.8 %all-to-all-start.3 = ((bf16[4,128,4,256]{3,2,1,0:T(4,128)(2,1)}), bf16[4,128,4,256]{3,2,1,0:T(4,128)(2,1)S(1)}, u32[]{:S(2)}, u32[]{:S(2)}) async-start(bf16[4,128,4,256]{3,2,1,0:T(4,128)(2,1)} %reshape.402), calls=%async_computation.5 | async-start | bytes 2097152 | tf_op jit(solution)/shard_map/all_to_all | solution.py:877
  (54 other events, 400.9 us)
Sparse Core Ops, SparseCore 0:
  11.5 132.2 all-gather.2
  172.0 130.3 all-gather.4
  324.3 52.5 reduce-scatter.2
  457.6 75.5 reduce-scatter.4
